TPU v7x, 256 devices: a whole 4x4x8 slice. The times are simulated.
256 devices in a mesh: row: 8 (over y, x_lo), col: 32 (over x_hi, z, core).
Axes of the slice: x: 4 (x_hi: 2, x_lo: 2; x = x_hi * 2 + x_lo), y: 4, z: 8, core: 2. Of those that a mesh axis runs over, the one named last changes fastest.
Arguments:
- out_grad: bfloat16 [65536, 256], P(('row', 'col')), may hold values from -6 to 6
- pre_act: bfloat16 [65536, 256], P(('row', 'col')), may hold values from -6 to 6
- features: bfloat16 [65536, 256], P(('col', 'row')), may hold values from -0.119628906 to 0.119628906
- weight: bfloat16 [256, 256], replicated, may hold values from -0.375 to 0.375
- inv_degree: float32 [65536], replicated, may hold values from 0.01 to 0.2
- node_time: int32 [65536], replicated, may hold values from 0 to 31
- decay_rate: float32 [1], replicated, may hold values from 0.03 to 0.15
- tile_value: bfloat16 [8, 5632, 128, 128], P('row', 'col'), may hold values from 0 to 1
- tile_row: int32 [8, 5632], P('row', 'col'), may hold values from 0 to 63, as said below
- tile_col: int32 [8, 5632], P('row', 'col'), may hold values from 0 to 15
- tile_count: int32 [8, 32], P('row', 'col'), may hold values from 1 to 176, as said below
Outputs:
- grad_input: bfloat16 [65536, 256], P(('col', 'row'))
- weight_grad: float32 [256, 256], replicated
Inputs may be any that keep to these rules, and one draw needn't show every extreme that they name: `tile_count`: some block has exactly 176 live slots in every draw. `tile_row`: in each block the live slots (the first tile_count) name distinct tiles, in increasing order of tile row and then tile column; slots from tile_count on name arbitrary tiles.
All inputs are finite; a program needn't handle non-finite values.
Results may differ from a plain program's by a relative error of at most 0.0058.
Values may be sent and summed in bfloat16 or wider, within the bound.
No kernel may reach another device: no remote copies, remote signals or barrier semaphores. Data moves between devices by JAX's collectives and lax.ppermute only.
A program may use at most 64 MiB of HBM per device.

v0:
```python
import jax
import jax.numpy as jnp
from jax import lax
from jax.sharding import PartitionSpec as P

slot_block = 16


def edge_tiles(values, tile_rows, tile_cols, inside, row_times, col_times, row_scale, decay):
    tile_width = values.shape[2]
    offsets = jnp.arange(tile_width, dtype=jnp.int32)
    source_index = tile_rows[:, None] * tile_width + offsets[None, :]
    target_index = tile_cols[:, None] * tile_width + offsets[None, :]
    source_time = jnp.take(row_times, source_index, axis=0, mode="clip")
    target_time = jnp.take(col_times, target_index, axis=0, mode="clip")
    source_scale = jnp.take(row_scale, source_index, axis=0, mode="clip")
    time_gap = jnp.abs(target_time[:, None, :] - source_time[:, :, None]).astype(jnp.float32)
    edges = (
        values.astype(jnp.float32)
        * jnp.exp(-decay * time_gap)
        * source_scale[:, :, None]
        * inside[:, None, None]
    )
    return edges.astype(jnp.bfloat16)


def shards(
    out_grad,
    pre_act,
    features,
    weight,
    inv_degree,
    node_time,
    decay_rate,
    tile_value,
    tile_row,
    tile_col,
    tile_count,
):
    node_dev, width_out = out_grad.shape
    tile_width = tile_value.shape[3]
    rows_per_block = node_dev * lax.axis_size("col")
    cols_per_block = node_dev * lax.axis_size("row")
    row_index = lax.axis_index("row")
    col_index = lax.axis_index("col")
    row_times = lax.dynamic_slice_in_dim(node_time, row_index * rows_per_block, rows_per_block)
    col_times = lax.dynamic_slice_in_dim(node_time, col_index * cols_per_block, cols_per_block)
    row_scale = lax.dynamic_slice_in_dim(inv_degree, row_index * rows_per_block, rows_per_block)
    decay = decay_rate[0]
    values = tile_value[0]
    tile_rows = tile_row[0]
    tile_cols = tile_col[0]
    live_count = tile_count[0, 0]
    masked_grad = jnp.where(pre_act > 0, out_grad, jnp.zeros_like(out_grad))
    grad_zero = jnp.zeros((cols_per_block // tile_width, tile_width, width_out), jnp.float32)
    gathered = lax.all_gather(masked_grad, "col", axis=0, tiled=True)
    panel = gathered.reshape(rows_per_block // tile_width, tile_width, width_out)
    lower = jnp.int32(0)

    def one_block(step_index, running):
        slot_start = step_index * slot_block
        chosen = slot_start + jnp.arange(slot_block, dtype=jnp.int32)
        inside = ((chosen >= lower) & (chosen < live_count)).astype(jnp.float32)
        slot_rows = lax.dynamic_slice_in_dim(tile_rows, slot_start, slot_block, 0)
        slot_cols = lax.dynamic_slice_in_dim(tile_cols, slot_start, slot_block, 0)
        slot_values = lax.dynamic_slice_in_dim(values, slot_start, slot_block, 0)
        edges = edge_tiles(
            slot_values, slot_rows, slot_cols, inside, row_times, col_times, row_scale, decay
        )
        inputs = jnp.take(panel, slot_rows - 0 // tile_width, axis=0, mode="clip")
        return running.at[slot_cols].add(
            jnp.einsum("bij,bif->bjf", edges, inputs, preferred_element_type=jnp.float32)
        )

    partial_value = lax.fori_loop(
        lower // slot_block, (live_count + slot_block - 1) // slot_block, one_block, grad_zero
    )
    summed = lax.psum_scatter(
        partial_value.reshape(cols_per_block, width_out), "row", scatter_dimension=0, tiled=True
    )
    node_grad = summed.astype(jnp.bfloat16)
    grad_input = jnp.einsum(
        "ng,fg->nf", node_grad, weight, preferred_element_type=jnp.float32
    ).astype(jnp.bfloat16)
    local_grad = jnp.einsum(
        "nf,ng->fg", features.astype(jnp.float32), summed, precision=lax.Precision.HIGHEST
    )
    weight_grad = lax.psum(local_grad, ("row", "col"))
    return (grad_input, weight_grad)


def solution(mesh):
    placed = (
        P(("row", "col"), None),
        P(("row", "col"), None),
        P(("col", "row"), None),
        P(),
        P(),
        P(),
        P(),
        P("row", "col", None, None),
        P("row", "col"),
        P("row", "col"),
        P("row", "col"),
    )
    return jax.shard_map(
        shards,
        mesh=mesh,
        in_specs=placed,
        out_specs=(P(("col", "row"), None), P()),
        check_vma=False,
    )
```

profile of v0, /device:TPU:1, one launch (start us, length us, event | category | flops | bytes accessed | tf_op | source)
XLA Modules:
  0.0 915.7 jit_solution(12282786092431665306)
XLA Ops:
  7.2 0.0 all-gather.2.cloned.1.call-start
  7.2 1.7 compare_select_fusion.1
  8.9 0.0 reduce-scatter.2.cloned.1.call-start
  10.3 0.7 dynamic_slice.24
  11.0 8.3 copy.15
  19.3 83.2 %all-gather.2.cloned.1.call-done = bf16[8192,256]{1,0:T(8,128)(2,1)} async-done(((bf16[256,256]{1,0:T(8,128)(2,1)}), bf16[8192,256]{1,0:T(8,128)(2,1)}) %all-gather.2.cloned.1.call-update) | async-done | bytes 4194320 | tf_op jit(solution)/shard_map/all_gather | solution.py:56
  102.4 1.5 broadcast_in_dim.28
  104.0 45.4 %while.12 = (s32[]{:T(128)}, f32[16,128,256]{2,1,0:T(8,128)}, s32[]{:T(128)}, s32[176]{0:T(256)S(1)}, bf16[176,128,128]{1,2,0:T(8,128)(2,1)}, /*index=5*/f32[]{:...) while((s32[]{:T(128)}, f32[16,128,256]{2,1,0:T(8,128)}, ...), condition=%wide.region_2.3_spmd, body=%wide.region_0.2_spmd.sunk | while | flops 137110688 | bytes 12178963 | solution.py:75
  104.0 0.7 and_convert_fusion.2
  104.7 0.1 broadcast_multiply_fusion.3
  104.8 0.1 bitcast_clamp_fusion.4
  104.8 11.8 %gather_fusion.2 = s32[2048]{0:T(1024)S(1)} fusion(s32[8192]{0:T(1024)S(1)} %get-tuple-element.300, s32[2048]{0:T(1024)S(1)} %bitcast_clamp_fusion.4), kind=kCustom, calls=%fused_computation.1.clone.1 | custom fusion | bytes 24576 | tf_op jit(solution)/shard_map/while/body/jit(_take)/gather | solution.py:14
  116.6 11.8 %gather_fusion.1 = f32[2048]{0:T(1024)S(1)} fusion(f32[8192]{0:T(1024)S(1)} %get-tuple-element.301, s32[2048]{0:T(1024)S(1)} %bitcast_clamp_fusion.4), kind=kCustom, calls=%fused_computation.2.clone.1 | custom fusion | bytes 24576 | tf_op jit(solution)/shard_map/while/body/jit(_take)/gather | solution.py:16
  128.4 0.1 bitcast_clamp_fusion.5
  128.5 11.8 %gather_fusion.3 = s32[2048]{0:T(1024)S(1)} fusion(s32[2048]{0:T(1024)S(1)} %get-tuple-element.298, s32[2048]{0:T(1024)S(1)} %bitcast_clamp_fusion.5), kind=kCustom, calls=%fused_computation.clone.1 | custom fusion | bytes 24576 | tf_op jit(solution)/shard_map/while/body/jit(_take)/gather | solution.py:15
  140.3 2.8 gather_fusion
  143.1 1.8 fusion.16
  144.9 4.4 scatter_fusion
  149.4 0.0 all-reduce.2.cloned.1.call-start
  149.4 503.6 %reduce-scatter.2.cloned.1.call-done = f32[256,256]{1,0:T(8,128)} async-done(((f32[2048,256]{1,0:T(8,128)}), f32[256,256]{1,0:T(8,128)}) %reduce-scatter.2.cloned.1.call-update) | async-done | bytes 262160 | tf_op jit(solution)/shard_map/reduce_scatter | solution.py:78
  653.0 2.0 convolution_bitcast_fusion
  655.1 1.8 convolution_convert_fusion
  656.9 250.5 %all-reduce.2.cloned.1.call-done = f32[256,256]{0,1:T(8,128)} async-done(((f32[256,256]{0,1:T(8,128)}), f32[256,256]{0,1:T(8,128)}) %all-reduce.2.cloned.1.call-update) | async-done | bytes 262160 | tf_op jit(solution)/shard_map/psum | solution.py:88
  907.4 1.8 copy.16
  (16 shorter events, 0.1 us)
Async XLA Ops:
  7.2 645.8 %copy-start = (bf16[256,256]{1,0:T(8,128)(2,1)S(1)}, bf16[256,256]{1,0:T(8,128)(2,1)}, u32[]{:S(2)}) copy-start(bf16[256,256]{1,0:T(8,128)(2,1)} %param.15) | copy-start | bytes 393220
  7.2 95.3 %all-gather.2.cloned.1.call-start = ((), (), s32[]{:S(2)}) async-start(), calls=%async_computation.1 | async-start | bytes 4325376 | tf_op jit(solution)/shard_map/all_gather | solution.py:56
  8.9 644.1 %reduce-scatter.2.cloned.1.call-start = ((), (), s32[]{:S(2)}) async-start(), calls=%async_computation.2 | async-start | bytes 2359296 | tf_op jit(solution)/shard_map/reduce_scatter | solution.py:78
  19.2 84.7 %dynamic-slice-start = ((s32[65536]{0:T(1024)}, s32[]{:T(128)}), s32[8192]{0:T(1024)S(1)}, s32[]{:S(2)}) async-start(s32[65536]{0:T(1024)} %param.18, s32[]{:T(128)} %select_n.31), calls=%async_computation.4 | async-start | bytes 66048 | tf_op jit(solution)/shard_map/dynamic_slice | solution.py:46
  19.3 84.7 %dynamic-slice-start.1 = ((f32[65536]{0:T(1024)}, s32[]{:T(128)}), f32[8192]{0:T(1024)S(1)}, s32[]{:S(2)}) async-start(f32[65536]{0:T(1024)} %param.17, s32[]{:T(128)} %select_n.31), calls=%async_computation.5 | async-start | bytes 66048 | tf_op jit(solution)/shard_map/dynamic_slice | solution.py:48
  19.3 84.7 %copy-start.2 = (s32[1,176]{1,0:T(1,128)S(1)}, s32[1,176]{1,0:T(1,128)}, u32[]{:S(2)}) copy-start(s32[1,176]{1,0:T(1,128)} %param.22) | copy-start | bytes 2116
  19.3 84.7 %copy-start.3 = (s32[1,176]{1,0:T(1,128)S(1)}, s32[1,176]{1,0:T(1,128)}, u32[]{:S(2)}) copy-start(s32[1,176]{1,0:T(1,128)} %param.21) | copy-start | bytes 2116
  149.3 505.7 %copy-start.1 = (bf16[256,256]{1,0:T(8,128)(2,1)S(1)}, bf16[256,256]{1,0:T(8,128)(2,1)}, u32[]{:S(2)}) copy-start(bf16[256,256]{1,0:T(8,128)(2,1)} %param.16) | copy-start | bytes 393220
  149.4 758.0 %all-reduce.2.cloned.1.call-start = ((), (), s32[]{:S(2)}) async-start(), calls=%async_computation.3 | async-start | bytes 524288 | tf_op jit(solution)/shard_map/psum | solution.py:88
Sparse Core Ops, SparseCore 0:
  11.4 91.0 all-gather.1
  149.5 503.4 reduce-scatter.1
  659.0 248.3 all-reduce.1
where the time goes:
time: 918 us; the launch traced here: 916 us
  waiting for transfers between devices  837 us (91%)
  local copies, waits for them, and re-layouts  50.4 us (5%)
  between operations  15.1 us (2%)
    reduce_scatter x1, waiting for transfers between devices, shards(): lax.psum_scatter(partial_value.reshape(cols_per_block, width_out), 'row',...  504 us
    psum x1, waiting for transfers between devices, shards(): weight_grad = lax.psum(local_grad, ('row', 'col'))  251 us
    all_gather x1, waiting for transfers between devices, shards(): gathered = lax.all_gather(masked_grad, 'col', axis=0, tiled=True)  83.2 us
  transfers between devices with their start and end apart: 3, of which 3 were waited for; matrix products, arithmetic and copies ran while one was open for 1% of the time, Pallas kernels for 0%

commit v1 on v0

v1 whole, which is shorter than its diff:
```python
import jax
import jax.numpy as jnp
from jax import lax
from jax.experimental import pallas as pl
from jax.experimental.pallas import tpu as pltpu
from jax.sharding import Mesh, PartitionSpec as P

ROW = ("y", "xl")
COL = ("xh", "z", "c")
NEAR = ROW + ("c",)
FAR = ("xh", "z")
TILE = 128
CHUNK = 16
UNROLL = 8
VMEM = pl.BlockSpec(memory_space=pltpu.VMEM)
SMEM = pl.BlockSpec(memory_space=pltpu.SMEM)
ANY = pl.BlockSpec(memory_space=pl.ANY)
BIG = pltpu.CompilerParams(vmem_limit_bytes=48 << 20)
F32 = jnp.float32
BF16 = jnp.bfloat16


def mask_kernel(grad_ref, act_ref, feat_ref, out_ref, feat_t_ref):
    grad = grad_ref[...].astype(F32)
    kept = jnp.where(act_ref[...].astype(F32) > 0, grad, 0.0)
    out_ref[...] = kept.T.astype(BF16)
    feat_t_ref[...] = feat_ref[...].astype(F32).T.astype(BF16)


def edge_kernel(
    where_ref,
    rows_ref,
    cols_ref,
    count_ref,
    decay_ref,
    values_ref,
    time_ref,
    degree_ref,
    edge_ref,
    row_time,
    col_time,
    row_scale,
    near_row,
    far_row,
    near_col,
    far_col,
    value_sem,
    node_sem,
):
    slots = edge_ref.shape[0]
    chunks = slots // CHUNK
    tile_rows = row_time.shape[0]
    tile_cols = col_time.shape[0]
    row_at = pl.multiple_of(where_ref[0] * tile_rows, 8)
    col_at = pl.multiple_of(where_ref[1] * tile_cols, 8)
    node_copies = [
        pltpu.make_async_copy(
            time_ref.at[pl.ds(row_at, tile_rows)], row_time, node_sem.at[0]
        ),
        pltpu.make_async_copy(
            time_ref.at[pl.ds(col_at, tile_cols)], col_time, node_sem.at[1]
        ),
        pltpu.make_async_copy(
            degree_ref.at[pl.ds(row_at, tile_rows)], row_scale, node_sem.at[2]
        ),
    ]
    for copy in node_copies:
        copy.start()

    def value_copy(chunk):
        part = pl.ds(pl.multiple_of(chunk * CHUNK, CHUNK), CHUNK)
        return pltpu.make_async_copy(
            values_ref.at[0, part], edge_ref.at[part], value_sem.at[chunk]
        )

    for chunk in range(chunks):
        value_copy(chunk).start()
    for copy in node_copies:
        copy.wait()

    decay = decay_ref[0]
    count = count_ref[0, 0]
    later = decay * row_time[...].astype(F32)
    scale = row_scale[...]
    down = (jnp.exp(-later) * scale).T
    up = (jnp.exp(later) * scale).T
    for row in range(tile_rows):
        near_row[row] = jnp.broadcast_to(down[:, row : row + 1], (TILE, TILE))
        far_row[row] = jnp.broadcast_to(up[:, row : row + 1], (TILE, TILE))
    later = decay * col_time[...].astype(F32)
    near_col[...] = jnp.exp(later).reshape(tile_cols, 1, TILE)
    far_col[...] = jnp.exp(-later).reshape(tile_cols, 1, TILE)

    def one_chunk(chunk, carry):
        value_copy(chunk).wait()

        @pl.when(chunk * CHUNK < count)
        def _():
            for offset in range(CHUNK):
                slot = chunk * CHUNK + offset
                row = rows_ref[0, slot]
                col = cols_ref[0, slot]
                inside = jnp.where(slot < count, 1.0, 0.0).astype(F32)
                weight = jnp.minimum(
                    near_row[row] * (near_col[col] * inside),
                    far_row[row] * (far_col[col] * inside),
                )
                edge_ref[slot] = (edge_ref[slot].astype(F32) * weight).astype(BF16)

        return carry

    lax.fori_loop(0, chunks, one_chunk, 0)


def sum_kernel(n, ids_ref, rows_ref, cols_ref, count_ref, *refs):
    blocks = refs[:n]
    edge_ref, out_ref, panel, total = refs[n:]
    for k in range(n):
        at = ids_ref[k] * 2
        panel[at] = blocks[k][:, :TILE]
        panel[at + 1] = blocks[k][:, TILE:]
    total[...] = jnp.zeros_like(total)
    count = count_ref[0, 0]

    def group(index, carry):
        parts = []
        for offset in range(UNROLL):
            slot = index * UNROLL + offset
            parts.append(
                jnp.dot(
                    panel[rows_ref[0, slot]],
                    edge_ref[slot],
                    preferred_element_type=F32,
                )
            )
        for offset in range(UNROLL):
            total[cols_ref[0, index * UNROLL + offset]] += parts[offset]
        return carry

    lax.fori_loop(0, (count + UNROLL - 1) // UNROLL, group, 0)
    for col in range(total.shape[0]):
        half = (col % 2) * TILE
        out_ref[col // 2, :, half : half + TILE] = total[col].astype(BF16)


def finish_kernel(part_ref, feat_t_ref, weight_ref, input_ref, local_ref):
    summed = part_ref[0].astype(F32)
    for k in range(1, part_ref.shape[0]):
        summed = summed + part_ref[k].astype(F32)
    summed = summed.T
    high = summed.astype(BF16)
    low = (summed - high.astype(F32)).astype(BF16)
    input_ref[...] = lax.dot_general(
        high, weight_ref[...], (((1,), (1,)), ((), ())), preferred_element_type=F32
    ).astype(BF16)
    local = jnp.dot(feat_t_ref[...], high, preferred_element_type=F32) + jnp.dot(
        feat_t_ref[...], low, preferred_element_type=F32
    )
    local_ref[...] = local.reshape(local_ref.shape)


def spread_kernel(in_ref, out_ref):
    total = in_ref[0]
    for k in range(1, in_ref.shape[0]):
        total = total + in_ref[k]
    for k in range(out_ref.shape[0]):
        out_ref[k] = total


def shift(block, axis, step):
    size = lax.axis_size(axis)
    return lax.ppermute(block, axis, [(i, (i + step) % size) for i in range(size)])


def gather(own):
    ring = lax.axis_size("z")
    half = ring // 2
    blocks = []
    across = shift(own, "xh", 1)
    for flip, block in ((0, own), (1, across)):
        blocks.append((flip, 0, block))
        for sign in (1, -1):
            reach = half if (sign == 1) == (flip == 0) else half - 1
            moving = block
            for step in range(1, reach + 1):
                moving = shift(moving, "z", sign)
                blocks.append((flip, -sign * step, moving))
    found = []
    for flip, dz, block in blocks:
        found.append((flip, dz, 0, block))
        found.append((flip, dz, 1, shift(block, "c", 1)))
    return found


def shards(
    out_grad,
    pre_act,
    features,
    weight,
    inv_degree,
    node_time,
    decay_rate,
    tile_value,
    tile_row,
    tile_col,
    tile_count,
):
    nodes, width = out_grad.shape
    slots = tile_value.shape[1]
    n_row = lax.axis_size(ROW)
    n_col = lax.axis_size(COL)
    tile_rows = nodes * n_col // TILE
    tile_cols = nodes * n_row // TILE
    where = jnp.stack([lax.axis_index(ROW), lax.axis_index(COL)]).astype(jnp.int32)

    masked, features_t = pl.pallas_call(
        mask_kernel,
        out_shape=(
            jax.ShapeDtypeStruct((width, nodes), BF16),
            jax.ShapeDtypeStruct((features.shape[1], nodes), BF16),
        ),
        in_specs=[VMEM] * 3,
        out_specs=(VMEM, VMEM),
    )(out_grad, pre_act, features)

    found = gather(masked)

    edges = pl.pallas_call(
        edge_kernel,
        out_shape=jax.ShapeDtypeStruct((slots, TILE, TILE), BF16),
        in_specs=[SMEM] * 5 + [ANY] * 3,
        out_specs=VMEM,
        scratch_shapes=[
            pltpu.VMEM((tile_rows, TILE), jnp.int32),
            pltpu.VMEM((tile_cols, TILE), jnp.int32),
            pltpu.VMEM((tile_rows, TILE), F32),
            pltpu.VMEM((tile_rows, TILE, TILE), F32),
            pltpu.VMEM((tile_rows, TILE, TILE), F32),
            pltpu.VMEM((tile_cols, 1, TILE), F32),
            pltpu.VMEM((tile_cols, 1, TILE), F32),
            pltpu.SemaphoreType.DMA((slots // CHUNK,)),
            pltpu.SemaphoreType.DMA((3,)),
        ],
        compiler_params=BIG,
        cost_estimate=pl.CostEstimate(
            flops=6 * slots * TILE * TILE,
            bytes_accessed=4 * slots * TILE * TILE,
            transcendentals=0,
        ),
    )(
        where,
        tile_row,
        tile_col,
        tile_count,
        decay_rate,
        tile_value,
        node_time.reshape(-1, TILE),
        inv_degree.reshape(-1, TILE),
    )

    xh, z, c = (lax.axis_index(name) for name in COL)
    ids = jnp.stack(
        [
            ((xh ^ flip) * lax.axis_size("z") + ((z + dz) % lax.axis_size("z"))) * 2
            + (c ^ other)
            for flip, dz, other, _ in found
        ]
    ).astype(jnp.int32)
    blocks = [block for _, _, _, block in found]
    partial = pl.pallas_call(
        lambda *refs: sum_kernel(len(blocks), *refs),
        out_shape=jax.ShapeDtypeStruct((n_row, width, nodes), BF16),
        in_specs=[SMEM] * 4 + [VMEM] * (len(blocks) + 1),
        out_specs=VMEM,
        scratch_shapes=[
            pltpu.VMEM((tile_rows, width, TILE), BF16),
            pltpu.VMEM((tile_cols, width, TILE), F32),
        ],
        compiler_params=BIG,
    )(ids, tile_row, tile_col, tile_count, *blocks, edges)

    parts = lax.all_to_all(partial, ROW, 0, 0, tiled=True)

    n_near = lax.axis_size(NEAR)
    n_far = lax.axis_size(FAR)
    part_rows = features.shape[1] // n_near
    grad_input, local = pl.pallas_call(
        finish_kernel,
        out_shape=(
            jax.ShapeDtypeStruct((nodes, features.shape[1]), BF16),
            jax.ShapeDtypeStruct((n_near, part_rows, width), F32),
        ),
        in_specs=[VMEM] * 3,
        out_specs=(VMEM, VMEM),
    )(parts, features_t, weight)

    def spread(array, copies):
        return pl.pallas_call(
            spread_kernel,
            out_shape=jax.ShapeDtypeStruct((copies,) + array.shape[1:], F32),
            in_specs=[VMEM],
            out_specs=VMEM,
        )(array)

    slices = lax.all_to_all(local, NEAR, 0, 0, tiled=True)
    slices = lax.all_to_all(spread(slices, n_far), FAR, 0, 0, tiled=True)
    slices = lax.all_to_all(spread(slices, n_near), NEAR, 0, 0, tiled=True)
    return grad_input, slices.reshape(features.shape[1], width)


def solution(mesh):
    fine = Mesh(mesh.devices.reshape(4, 2, 2, 8, 2), ROW + COL)
    placed = (
        P(ROW + COL, None),
        P(ROW + COL, None),
        P(COL + ROW, None),
        P(),
        P(),
        P(),
        P(),
        P(ROW, COL, None, None),
        P(ROW, COL),
        P(ROW, COL),
        P(ROW, COL),
    )
    return jax.shard_map(
        shards,
        mesh=fine,
        in_specs=placed,
        out_specs=(P(COL + ROW, None), P()),
        check_vma=False,
    )
```

time: 918 us -> 135 us (0.15)
  waiting for transfers between devices: 837 us -> 6.99 us
  blocking collectives: 0 us -> 66.9 us
  local copies, waits for them, and re-layouts: 50.4 us -> 4.08 us
  starting transfers between devices: 0.12 us -> 34.1 us
  Pallas kernels: 0 us -> 19.6 us
  between operations: 15.1 us -> 2.04 us
    reduce_scatter x1 -> x0, waiting for transfers between devices: 504 us -> none  [shards(): lax.psum_scatter(partial_value.reshape(cols_per_block, width_out), 'row',...]
    psum x1 -> x0, waiting for transfers between devices: 251 us -> none  [shards(): weight_grad = lax.psum(local_grad, ('row', 'col'))]
    all_gather x1 -> x0, waiting for transfers between devices: 83.2 us -> none  [shards(): gathered = lax.all_gather(masked_grad, 'col', axis=0, tiled=True)]
    all_to_all x0 -> x4, blocking collectives: none -> 66.9 us  [the longest x1 23.5 us: shards(): parts = lax.all_to_all(partial, ROW, 0, 0, tiled=True)]
    gather x4 -> x0, local copies, waits for them, and re-layouts: 38.1 us -> none  [the longest x1 11.8 us: edge_tiles(): source_scale = jnp.take(row_scale, source_index, axis=0, mode='clip')]
    ppermute x0 -> x31, starting transfers between devices: none -> 34.1 us  [shift(): lax.ppermute(block, axis, [(i, (i + step) % size) for i in range(size)])]
    pallas_call x0 -> x6, Pallas kernels: none -> 19.6 us  [the longest x1 6.43 us: shards(): pl.pallas_call(edge_kernel, out_shape=jax.ShapeDtypeStruct((slots, TILE,...]
  transfers between devices with their start and end apart: 3 -> 31, of which waited for: 3 -> 8; matrix products, arithmetic and copies ran while one was open for 1% -> 0% of each run, Pallas kernels for 0% -> 5%
where the time goes in v1:
time: 135 us; the launch traced here: 134 us
  blocking collectives  66.9 us (50%)
  starting transfers between devices  34.1 us (25%)
  Pallas kernels  19.6 us (15%)
  waiting for transfers between devices  6.99 us (5%)
  local copies, waits for them, and re-layouts  4.08 us (3%)
  between operations  2.04 us (2%)
    ppermute x31, starting transfers between devices, shift(): lax.ppermute(block, axis, [(i, (i + step) % size) for i in range(size)])  34.1 us
    all_to_all x1, blocking collectives, shards(): parts = lax.all_to_all(partial, ROW, 0, 0, tiled=True)  23.5 us
    all_to_all x1, blocking collectives, shards(): slices = lax.all_to_all(spread(slices, n_far), FAR, 0, 0, tiled=True)  15.8 us
    all_to_all x1, blocking collectives, shards(): slices = lax.all_to_all(local, NEAR, 0, 0, tiled=True)  13.9 us
    all_to_all x1, blocking collectives, shards(): slices = lax.all_to_all(spread(slices, n_near), NEAR, 0, 0, tiled=True)  13.6 us
    ppermute x31, waiting for transfers between devices, shift(): lax.ppermute(block, axis, [(i, (i + step) % size) for i in range(size)])  6.99 us
    pallas_call x1, Pallas kernels, shards(): pl.pallas_call(edge_kernel, out_shape=jax.ShapeDtypeStruct((slots, TILE,...  6.43 us
    pallas_call x1, Pallas kernels, shards(): pl.pallas_call(lambda *refs: sum_kernel(len(blocks), *refs), out_shape=ja...  5.45 us
  transfers between devices with their start and end apart: 31, of which 8 were waited for; matrix products, arithmetic and copies ran while one was open for 0% of the time, Pallas kernels for 5%

profile of v1, /device:TPU:1, one launch (start us, length us, event | category | flops | bytes accessed | tf_op | source)
XLA Modules:
  0.0 133.8 jit_solution(1500623525137490550)
XLA Ops:
  0.6 1.8 %shard_map.122 = (bf16[256,256]{1,0:T(8,128)(2,1)}, bf16[256,256]{1,0:T(8,128)(2,1)}) custom-call(bf16[256,256]{1,0:T(8,128)(2,1)} %grad_ref.1, bf16[256,256]{1,0:T(8,128)(2,1)} %act_ref.1, bf16[256,256]{1,0:T(8,128)(2,1)} %feat_ref.1), custom_call_target="tpu_custom_call" | custom-call | tf_op jit(solution)/shard_map/pallas_call | solution.py:216
  2.5 3.6 %collective-permute-start.15 = (bf16[256,256]{1,0:T(8,128)(2,1)}, bf16[256,256]{1,0:T(8,128)(2,1)S(1)}, u32[]{:S(2)}, u32[]{:S(2)}) collective-permute-start(bf16[256,256]{1,0:T(8,128)(2,1)} %get-tuple-element.6.refs_4_), channel_id=1, source_target_pairs={{0,16},{16,0},{1,17},{17,1},{2,18},{18,2},{3,19},{19,3},{4,20},{20... | collective-permute-start | bytes 393224 | tf_op jit(solution)/shard_map/ppermute | solution.py:172
  6.0 5.6 %collective-permute-start.9 = (bf16[256,256]{1,0:T(8,128)(2,1)}, bf16[256,256]{1,0:T(8,128)(2,1)S(1)}, u32[]{:S(2)}, u32[]{:S(2)}) collective-permute-start(bf16[256,256]{1,0:T(8,128)(2,1)} %get-tuple-element.6.refs_4_), channel_id=1, source_target_pairs={{0,14},{2,0},{4,2},{6,4},{8,6},{10,8},{12,10},{14,12},{1,15},{3,1}... | collective-permute-start | bytes 393224 | tf_op jit(solution)/shard_map/ppermute | solution.py:172
  11.6 1.2 collective-permute-start
  12.9 3.0 %collective-permute-start.23 = (bf16[256,256]{1,0:T(8,128)(2,1)S(1)}, bf16[256,256]{1,0:T(8,128)(2,1)S(1)}, u32[]{:S(2)}, u32[]{:S(2)}) collective-permute-start(bf16[256,256]{1,0:T(8,128)(2,1)S(1)} %collective-permute-done.15.refs_20_), channel_id=1, source_target_pairs={{0,14},{2,0},{4,2},{6,4},{8,6},{10,8},{12,10},{14,12},{1,15},{3,1}... | collective-permute-start | bytes 393224 | tf_op jit(solution)/shard_map/ppermute | solution.py:172
  15.8 1.0 collective-permute-start.16
  16.9 2.9 %collective-permute-start.11 = (bf16[256,256]{1,0:T(8,128)(2,1)S(1)}, bf16[256,256]{1,0:T(8,128)(2,1)S(1)}, u32[]{:S(2)}, u32[]{:S(2)}) collective-permute-start(bf16[256,256]{1,0:T(8,128)(2,1)S(1)} %collective-permute-done.9.refs_14_), channel_id=1, source_target_pairs={{0,14},{2,0},{4,2},{6,4},{8,6},{10,8},{12,10},{14,12},{1,15},{3,1}... | collective-permute-start | bytes 393224 | tf_op jit(solution)/shard_map/ppermute | solution.py:172
  21.0 1.9 %collective-permute-start.2 = (bf16[256,256]{1,0:T(8,128)(2,1)S(1)}, bf16[256,256]{1,0:T(8,128)(2,1)S(1)}, u32[]{:S(2)}, u32[]{:S(2)}) collective-permute-start(bf16[256,256]{1,0:T(8,128)(2,1)S(1)} %collective-permute-done.1.refs_6_), channel_id=1, source_target_pairs={{0,1},{1,0},{2,3},{3,2},{4,5},{5,4},{6,7},{7,6},{8,9},{9,8},{10,11... | collective-permute-start | bytes 393224 | tf_op jit(solution)/shard_map/ppermute | solution.py:172
  24.7 1.5 %collective-permute-done.3.refs_8_ = bf16[256,256]{1,0:T(8,128)(2,1)S(1)} collective-permute-done((bf16[256,256]{1,0:T(8,128)(2,1)S(1)}, bf16[256,256]{1,0:T(8,128)(2,1)S(1)}, u32[]{:S(2)}, u32[]{:S(2)}) %collective-permute-start.3) | collective-permute-done | bytes 131104 | tf_op jit(solution)/shard_map/ppermute | solution.py:172
  29.0 1.6 %collective-permute-done.19.refs_24_ = bf16[256,256]{1,0:T(8,128)(2,1)S(1)} collective-permute-done((bf16[256,256]{1,0:T(8,128)(2,1)S(1)}, bf16[256,256]{1,0:T(8,128)(2,1)S(1)}, u32[]{:S(2)}, u32[]{:S(2)}) %collective-permute-start.19) | collective-permute-done | bytes 131104 | tf_op jit(solution)/shard_map/ppermute | solution.py:172
  31.3 1.5 %collective-permute-start.27 = (bf16[256,256]{1,0:T(8,128)(2,1)S(1)}, bf16[256,256]{1,0:T(8,128)(2,1)S(1)}, u32[]{:S(2)}, u32[]{:S(2)}) collective-permute-start(bf16[256,256]{1,0:T(8,128)(2,1)S(1)} %collective-permute-done.25.refs_30_), channel_id=1, source_target_pairs={{0,14},{2,0},{4,2},{6,4},{8,6},{10,8},{12,10},{14,12},{1,15},{3,1}... | collective-permute-start | bytes 393224 | tf_op jit(solution)/shard_map/ppermute | solution.py:172
  33.2 2.1 %collective-permute-done.5.refs_10_ = bf16[256,256]{1,0:T(8,128)(2,1)S(1)} collective-permute-done((bf16[256,256]{1,0:T(8,128)(2,1)S(1)}, bf16[256,256]{1,0:T(8,128)(2,1)S(1)}, u32[]{:S(2)}, u32[]{:S(2)}) %collective-permute-start.5) | collective-permute-done | bytes 131104 | tf_op jit(solution)/shard_map/ppermute | solution.py:172
  36.5 2.7 %collective-permute-start.29 = (bf16[256,256]{1,0:T(8,128)(2,1)S(1)}, bf16[256,256]{1,0:T(8,128)(2,1)S(1)}, u32[]{:S(2)}, u32[]{:S(2)}) collective-permute-start(bf16[256,256]{1,0:T(8,128)(2,1)S(1)} %collective-permute-done.27.refs_32_), channel_id=1, source_target_pairs={{0,14},{2,0},{4,2},{6,4},{8,6},{10,8},{12,10},{14,12},{1,15},{3,1}... | collective-permute-start | bytes 393224 | tf_op jit(solution)/shard_map/ppermute | solution.py:172
  39.3 1.2 collective-permute-start.6
  41.9 1.7 %collective-permute-start.8 = (bf16[256,256]{1,0:T(8,128)(2,1)S(1)}, bf16[256,256]{1,0:T(8,128)(2,1)}, u32[]{:S(2)}, u32[]{:S(2)}) collective-permute-start(bf16[256,256]{1,0:T(8,128)(2,1)S(1)} %collective-permute-done.7.refs_12_), channel_id=1, source_target_pairs={{0,1},{1,0},{2,3},{3,2},{4,5},{5,4},{6,7},{7,6},{8,9},{9,8},{10,11... | collective-permute-start | bytes 393224 | tf_op jit(solution)/shard_map/ppermute | solution.py:172
  48.4 6.4 %shard_map.123.refs_36_ = bf16[176,128,128]{2,1,0:T(8,128)(2,1)} custom-call(s32[2]{0:T(128)S(1)} %pad_add_fusion.where_ref, s32[1,176]{1,0:T(1,128)S(1)} %copy-done.3, s32[1,176]{1,0:T(1,128)S(1)} %copy-done.4, s32[1,1]{1,0:T(1,128)S(6)} %copy.15.count_ref.refs_3_, f32[1]{0:T(128)S(6)} %copy.14.decay_ref, bf16[1,176,128,128]{3,2,1,0:T(8,128)(2,1)} %values_ref.1, ...), custom_call_target="tpu_custom_call" | custom-call | flops 17301504 | bytes 11534336 | tf_op jit(solution)/shard_map/pallas_call | solution.py:228
  54.9 5.4 %shard_map.124 = bf16[8,256,256]{2,1,0:T(8,128)(2,1)S(1)} custom-call(s32[32]{0:T(128)S(1)} %stack.140.refs_0_, s32[1,176]{1,0:T(1,128)S(1)} %copy-done.3, s32[1,176]{1,0:T(1,128)S(1)} %copy-done.4, s32[1,1]{1,0:T(1,128)S(6)} %copy.15.count_ref.refs_3_, bf16[256,256]{1,0:T(8,128)(2,1)S(1)} %copy-done.2, bf16[256,256]{1,0:T(8,128)(2,1)S(1)} %collective-permute-done.refs_5_, ...), custom_call_target="tpu_custom_call" | custom-call | tf_op jit(solution)/shard_map/pallas_call | solution.py:270
  60.3 23.5 %all_to_all.20.part_ref = bf16[8,256,256]{2,1,0:T(8,128)(2,1)} all-to-all(bf16[8,256,256]{2,1,0:T(8,128)(2,1)S(1)} %shard_map.124), channel_id=1, replica_groups=mesh['y'=4,'xl'=2,'xh'=2,'z'=8,'c'=2] {'y','xl'}, dimensions={0} | all-to-all | bytes 2097152 | tf_op jit(solution)/shard_map/all_to_all | solution.py:282
  83.9 2.5 %shard_map.125 = (bf16[256,256]{1,0:T(8,128)(2,1)}, f32[16,16,256]{2,1,0:T(8,128)}) custom-call(bf16[8,256,256]{2,1,0:T(8,128)(2,1)} %all_to_all.20.part_ref, bf16[256,256]{1,0:T(8,128)(2,1)} %get-tuple-element.7.feat_t_ref, bf16[256,256]{1,0:T(8,128)(2,1)} %weight_ref.1), custom_call_target="tpu_custom_call" | custom-call | tf_op jit(solution)/shard_map/pallas_call | solution.py:287
  86.3 13.9 %all_to_all.21.in_ref = f32[16,16,256]{2,1,0:T(8,128)} all-to-all(f32[16,16,256]{2,1,0:T(8,128)} %get-tuple-element.9), channel_id=1, replica_groups=mesh['y'=4,'xl'=2,'xh'=2,'z'=8,'c'=2] {'y','xl','c'}, dimensions={0} | all-to-all | bytes 524288 | tf_op jit(solution)/shard_map/all_to_all | solution.py:305
  100.2 1.7 %shard_map.126 = f32[16,16,256]{2,1,0:T(8,128)} custom-call(f32[16,16,256]{2,1,0:T(8,128)} %all_to_all.21.in_ref), custom_call_target="tpu_custom_call" | custom-call | tf_op jit(solution)/shard_map/pallas_call | solution.py:298
  101.9 15.8 %all_to_all.22.in_ref = f32[16,16,256]{2,1,0:T(8,128)} all-to-all(f32[16,16,256]{2,1,0:T(8,128)} %shard_map.126), channel_id=1, replica_groups=mesh['y'=4,'xl'=2,'xh'=2,'z'=8,'c'=2] {'xh','z'}, dimensions={0} | all-to-all | bytes 524288 | tf_op jit(solution)/shard_map/all_to_all | solution.py:306
  117.8 1.7 %shard_map.127 = f32[16,16,256]{2,1,0:T(8,128)} custom-call(f32[16,16,256]{2,1,0:T(8,128)} %all_to_all.22.in_ref), custom_call_target="tpu_custom_call" | custom-call | tf_op jit(solution)/shard_map/pallas_call | solution.py:298
  119.5 13.6 %all_to_all.23 = f32[16,16,256]{2,1,0:T(8,128)S(1)} all-to-all(f32[16,16,256]{2,1,0:T(8,128)} %shard_map.127), channel_id=1, replica_groups=mesh['y'=4,'xl'=2,'xh'=2,'z'=8,'c'=2] {'y','xl','c'}, dimensions={0} | all-to-all | bytes 524288 | tf_op jit(solution)/shard_map/all_to_all | solution.py:307
  (61 shorter events, 14.0 us)
Async XLA Ops:
  2.5 10.4 %collective-permute-start.15 = (bf16[256,256]{1,0:T(8,128)(2,1)}, bf16[256,256]{1,0:T(8,128)(2,1)S(1)}, u32[]{:S(2)}, u32[]{:S(2)}) collective-permute-start(bf16[256,256]{1,0:T(8,128)(2,1)} %get-tuple-element.6.refs_4_), channel_id=1, source_target_pairs={{0,16},{16,0},{1,17},{17,1},{2,18},{18,2},{3,19},{19,3},{4,20},{20... | collective-permute-start | bytes 393224 | tf_op jit(solution)/shard_map/ppermute | solution.py:172
  6.0 9.8 %collective-permute-start.9 = (bf16[256,256]{1,0:T(8,128)(2,1)}, bf16[256,256]{1,0:T(8,128)(2,1)S(1)}, u32[]{:S(2)}, u32[]{:S(2)}) collective-permute-start(bf16[256,256]{1,0:T(8,128)(2,1)} %get-tuple-element.6.refs_4_), channel_id=1, source_target_pairs={{0,14},{2,0},{4,2},{6,4},{8,6},{10,8},{12,10},{14,12},{1,15},{3,1}... | collective-permute-start | bytes 393224 | tf_op jit(solution)/shard_map/ppermute | solution.py:172
  11.6 5.2 %collective-permute-start.1 = (bf16[256,256]{1,0:T(8,128)(2,1)}, bf16[256,256]{1,0:T(8,128)(2,1)S(1)}, u32[]{:S(2)}, u32[]{:S(2)}) collective-permute-start(bf16[256,256]{1,0:T(8,128)(2,1)} %get-tuple-element.6.refs_4_), channel_id=1, source_target_pairs={{0,2},{2,4},{4,6},{6,8},{8,10},{10,12},{12,14},{14,0},{1,3},{3,5},... | collective-permute-start | bytes 393224 | tf_op jit(solution)/shard_map/ppermute | solution.py:172
  11.6 8.1 %collective-permute-start = (bf16[256,256]{1,0:T(8,128)(2,1)}, bf16[256,256]{1,0:T(8,128)(2,1)S(1)}, u32[]{:S(2)}, u32[]{:S(2)}) collective-permute-start(bf16[256,256]{1,0:T(8,128)(2,1)} %get-tuple-element.6.refs_4_), channel_id=1, source_target_pairs={{0,1},{1,0},{2,3},{3,2},{4,5},{5,4},{6,7},{7,6},{8,9},{9,8},{10,11... | collective-permute-start | bytes 393224 | tf_op jit(solution)/shard_map/ppermute | solution.py:172
  12.9 7.3 %collective-permute-start.23 = (bf16[256,256]{1,0:T(8,128)(2,1)S(1)}, bf16[256,256]{1,0:T(8,128)(2,1)S(1)}, u32[]{:S(2)}, u32[]{:S(2)}) collective-permute-start(bf16[256,256]{1,0:T(8,128)(2,1)S(1)} %collective-permute-done.15.refs_20_), channel_id=1, source_target_pairs={{0,14},{2,0},{4,2},{6,4},{8,6},{10,8},{12,10},{14,12},{1,15},{3,1}... | collective-permute-start | bytes 393224 | tf_op jit(solution)/shard_map/ppermute | solution.py:172
  15.8 5.2 %collective-permute-start.17 = (bf16[256,256]{1,0:T(8,128)(2,1)S(1)}, bf16[256,256]{1,0:T(8,128)(2,1)S(1)}, u32[]{:S(2)}, u32[]{:S(2)}) collective-permute-start(bf16[256,256]{1,0:T(8,128)(2,1)S(1)} %collective-permute-done.15.refs_20_), channel_id=1, source_target_pairs={{0,2},{2,4},{4,6},{6,8},{8,10},{10,12},{12,14},{14,0},{1,3},{3,5},... | collective-permute-start | bytes 393224 | tf_op jit(solution)/shard_map/ppermute | solution.py:172
  15.8 7.1 %collective-permute-start.16 = (bf16[256,256]{1,0:T(8,128)(2,1)S(1)}, bf16[256,256]{1,0:T(8,128)(2,1)S(1)}, u32[]{:S(2)}, u32[]{:S(2)}) collective-permute-start(bf16[256,256]{1,0:T(8,128)(2,1)S(1)} %collective-permute-done.15.refs_20_), channel_id=1, source_target_pairs={{0,1},{1,0},{2,3},{3,2},{4,5},{5,4},{6,7},{7,6},{8,9},{9,8},{10,11... | collective-permute-start | bytes 393224 | tf_op jit(solution)/shard_map/ppermute | solution.py:172
  16.9 6.4 %collective-permute-start.11 = (bf16[256,256]{1,0:T(8,128)(2,1)S(1)}, bf16[256,256]{1,0:T(8,128)(2,1)S(1)}, u32[]{:S(2)}, u32[]{:S(2)}) collective-permute-start(bf16[256,256]{1,0:T(8,128)(2,1)S(1)} %collective-permute-done.9.refs_14_), channel_id=1, source_target_pairs={{0,14},{2,0},{4,2},{6,4},{8,6},{10,8},{12,10},{14,12},{1,15},{3,1}... | collective-permute-start | bytes 393224 | tf_op jit(solution)/shard_map/ppermute | solution.py:172
  20.1 6.2 %collective-permute-start.3 = (bf16[256,256]{1,0:T(8,128)(2,1)S(1)}, bf16[256,256]{1,0:T(8,128)(2,1)S(1)}, u32[]{:S(2)}, u32[]{:S(2)}) collective-permute-start(bf16[256,256]{1,0:T(8,128)(2,1)S(1)} %collective-permute-done.1.refs_6_), channel_id=1, source_target_pairs={{0,2},{2,4},{4,6},{6,8},{8,10},{10,12},{12,14},{14,0},{1,3},{3,5},... | collective-permute-start | bytes 393224 | tf_op jit(solution)/shard_map/ppermute | solution.py:172
  21.0 6.2 %collective-permute-start.2 = (bf16[256,256]{1,0:T(8,128)(2,1)S(1)}, bf16[256,256]{1,0:T(8,128)(2,1)S(1)}, u32[]{:S(2)}, u32[]{:S(2)}) collective-permute-start(bf16[256,256]{1,0:T(8,128)(2,1)S(1)} %collective-permute-done.1.refs_6_), channel_id=1, source_target_pairs={{0,1},{1,0},{2,3},{3,2},{4,5},{5,4},{6,7},{7,6},{8,9},{9,8},{10,11... | collective-permute-start | bytes 393224 | tf_op jit(solution)/shard_map/ppermute | solution.py:172
  23.3 5.6 %collective-permute-start.24 = (bf16[256,256]{1,0:T(8,128)(2,1)S(1)}, bf16[256,256]{1,0:T(8,128)(2,1)S(1)}, u32[]{:S(2)}, u32[]{:S(2)}) collective-permute-start(bf16[256,256]{1,0:T(8,128)(2,1)S(1)} %collective-permute-done.23.refs_28_), channel_id=1, source_target_pairs={{0,1},{1,0},{2,3},{3,2},{4,5},{5,4},{6,7},{7,6},{8,9},{9,8},{10,11... | collective-permute-start | bytes 393224 | tf_op jit(solution)/shard_map/ppermute | solution.py:172
  24.2 6.3 %collective-permute-start.19 = (bf16[256,256]{1,0:T(8,128)(2,1)S(1)}, bf16[256,256]{1,0:T(8,128)(2,1)S(1)}, u32[]{:S(2)}, u32[]{:S(2)}) collective-permute-start(bf16[256,256]{1,0:T(8,128)(2,1)S(1)} %collective-permute-done.17.refs_22_), channel_id=1, source_target_pairs={{0,2},{2,4},{4,6},{6,8},{8,10},{10,12},{12,14},{14,0},{1,3},{3,5},... | collective-permute-start | bytes 393224 | tf_op jit(solution)/shard_map/ppermute | solution.py:172
  27.2 5.6 %collective-permute-start.13 = (bf16[256,256]{1,0:T(8,128)(2,1)S(1)}, bf16[256,256]{1,0:T(8,128)(2,1)S(1)}, u32[]{:S(2)}, u32[]{:S(2)}) collective-permute-start(bf16[256,256]{1,0:T(8,128)(2,1)S(1)} %collective-permute-done.11.refs_16_), channel_id=1, source_target_pairs={{0,14},{2,0},{4,2},{6,4},{8,6},{10,8},{12,10},{14,12},{1,15},{3,1}... | collective-permute-start | bytes 393224 | tf_op jit(solution)/shard_map/ppermute | solution.py:172
  28.9 6.3 %collective-permute-start.5 = (bf16[256,256]{1,0:T(8,128)(2,1)S(1)}, bf16[256,256]{1,0:T(8,128)(2,1)S(1)}, u32[]{:S(2)}, u32[]{:S(2)}) collective-permute-start(bf16[256,256]{1,0:T(8,128)(2,1)S(1)} %collective-permute-done.3.refs_8_), channel_id=1, source_target_pairs={{0,2},{2,4},{4,6},{6,8},{8,10},{10,12},{12,14},{14,0},{1,3},{3,5},... | collective-permute-start | bytes 393224 | tf_op jit(solution)/shard_map/ppermute | solution.py:172
  30.6 5.5 %collective-permute-start.4 = (bf16[256,256]{1,0:T(8,128)(2,1)S(1)}, bf16[256,256]{1,0:T(8,128)(2,1)S(1)}, u32[]{:S(2)}, u32[]{:S(2)}) collective-permute-start(bf16[256,256]{1,0:T(8,128)(2,1)S(1)} %collective-permute-done.3.refs_8_), channel_id=1, source_target_pairs={{0,1},{1,0},{2,3},{3,2},{4,5},{5,4},{6,7},{7,6},{8,9},{9,8},{10,11... | collective-permute-start | bytes 393224 | tf_op jit(solution)/shard_map/ppermute | solution.py:172
  33.2 6.2 %collective-permute-start.21 = (bf16[256,256]{1,0:T(8,128)(2,1)S(1)}, bf16[256,256]{1,0:T(8,128)(2,1)S(1)}, u32[]{:S(2)}, u32[]{:S(2)}) collective-permute-start(bf16[256,256]{1,0:T(8,128)(2,1)S(1)} %collective-permute-done.19.refs_24_), channel_id=1, source_target_pairs={{0,2},{2,4},{4,6},{6,8},{8,10},{10,12},{12,14},{14,0},{1,3},{3,5},... | collective-permute-start | bytes 393224 | tf_op jit(solution)/shard_map/ppermute | solution.py:172
  35.2 5.3 %collective-permute-start.20 = (bf16[256,256]{1,0:T(8,128)(2,1)S(1)}, bf16[256,256]{1,0:T(8,128)(2,1)S(1)}, u32[]{:S(2)}, u32[]{:S(2)}) collective-permute-start(bf16[256,256]{1,0:T(8,128)(2,1)S(1)} %collective-permute-done.19.refs_24_), channel_id=1, source_target_pairs={{0,1},{1,0},{2,3},{3,2},{4,5},{5,4},{6,7},{7,6},{8,9},{9,8},{10,11... | collective-permute-start | bytes 393224 | tf_op jit(solution)/shard_map/ppermute | solution.py:172
  36.5 5.5 %collective-permute-start.7 = (bf16[256,256]{1,0:T(8,128)(2,1)S(1)}, bf16[256,256]{1,0:T(8,128)(2,1)S(1)}, u32[]{:S(2)}, u32[]{:S(2)}) collective-permute-start(bf16[256,256]{1,0:T(8,128)(2,1)S(1)} %collective-permute-done.5.refs_10_), channel_id=1, source_target_pairs={{0,2},{2,4},{4,6},{6,8},{8,10},{10,12},{12,14},{14,0},{1,3},{3,5},... | collective-permute-start | bytes 393224 | tf_op jit(solution)/shard_map/ppermute | solution.py:172
  36.5 7.1 %collective-permute-start.29 = (bf16[256,256]{1,0:T(8,128)(2,1)S(1)}, bf16[256,256]{1,0:T(8,128)(2,1)S(1)}, u32[]{:S(2)}, u32[]{:S(2)}) collective-permute-start(bf16[256,256]{1,0:T(8,128)(2,1)S(1)} %collective-permute-done.27.refs_32_), channel_id=1, source_target_pairs={{0,14},{2,0},{4,2},{6,4},{8,6},{10,8},{12,10},{14,12},{1,15},{3,1}... | collective-permute-start | bytes 393224 | tf_op jit(solution)/shard_map/ppermute | solution.py:172
  39.3 15.5 %collective-permute-start.6 = (bf16[256,256]{1,0:T(8,128)(2,1)S(1)}, bf16[256,256]{1,0:T(8,128)(2,1)S(1)}, u32[]{:S(2)}, u32[]{:S(2)}) collective-permute-start(bf16[256,256]{1,0:T(8,128)(2,1)S(1)} %collective-permute-done.5.refs_10_), channel_id=1, source_target_pairs={{0,1},{1,0},{2,3},{3,2},{4,5},{5,4},{6,7},{7,6},{8,9},{9,8},{10,11... | collective-permute-start | bytes 393224 | tf_op jit(solution)/shard_map/ppermute | solution.py:172
  40.5 14.3 %collective-permute-start.28 = (bf16[256,256]{1,0:T(8,128)(2,1)S(1)}, bf16[256,256]{1,0:T(8,128)(2,1)}, u32[]{:S(2)}, u32[]{:S(2)}) collective-permute-start(bf16[256,256]{1,0:T(8,128)(2,1)S(1)} %collective-permute-done.27.refs_32_), channel_id=1, source_target_pairs={{0,1},{1,0},{2,3},{3,2},{4,5},{5,4},{6,7},{7,6},{8,9},{9,8},{10,11... | collective-permute-start | bytes 393224 | tf_op jit(solution)/shard_map/ppermute | solution.py:172
  40.6 14.2 %collective-permute-start.22 = (bf16[256,256]{1,0:T(8,128)(2,1)S(1)}, bf16[256,256]{1,0:T(8,128)(2,1)}, u32[]{:S(2)}, u32[]{:S(2)}) collective-permute-start(bf16[256,256]{1,0:T(8,128)(2,1)S(1)} %collective-permute-done.21.refs_26_), channel_id=1, source_target_pairs={{0,1},{1,0},{2,3},{3,2},{4,5},{5,4},{6,7},{7,6},{8,9},{9,8},{10,11... | collective-permute-start | bytes 393224 | tf_op jit(solution)/shard_map/ppermute | solution.py:172
  41.9 12.9 %collective-permute-start.8 = (bf16[256,256]{1,0:T(8,128)(2,1)S(1)}, bf16[256,256]{1,0:T(8,128)(2,1)}, u32[]{:S(2)}, u32[]{:S(2)}) collective-permute-start(bf16[256,256]{1,0:T(8,128)(2,1)S(1)} %collective-permute-done.7.refs_12_), channel_id=1, source_target_pairs={{0,1},{1,0},{2,3},{3,2},{4,5},{5,4},{6,7},{7,6},{8,9},{9,8},{10,11... | collective-permute-start | bytes 393224 | tf_op jit(solution)/shard_map/ppermute | solution.py:172
  43.6 11.2 %collective-permute-start.30 = (bf16[256,256]{1,0:T(8,128)(2,1)S(1)}, bf16[256,256]{1,0:T(8,128)(2,1)}, u32[]{:S(2)}, u32[]{:S(2)}) collective-permute-start(bf16[256,256]{1,0:T(8,128)(2,1)S(1)} %collective-permute-done.29.refs_34_), channel_id=1, source_target_pairs={{0,1},{1,0},{2,3},{3,2},{4,5},{5,4},{6,7},{7,6},{8,9},{9,8},{10,11... | collective-permute-start | bytes 393224 | tf_op jit(solution)/shard_map/ppermute | solution.py:172
  (12 other events, 42.9 us)

commit v2 on v0

v2 whole, which is shorter than its diff:
```python
import functools

import jax
import jax.numpy as jnp
from jax import lax
from jax.experimental import pallas as pl
from jax.experimental.pallas import tpu as pltpu
from jax.sharding import Mesh, PartitionSpec as P

ROW = ("y", "xl")
COL = ("xh", "z", "c")
NEAR = ROW + ("c",)
FAR = ("xh", "z")
TILE = 128
UNROLL = 4
STAGES = ((0, 1), (2, 3), (4, 5, 6))
VMEM = pl.BlockSpec(memory_space=pltpu.VMEM)
SMEM = pl.BlockSpec(memory_space=pltpu.SMEM)
HBM = pl.BlockSpec(memory_space=pltpu.HBM)
ROOM = pltpu.CompilerParams(vmem_limit_bytes=20 << 20)
TIGHT = pltpu.CompilerParams(vmem_limit_bytes=8 << 20)
F32 = jnp.float32
BF16 = jnp.bfloat16


def mask_kernel(grad_ref, act_ref, out_ref):
    grad = grad_ref[...].astype(F32)
    kept = jnp.where(act_ref[...].astype(F32) > 0, grad, 0.0)
    out_ref[...] = kept.T.astype(BF16)


def turn_kernel(in_ref, out_ref):
    out_ref[...] = in_ref[...].astype(F32).T.astype(BF16)


def table_kernel(
    where_ref,
    count_ref,
    decay_ref,
    rows_ref,
    time_ref,
    degree_ref,
    near_row,
    far_row,
    near_col,
    far_col,
    ends_ref,
    row_time,
    col_time,
    row_scale,
    node_sem,
):
    tile_rows = row_time.shape[0]
    tile_cols = col_time.shape[0]
    row_at = pl.multiple_of(where_ref[0] * tile_rows, 8)
    col_at = pl.multiple_of(where_ref[1] * tile_cols, 8)
    copies = [
        (time_ref.at[pl.ds(row_at, tile_rows)], row_time),
        (time_ref.at[pl.ds(col_at, tile_cols)], col_time),
        (degree_ref.at[pl.ds(row_at, tile_rows)], row_scale),
    ]
    copies = [
        pltpu.make_async_copy(src, dst, node_sem.at[k])
        for k, (src, dst) in enumerate(copies)
    ]
    for copy in copies:
        copy.start()

    xh, z, ring = where_ref[2], where_ref[3], where_ref[5]
    slot = lax.broadcasted_iota(jnp.int32, rows_ref.shape, 1)
    rows = jnp.where(slot < count_ref[0, 0], rows_ref[...], tile_rows)
    half = ring // 2
    here, there = xh * ring, (xh ^ 1) * ring
    last = here + lax.rem(z + half, ring)
    open_at = lax.rem(z + half - 1, ring)
    wrapped = open_at > ring - 3
    shut_at = jnp.where(wrapped, open_at + 3 - ring, open_at + 3)
    chips = (
        (here, last),
        (last + 1, here + ring),
        (there + jnp.where(wrapped, shut_at, 0), there + open_at),
        (there + jnp.where(wrapped, ring, shut_at), there + ring),
        (last, last + 1),
        (there + open_at, there + jnp.where(wrapped, ring, shut_at)),
        (there, there + jnp.where(wrapped, shut_at, 0)),
    )
    for k, pair in enumerate(chips):
        for side, chip in enumerate(pair):
            ends_ref[2 * k + side] = jnp.sum(
                jnp.where(rows < chip * 4, 1, 0).astype(jnp.int32)
            )

    for copy in copies:
        copy.wait()
    decay = decay_ref[0]
    later = decay * row_time[...].astype(F32)
    scale = row_scale[...]
    down = (jnp.exp(-later) * scale).T
    up = (jnp.exp(later) * scale).T
    for row in range(tile_rows):
        near_row[row] = jnp.broadcast_to(down[:, row : row + 1], (TILE, TILE))
        far_row[row] = jnp.broadcast_to(up[:, row : row + 1], (TILE, TILE))
    later = decay * col_time[...].astype(F32)
    near_col[...] = jnp.exp(later).reshape(tile_cols, 1, TILE)
    far_col[...] = jnp.exp(-later).reshape(tile_cols, 1, TILE)


def take_panels(places, blocks, where_ref, panel):
    xh, z, c, ring = (where_ref[k] for k in range(2, 6))
    for (flip, dz, other), block in zip(places, blocks):
        chip = (xh ^ flip) * ring + lax.rem(z + (2 * c - 1) * dz + ring, ring)
        for k in range(block.shape[0]):
            at = chip * 4 + (c ^ other ^ k) * 2
            panel[at] = block[k, :, :TILE]
            panel[at + 1] = block[k, :, TILE:]


def add_slots(ranges, ints, tables, values_ref, panel, total):
    rows_ref, cols_ref = ints
    near_row, far_row, near_col, far_col = tables
    slots = rows_ref.shape[1]
    empty = jnp.zeros((TILE, TILE), BF16)
    lengths = [end - start for start, end in ranges]
    live = sum(lengths)

    def find(place):
        index = jnp.minimum(place, live - 1)
        slot = ranges[0][0] + index
        before = lengths[0]
        for (start, _), length in zip(ranges[1:], lengths[1:]):
            slot = jnp.where(index < before, slot, start + index - before)
            before = before + length
        return slot, jnp.where(place < live, 1.0, 0.0).astype(F32)

    def edges(slot, row, col, inside):
        weight = jnp.minimum(
            near_row[row] * (near_col[col] * inside),
            far_row[row] * (far_col[col] * inside),
        )
        return (values_ref[0, slot].astype(F32) * weight).astype(BF16)

    def group(index, carry):
        parts = []
        for k in range(UNROLL):
            at = index * (2 * UNROLL) + 2 * k
            left, left_in = find(at)
            right, right_in = find(at + 1)
            left_row, left_col = rows_ref[0, left], cols_ref[0, left]
            right_row, right_col = rows_ref[0, right], cols_ref[0, right]
            upper = jnp.concatenate(
                [edges(left, left_row, left_col, left_in), empty], axis=1
            )
            lower = jnp.concatenate(
                [empty, edges(right, right_row, right_col, right_in)], axis=1
            )
            part = jnp.dot(
                jnp.concatenate([panel[left_row], panel[right_row]], axis=1),
                jnp.concatenate([upper, lower], axis=0),
                preferred_element_type=F32,
            )
            parts.append((left_col, right_col, part))
        for left_col, right_col, part in parts:
            total[left_col] += part[:, :TILE]
            total[right_col] += part[:, TILE:]
        return carry

    lax.fori_loop(0, (live + 2 * UNROLL - 1) // (2 * UNROLL), group, 0)


def stage_ranges(ends_ref, stage):
    return [(ends_ref[2 * k], ends_ref[2 * k + 1]) for k in STAGES[stage]]


def early_kernel(stage, places, where_ref, ends_ref, rows_ref, cols_ref, *refs):
    n = len(places)
    values_ref, *tables = refs[n : n + 5]
    *before, total, panel = refs[n + 5 :]
    take_panels(places, refs[:n], where_ref, panel)
    total[...] = before[0][...] if before else jnp.zeros_like(total)
    ranges = stage_ranges(ends_ref, stage)
    add_slots(ranges, (rows_ref, cols_ref), tables, values_ref, panel, total)


def last_kernel(places, spots, where_ref, ends_ref, rows_ref, cols_ref, *refs):
    n, m = len(places), len(spots)
    values_ref, *tables = refs[n + m : n + m + 5]
    before, keep_ref, give_ref, local_ref, panel, total = refs[n + m + 5 :]
    take_panels(places, refs[:n], where_ref, panel)
    total[...] = before[...]
    ranges = stage_ranges(ends_ref, 2)
    add_slots(ranges, (rows_ref, cols_ref), tables, values_ref, panel, total)
    y, xl, reach = (where_ref[k] for k in range(6, 9))
    local = jnp.zeros((panel.shape[1], panel.shape[1]), F32)
    for (dy, flip), feat_ref in zip(spots, refs[n : n + m]):
        at = lax.rem(y + dy + reach, reach)
        owner = at * 2 + (xl ^ flip)
        sums = jnp.concatenate([total[owner * 2], total[owner * 2 + 1]], axis=1)
        high = sums.astype(BF16)
        low = (sums - high.astype(F32)).astype(BF16)
        if flip:
            give_ref[at] = high
        else:
            keep_ref[at] = sums
        for part in (high, low):
            local = local + lax.dot_general(
                feat_ref[flip],
                part,
                (((1,), (1,)), ((), ())),
                preferred_element_type=F32,
            )
    local_ref[...] = local.reshape(local_ref.shape)


def half_kernel(where_ref, keep_ref, got_ref, kept_ref, give_ref):
    y = where_ref[6]
    for k in range(4):
        summed = keep_ref[y ^ k] + got_ref[y ^ k].astype(F32)
        if k < 2:
            kept_ref[k] = summed
        else:
            give_ref[k - 2] = summed.astype(BF16)


def quarter_kernel(keep_ref, got_ref, kept_ref, give_ref):
    kept_ref[...] = keep_ref[0] + got_ref[0].astype(F32)
    give_ref[...] = (keep_ref[1] + got_ref[1].astype(F32)).astype(BF16)


def finish_kernel(weight_ref, keep_ref, got_ref, out_ref):
    summed = keep_ref[...] + got_ref[...].astype(F32)
    out_ref[...] = lax.dot_general(
        summed.T.astype(BF16),
        weight_ref[...],
        (((1,), (1,)), ((), ())),
        preferred_element_type=F32,
    ).astype(BF16)


def spread_kernel(in_ref, out_ref):
    total = in_ref[0].astype(F32)
    for k in range(1, in_ref.shape[0]):
        total = total + in_ref[k].astype(F32)
    total = total.astype(out_ref.dtype)
    for k in range(out_ref.shape[0]):
        out_ref[k] = total


def shift(block, axis, step):
    size = lax.axis_size(axis)
    return lax.ppermute(block, axis, [(i, (i + step) % size) for i in range(size)])


def onward(block):
    ring = lax.axis_size("z")
    pairs = []
    for z in range(ring):
        pairs.append((z * 2, (z + 1) % ring * 2))
        pairs.append((z * 2 + 1, (z - 1) % ring * 2 + 1))
    return lax.ppermute(block, ("z", "c"), pairs)


def gather(own, features, where, turn, make_tables, early):
    tie = lax.optimization_barrier

    def both(flip, step, block):
        return [(flip, step, 0, block), (flip, -step, 1, shift(block, "c", 1))]

    pair = jnp.stack([own, shift(own, "c", 1)])
    other = shift(pair, "xh", 1)
    first, features_t = tie((onward(pair), turn(features)))
    second, other, beside_t = tie(
        (onward(first), other, shift(features_t, "xl", 1))
    )
    second, where = tie((second, where))
    sides = jnp.stack([features_t, beside_t])
    below, above = shift(sides, "y", 1), shift(sides, "y", -1)
    third, other_first, *beside = tie(
        (onward(second), onward(other), *make_tables(where))
    )
    third, below, above = tie((third, below, above))
    near = [(0, 0, 0, pair)] + both(0, 1, first) + both(0, 2, second)
    near += both(0, 3, third)
    fourth = onward(third[:1])
    other_second = onward(other_first)
    other_third = shift(third, "xh", 1)
    total = early(0, near, beside)
    under = shift(below, "y", 1)
    fourth, other_second, under, total = tie((fourth, other_second, under, total))
    other_fourth = shift(fourth, "xh", 1)
    sides = {0: sides, -1: below, 1: above, -2: under}
    far = [(1, 0, 0, other)] + both(1, 1, other_first) + both(1, 2, other_second)
    total = early(1, far, beside, total)
    other_fourth, total = tie((other_fourth, total))
    late = both(0, 4, fourth) + both(1, 3, other_third) + both(1, 4, other_fourth)
    return late, total, beside, sides


def shards(
    out_grad,
    pre_act,
    features,
    weight,
    inv_degree,
    node_time,
    decay_rate,
    tile_value,
    tile_row,
    tile_col,
    tile_count,
):
    nodes, width = out_grad.shape
    slots = tile_value.shape[1]
    n_row = lax.axis_size(ROW)
    n_col = lax.axis_size(COL)
    tile_rows = nodes * n_col // TILE
    tile_cols = nodes * n_row // TILE
    xh, z, c = (lax.axis_index(name) for name in COL)
    where = jnp.stack(
        [lax.axis_index(ROW), lax.axis_index(COL), xh, z, c, lax.axis_size("z")]
        + [lax.axis_index("y"), lax.axis_index("xl"), lax.axis_size("y")]
    ).astype(jnp.int32)

    masked = pl.pallas_call(
        mask_kernel,
        out_shape=jax.ShapeDtypeStruct((width, nodes), BF16),
        in_specs=[VMEM] * 2,
        out_specs=VMEM,
        compiler_params=TIGHT,
    )(out_grad, pre_act)

    def make_tables(where):
        lane = (tile_cols, 1, TILE)
        return pl.pallas_call(
            table_kernel,
            out_shape=(
                jax.ShapeDtypeStruct((tile_rows, TILE, TILE), F32),
                jax.ShapeDtypeStruct((tile_rows, TILE, TILE), F32),
                jax.ShapeDtypeStruct(lane, F32),
                jax.ShapeDtypeStruct(lane, F32),
                jax.ShapeDtypeStruct((14,), jnp.int32),
            ),
            in_specs=[SMEM] * 3 + [VMEM] + [HBM] * 2,
            out_specs=(VMEM,) * 4 + (SMEM,),
            scratch_shapes=[
                pltpu.VMEM((tile_rows, TILE), jnp.int32),
                pltpu.VMEM((tile_cols, TILE), jnp.int32),
                pltpu.VMEM((tile_rows, TILE), F32),
                pltpu.SemaphoreType.DMA((3,)),
            ],
            compiler_params=ROOM,
            cost_estimate=pl.CostEstimate(
                flops=3 * 10**9, bytes_accessed=0, transcendentals=0
            ),
        )(
            where,
            tile_count,
            decay_rate,
            tile_row,
            node_time.reshape(-1, TILE),
            inv_degree.reshape(-1, TILE),
        )

    def turn(array):
        return pl.pallas_call(
            turn_kernel,
            out_shape=jax.ShapeDtypeStruct(array.shape[::-1], BF16),
            in_specs=[VMEM],
            out_specs=VMEM,
            compiler_params=TIGHT,
        )(array)

    def split(found):
        return [place[:3] for place in found], [place[3] for place in found]

    panel = pltpu.VMEM((tile_rows, width, TILE), BF16)
    totals = (tile_cols, width, TILE)

    def early(stage, found, beside, *before):
        places, blocks = split(found)
        *tables, ends = beside
        return pl.pallas_call(
            functools.partial(early_kernel, stage, places),
            out_shape=jax.ShapeDtypeStruct(totals, F32),
            in_specs=[SMEM] * 4 + [VMEM] * (len(blocks) + 5 + len(before)),
            out_specs=VMEM,
            scratch_shapes=[panel],
            compiler_params=ROOM,
            cost_estimate=pl.CostEstimate(
                flops=4 * 10**9, bytes_accessed=0, transcendentals=0
            ),
        )(where, ends, tile_row, tile_col, *blocks, tile_value, *tables, *before)

    late, total, (*tables, ends), sides = gather(
        masked, features, where, turn, make_tables, early
    )
    places, blocks = split(late)
    spots = [(dy, flip) for dy in sides for flip in (0, 1)]
    around = [sides[dy] for dy in sides for flip in (0, 1)]
    n_near = lax.axis_size(NEAR)
    n_far = lax.axis_size(FAR)
    part_rows = features.shape[1] // n_near
    reach = lax.axis_size("y")
    keep, give, local = pl.pallas_call(
        functools.partial(last_kernel, places, spots),
        out_shape=(
            jax.ShapeDtypeStruct((reach, width, nodes), F32),
            jax.ShapeDtypeStruct((reach, width, nodes), BF16),
            jax.ShapeDtypeStruct((n_near, part_rows, width), F32),
        ),
        in_specs=[SMEM] * 4 + [VMEM] * (len(blocks) + len(around) + 6),
        out_specs=(VMEM, VMEM, VMEM),
        scratch_shapes=[panel, pltpu.VMEM(totals, F32)],
        compiler_params=ROOM,
        cost_estimate=pl.CostEstimate(
            flops=4 * 10**9, bytes_accessed=0, transcendentals=0
        ),
    )(
        where,
        ends,
        tile_row,
        tile_col,
        *blocks,
        *around,
        tile_value,
        *tables,
        total,
    )

    def spread(array, copies, dtype):
        return pl.pallas_call(
            spread_kernel,
            out_shape=jax.ShapeDtypeStruct((copies,) + array.shape[1:], dtype),
            in_specs=[VMEM],
            out_specs=VMEM,
            compiler_params=TIGHT,
        )(array)

    got = shift(give, "xl", 1)
    slices = lax.all_to_all(local, NEAR, 0, 0, tiled=True)
    slices, got = lax.optimization_barrier((slices, got))
    block = (2, width, nodes)
    keep, give = pl.pallas_call(
        half_kernel,
        out_shape=(
            jax.ShapeDtypeStruct(block, F32),
            jax.ShapeDtypeStruct(block, BF16),
        ),
        in_specs=[SMEM, VMEM, VMEM],
        out_specs=(VMEM, VMEM),
        compiler_params=TIGHT,
    )(where, keep, got)
    got = shift(give, "y", 2)
    slices = lax.all_to_all(spread(slices, n_far, BF16), FAR, 0, 0, tiled=True)
    slices, got = lax.optimization_barrier((slices, got))
    keep, give = pl.pallas_call(
        quarter_kernel,
        out_shape=(
            jax.ShapeDtypeStruct((width, nodes), F32),
            jax.ShapeDtypeStruct((width, nodes), BF16),
        ),
        in_specs=[VMEM, VMEM],
        out_specs=(VMEM, VMEM),
        compiler_params=TIGHT,
    )(keep, got)
    slices, give = lax.optimization_barrier((spread(slices, n_near, F32), give))
    got = lax.ppermute(give, "y", [(y, y ^ 1) for y in range(reach)])
    grad_input = pl.pallas_call(
        finish_kernel,
        out_shape=jax.ShapeDtypeStruct((nodes, features.shape[1]), BF16),
        in_specs=[VMEM] * 3,
        out_specs=VMEM,
        compiler_params=TIGHT,
    )(weight, keep, got)
    slices = lax.all_to_all(slices, NEAR, 0, 0, tiled=True)
    return grad_input, slices.reshape(features.shape[1], width)


def solution(mesh):
    fine = Mesh(mesh.devices.reshape(4, 2, 2, 8, 2), ROW + COL)
    placed = (
        P(ROW + COL, None),
        P(ROW + COL, None),
        P(COL + ROW, None),
        P(),
        P(),
        P(),
        P(),
        P(ROW, COL, None, None),
        P(ROW, COL),
        P(ROW, COL),
        P(ROW, COL),
    )
    return jax.shard_map(
        shards,
        mesh=fine,
        in_specs=placed,
        out_specs=(P(COL + ROW, None), P()),
        check_vma=False,
    )
```

time: 918 us -> 112 us (0.12)
  waiting for transfers between devices: 837 us -> 18.3 us
  local copies, waits for them, and re-layouts: 50.4 us -> 6.1 us
  starting transfers between devices: 0.12 us -> 43.4 us
  blocking collectives: 0 us -> 31.2 us
  between operations: 15.1 us -> 2.07 us
  Pallas kernels: 0 us -> 11 us
    reduce_scatter x1 -> x0, waiting for transfers between devices: 504 us -> none  [shards(): lax.psum_scatter(partial_value.reshape(cols_per_block, width_out), 'row',...]
    psum x1 -> x0, waiting for transfers between devices: 251 us -> none  [shards(): weight_grad = lax.psum(local_grad, ('row', 'col'))]
    all_gather x1 -> x0, waiting for transfers between devices: 83.2 us -> none  [shards(): gathered = lax.all_gather(masked_grad, 'col', axis=0, tiled=True)]
    gather x4 -> x0, local copies, waits for them, and re-layouts: 38.1 us -> none  [the longest x1 11.8 us: edge_tiles(): source_scale = jnp.take(row_scale, source_index, axis=0, mode='clip')]
    ppermute x0 -> x25, starting transfers between devices: none -> 37.1 us  [the longest x18 21.6 us: shift(): lax.ppermute(block, axis, [(i, (i + step) % size) for i in range(size)])]
    all_to_all x0 -> x2, blocking collectives: none -> 31.2 us  [the longest x1 16.1 us: shards(): slices = lax.all_to_all(local, NEAR, 0, 0, tiled=True)]
    ppermute x0 -> x25, waiting for transfers between devices: none -> 18.3 us  [the longest x18 11.2 us: shift(): lax.ppermute(block, axis, [(i, (i + step) % size) for i in range(size)])]
    pallas_call x0 -> x11, Pallas kernels: none -> 11 us  [the longest x1 3.26 us: make_tables(): pl.pallas_call(table_kernel, out_shape=(jax.ShapeDtypeStruct((tile_rows,...]
  transfers between devices with their start and end apart: 3 -> 26, of which waited for: 3 -> 7; matrix products, arithmetic and copies ran while one was open for 1% -> 0% of each run, Pallas kernels for 0% -> 7%
where the time goes in v2:
time: 112 us
  starting transfers between devices  43.4 us (39%)
  blocking collectives  31.2 us (28%)
  waiting for transfers between devices  18.3 us (16%)
  Pallas kernels  11 us (10%)
  local copies, waits for them, and re-layouts  6.1 us (5%)
  between operations  2.07 us (2%)
    ppermute x18, starting transfers between devices, shift(): lax.ppermute(block, axis, [(i, (i + step) % size) for i in range(size)])  21.6 us
    all_to_all x1, blocking collectives, shards(): slices = lax.all_to_all(local, NEAR, 0, 0, tiled=True)  16.1 us
    all_to_all x1, blocking collectives, shards(): slices = lax.all_to_all(spread(slices, n_far, BF16), FAR, 0, 0, tiled=True)  15.1 us
    ppermute x6, starting transfers between devices, onward(): return lax.ppermute(block, ('z', 'c'), pairs)  14.1 us
    ppermute x18, waiting for transfers between devices, shift(): lax.ppermute(block, axis, [(i, (i + step) % size) for i in range(size)])  11.2 us
    ppermute x1, waiting for transfers between devices, shards(): got = lax.ppermute(give, 'y', [(y, y ^ 1) for y in range(reach)])  6.59 us
    all_to_all x1, starting transfers between devices, shards(): slices = lax.all_to_all(slices, NEAR, 0, 0, tiled=True)  6.28 us
    unnamed x21, local copies, waits for them, and re-layouts  6 us
  transfers between devices with their start and end apart: 26, of which 7 were waited for; matrix products, arithmetic and copies ran while one was open for 0% of the time, Pallas kernels for 7%

profile of v2, /device:TPU:1, one launch (start us, length us, event | category | flops | bytes accessed | tf_op | source)
XLA Modules:
  0.0 112.1 jit_solution(14119302052738371123)
XLA Ops:
  2.6 3.3 %collective-permute-start = (bf16[256,256]{1,0:T(8,128)(2,1)S(1)}, bf16[256,256]{1,0:T(8,128)(2,1)S(1)}, u32[]{:S(2)}, u32[]{:S(2)}) collective-permute-start(bf16[256,256]{1,0:T(8,128)(2,1)S(1)} %shard_map.122), channel_id=1, source_target_pairs={{0,1},{1,0},{2,3},{3,2},{4,5},{5,4},{6,7},{7,6},{8,9},{9,8},{10,11... | collective-permute-start | bytes 393224 | tf_op jit(solution)/shard_map/ppermute | solution.py:250
  6.9 3.9 %collective-permute-start.1 = (bf16[2,256,256]{2,1,0:T(8,128)(2,1)S(1)}, bf16[2,256,256]{2,1,0:T(8,128)(2,1)S(1)}, u32[]{:S(2)}, u32[]{:S(2)}) collective-permute-start(bf16[2,256,256]{2,1,0:T(8,128)(2,1)S(1)} %pad_maximum_fusion.refs_0_), channel_id=1, source_target_pairs={{0,2},{1,15},{2,4},{3,1},{4,6},{5,3},{6,8},{7,5},{8,10},{9,7},{10,... | collective-permute-start | bytes 786440 | tf_op jit(solution)/shard_map/ppermute | solution.py:259
  11.8 2.8 %collective-permute-start.3 = (bf16[2,256,256]{2,1,0:T(8,128)(2,1)S(1)}, bf16[2,256,256]{2,1,0:T(8,128)(2,1)S(1)}, u32[]{:S(2)}, u32[]{:S(2)}) collective-permute-start(bf16[2,256,256]{2,1,0:T(8,128)(2,1)S(1)} %pad_maximum_fusion.refs_0_), channel_id=1, source_target_pairs={{0,16},{16,0},{1,17},{17,1},{2,18},{18,2},{3,19},{19,3},{4,20},{20... | collective-permute-start | bytes 786440 | tf_op jit(solution)/shard_map/ppermute | solution.py:250
  14.7 2.9 %collective-permute-start.2 = (bf16[2,256,256]{2,1,0:T(8,128)(2,1)S(1)}, bf16[2,256,256]{2,1,0:T(8,128)(2,1)S(1)}, u32[]{:S(2)}, u32[]{:S(2)}) collective-permute-start(bf16[2,256,256]{2,1,0:T(8,128)(2,1)S(1)} %collective-permute-done.1.refs_1_), channel_id=1, source_target_pairs={{0,2},{1,15},{2,4},{3,1},{4,6},{5,3},{6,8},{7,5},{8,10},{9,7},{10,... | collective-permute-start | bytes 786440 | tf_op jit(solution)/shard_map/ppermute | solution.py:259
  20.0 1.8 %collective-permute-done.4 = bf16[256,256]{1,0:T(8,128)(2,1)S(1)} collective-permute-done((bf16[256,256]{1,0:T(8,128)(2,1)S(1)}, bf16[256,256]{1,0:T(8,128)(2,1)S(1)}, u32[]{:S(2)}, u32[]{:S(2)}) %collective-permute-start.4) | collective-permute-done | bytes 131104 | tf_op jit(solution)/shard_map/ppermute | solution.py:250
  21.9 1.4 %collective-permute-start.7 = (bf16[2,256,256]{2,1,0:T(8,128)(2,1)S(1)}, bf16[2,256,256]{2,1,0:T(8,128)(2,1)S(1)}, u32[]{:S(2)}, u32[]{:S(2)}) collective-permute-start(bf16[2,256,256]{2,1,0:T(8,128)(2,1)S(1)} %pad_maximum_fusion.1.refs_6_.refs_7_), channel_id=1, source_target_pairs={{0,64},{64,128},{128,192},{192,0},{1,65},{65,129},{129,193},{193,1... | collective-permute-start | bytes 786440 | tf_op jit(solution)/shard_map/ppermute | solution.py:250
  23.2 1.5 %collective-permute-start.8 = (bf16[2,256,256]{2,1,0:T(8,128)(2,1)S(1)}, bf16[2,256,256]{2,1,0:T(8,128)(2,1)S(1)}, u32[]{:S(2)}, u32[]{:S(2)}) collective-permute-start(bf16[2,256,256]{2,1,0:T(8,128)(2,1)S(1)} %pad_maximum_fusion.1.refs_6_.refs_7_), channel_id=1, source_target_pairs={{0,192},{64,0},{128,64},{192,128},{1,193},{65,1},{129,65},{193,129... | collective-permute-start | bytes 786440 | tf_op jit(solution)/shard_map/ppermute | solution.py:250
  24.8 3.4 %collective-permute-start.5 = (bf16[2,256,256]{2,1,0:T(8,128)(2,1)S(1)}, bf16[2,256,256]{2,1,0:T(8,128)(2,1)S(1)}, u32[]{:S(2)}, u32[]{:S(2)}) collective-permute-start(bf16[2,256,256]{2,1,0:T(8,128)(2,1)S(1)} %collective-permute-done.2.refs_3_), channel_id=1, source_target_pairs={{0,2},{1,15},{2,4},{3,1},{4,6},{5,3},{6,8},{7,5},{8,10},{9,7},{10,... | collective-permute-start | bytes 786440 | tf_op jit(solution)/shard_map/ppermute | solution.py:259
  30.8 3.3 %shard_map.124 = (f32[64,128,128]{2,1,0:T(8,128)S(1)}, f32[64,128,128]{2,1,0:T(8,128)S(1)}, f32[16,1,128]{2,1,0:T(1,128)S(1)}, f32[16,1,128]{2,1,0:T(1,128)S(1)}, s32[14]{0:T(128)S(1)}) custom-call(s32[9]{0:T(128)S(1)} %stack.49.where_ref, s32[1,1]{1,0:T(1,128)S(6)} %copy.15.count_ref, f32[1]{0:T(128)S(6)} %copy.14.decay_ref, s32[1,176]{1,0:T(1,128)S(1)} %copy-done.4, ...), custom_call_target="tpu_custom_call" | custom-call | flops 3000000000 | tf_op jit(solution)/shard_map/pallas_call | solution.py:333
  34.3 2.8 %collective-permute-start.14 = (bf16[2,256,256]{2,1,0:T(8,128)(2,1)S(1)}, bf16[2,256,256]{2,1,0:T(8,128)(2,1)S(1)}, u32[]{:S(2)}, u32[]{:S(2)}) collective-permute-start(bf16[2,256,256]{2,1,0:T(8,128)(2,1)S(1)} %collective-permute-done.5.refs_5_), channel_id=1, source_target_pairs={{0,1},{1,0},{2,3},{3,2},{4,5},{5,4},{6,7},{7,6},{8,9},{9,8},{10,11... | collective-permute-start | bytes 786440 | tf_op jit(solution)/shard_map/ppermute | solution.py:250
  38.4 2.0 %collective-permute-start.16 = (bf16[2,256,256]{2,1,0:T(8,128)(2,1)S(1)}, bf16[2,256,256]{2,1,0:T(8,128)(2,1)S(1)}, u32[]{:S(2)}, u32[]{:S(2)}) collective-permute-start(bf16[2,256,256]{2,1,0:T(8,128)(2,1)S(1)} %collective-permute-done.5.refs_5_), channel_id=1, source_target_pairs={{0,16},{16,0},{1,17},{17,1},{2,18},{18,2},{3,19},{19,3},{4,20},{20... | collective-permute-start | bytes 786440 | tf_op jit(solution)/shard_map/ppermute | solution.py:250
  40.5 2.6 %collective-permute-start.9 = (bf16[1,256,256]{2,1,0:T(8,128)(2,1)S(1)}, bf16[1,256,256]{2,1,0:T(8,128)(2,1)S(1)}, u32[]{:S(2)}, u32[]{:S(2)}) collective-permute-start(bf16[1,256,256]{2,1,0:T(8,128)(2,1)S(1)} %slice.3), channel_id=1, source_target_pairs={{0,2},{1,15},{2,4},{3,1},{4,6},{5,3},{6,8},{7,5},{8,10},{9,7},{10,... | collective-permute-start | bytes 393224 | tf_op jit(solution)/shard_map/ppermute | solution.py:259
  43.1 1.4 %shard_map.125.refs_10_ = f32[16,256,128]{2,1,0:T(8,128)S(1)} custom-call(s32[9]{0:T(128)S(1)} %stack.49.where_ref, s32[14]{0:T(128)S(1)} %get-tuple-element.54.ends_ref, s32[1,176]{1,0:T(1,128)S(1)} %copy-done.4, s32[1,176]{1,0:T(1,128)S(1)} %copy-done.5, bf16[2,256,256]{2,1,0:T(8,128)(2,1)S(1)} %pad_maximum_fusion.refs_0_, ...), custom_call_target="tpu_custom_call" | custom-call | flops 4000000000 | tf_op jit(solution)/shard_map/pallas_call | solution.py:381
  45.0 3.9 %collective-permute-done.11.refs_12_.refs_13_ = bf16[2,256,256]{2,1,0:T(8,128)(2,1)S(1)} collective-permute-done((bf16[2,256,256]{2,1,0:T(8,128)(2,1)S(1)}, bf16[2,256,256]{2,1,0:T(8,128)(2,1)S(1)}, u32[]{:S(2)}, u32[]{:S(2)}) %collective-permute-start.11) | collective-permute-done | bytes 262176 | tf_op jit(solution)/shard_map/ppermute | solution.py:250
  48.9 1.4 %collective-permute-start.20 = (bf16[2,256,256]{2,1,0:T(8,128)(2,1)S(1)}, bf16[2,256,256]{2,1,0:T(8,128)(2,1)S(1)}, u32[]{:S(2)}, u32[]{:S(2)}) collective-permute-start(bf16[2,256,256]{2,1,0:T(8,128)(2,1)S(1)} %collective-permute-done.10.refs_3_), channel_id=1, source_target_pairs={{0,1},{1,0},{2,3},{3,2},{4,5},{5,4},{6,7},{7,6},{8,9},{9,8},{10,11... | collective-permute-start | bytes 786440 | tf_op jit(solution)/shard_map/ppermute | solution.py:250
  51.8 1.7 %shard_map.126.refs_19_ = f32[16,256,128]{2,1,0:T(8,128)S(1)} custom-call(s32[9]{0:T(128)S(1)} %stack.49.where_ref, s32[14]{0:T(128)S(1)} %get-tuple-element.54.ends_ref, s32[1,176]{1,0:T(1,128)S(1)} %copy-done.4, s32[1,176]{1,0:T(1,128)S(1)} %copy-done.5, bf16[2,256,256]{2,1,0:T(8,128)(2,1)S(1)} %collective-permute-done.3.refs_0_, ...), custom_call_target="tpu_custom_call" | custom-call | flops 4000000000 | tf_op jit(solution)/shard_map/pallas_call | solution.py:381
  53.5 3.5 %collective-permute-done.18.refs_4_ = bf16[1,256,256]{2,1,0:T(8,128)(2,1)S(1)} collective-permute-done((bf16[1,256,256]{2,1,0:T(8,128)(2,1)S(1)}, bf16[1,256,256]{2,1,0:T(8,128)(2,1)S(1)}, u32[]{:S(2)}, u32[]{:S(2)}) %collective-permute-start.18) | collective-permute-done | bytes 131104 | tf_op jit(solution)/shard_map/ppermute | solution.py:250
  58.7 2.1 %shard_map.127 = (f32[4,256,256]{2,1,0:T(8,128)S(1)}, bf16[4,256,256]{2,1,0:T(8,128)(2,1)S(1)}, f32[16,16,256]{2,1,0:T(8,128)S(1)}) custom-call(s32[9]{0:T(128)S(1)} %stack.49.where_ref, s32[14]{0:T(128)S(1)} %get-tuple-element.54.ends_ref, s32[1,176]{1,0:T(1,128)S(1)} %copy-done.4, s32[1,176]{1,0:T(1,128)S(1)} %copy-done.5, ...), custom_call_target="tpu_custom_call" | custom-call | flops 4000000000 | tf_op jit(solution)/shard_map/pallas_call | solution.py:403
  62.0 16.1 %all_to_all.15.in_ref = f32[16,16,256]{2,1,0:T(8,128)S(1)} all-to-all(f32[16,16,256]{2,1,0:T(8,128)S(1)} %get-tuple-element.72), channel_id=1, replica_groups=mesh['y'=4,'xl'=2,'xh'=2,'z'=8,'c'=2] {'y','xl','c'}, dimensions={0} | all-to-all | bytes 524288 | tf_op jit(solution)/shard_map/all_to_all | solution.py:439
  78.8 1.6 %collective-permute-start.23 = (bf16[2,256,256]{2,1,0:T(8,128)(2,1)S(1)}, bf16[2,256,256]{2,1,0:T(8,128)(2,1)S(1)}, u32[]{:S(2)}, u32[]{:S(2)}) collective-permute-start(bf16[2,256,256]{2,1,0:T(8,128)(2,1)S(1)} %get-tuple-element.77), channel_id=1, source_target_pairs={{0,128},{64,192},{128,0},{192,64},{1,129},{65,193},{129,1},{193,65... | collective-permute-start | bytes 786440 | tf_op jit(solution)/shard_map/ppermute | solution.py:250
  80.3 15.1 %all_to_all.16.in_ref = bf16[16,16,256]{2,1,0:T(8,128)(2,1)S(1)} all-to-all(bf16[16,16,256]{2,1,0:T(8,128)(2,1)S(1)} %shard_map.129), channel_id=1, replica_groups=mesh['y'=4,'xl'=2,'xh'=2,'z'=8,'c'=2] {'xh','z'}, dimensions={0} | all-to-all | bytes 262144 | tf_op jit(solution)/shard_map/all_to_all | solution.py:453
  96.3 6.3 %all-to-all-start.2 = ((f32[16,16,256]{2,1,0:T(8,128)}), f32[16,16,256]{2,1,0:T(8,128)S(1)}, u32[]{:S(2)}, u32[]{:S(2)}) async-start(f32[16,16,256]{2,1,0:T(8,128)} %shard_map.131), calls=%async_computation.2 | async-start | bytes 524288 | tf_op jit(solution)/shard_map/all_to_all | solution.py:474
  102.5 1.4 %collective-permute-start.24 = (bf16[256,256]{1,0:T(8,128)(2,1)S(1)}, bf16[256,256]{1,0:T(8,128)(2,1)S(1)}, u32[]{:S(2)}, u32[]{:S(2)}) collective-permute-start(bf16[256,256]{1,0:T(8,128)(2,1)S(1)} %get-tuple-element.82), channel_id=1, source_target_pairs={{0,64},{64,0},{128,192},{192,128},{1,65},{65,1},{129,193},{193,129... | collective-permute-start | bytes 393224 | tf_op jit(solution)/shard_map/ppermute | solution.py:466
  103.9 6.6 %collective-permute-done.24.got_ref = bf16[256,256]{1,0:T(8,128)(2,1)S(1)} collective-permute-done((bf16[256,256]{1,0:T(8,128)(2,1)S(1)}, bf16[256,256]{1,0:T(8,128)(2,1)S(1)}, u32[]{:S(2)}, u32[]{:S(2)}) %collective-permute-start.24) | collective-permute-done | bytes 131104 | tf_op jit(solution)/shard_map/ppermute | solution.py:466
  (67 shorter events, 17.4 us)
Async XLA Ops:
  2.6 4.3 %collective-permute-start = (bf16[256,256]{1,0:T(8,128)(2,1)S(1)}, bf16[256,256]{1,0:T(8,128)(2,1)S(1)}, u32[]{:S(2)}, u32[]{:S(2)}) collective-permute-start(bf16[256,256]{1,0:T(8,128)(2,1)S(1)} %shard_map.122), channel_id=1, source_target_pairs={{0,1},{1,0},{2,3},{3,2},{4,5},{5,4},{6,7},{7,6},{8,9},{9,8},{10,11... | collective-permute-start | bytes 393224 | tf_op jit(solution)/shard_map/ppermute | solution.py:250
  6.9 7.8 %collective-permute-start.1 = (bf16[2,256,256]{2,1,0:T(8,128)(2,1)S(1)}, bf16[2,256,256]{2,1,0:T(8,128)(2,1)S(1)}, u32[]{:S(2)}, u32[]{:S(2)}) collective-permute-start(bf16[2,256,256]{2,1,0:T(8,128)(2,1)S(1)} %pad_maximum_fusion.refs_0_), channel_id=1, source_target_pairs={{0,2},{1,15},{2,4},{3,1},{4,6},{5,3},{6,8},{7,5},{8,10},{9,7},{10,... | collective-permute-start | bytes 786440 | tf_op jit(solution)/shard_map/ppermute | solution.py:259
  11.8 8.2 %collective-permute-start.3 = (bf16[2,256,256]{2,1,0:T(8,128)(2,1)S(1)}, bf16[2,256,256]{2,1,0:T(8,128)(2,1)S(1)}, u32[]{:S(2)}, u32[]{:S(2)}) collective-permute-start(bf16[2,256,256]{2,1,0:T(8,128)(2,1)S(1)} %pad_maximum_fusion.refs_0_), channel_id=1, source_target_pairs={{0,16},{16,0},{1,17},{17,1},{2,18},{18,2},{3,19},{19,3},{4,20},{20... | collective-permute-start | bytes 786440 | tf_op jit(solution)/shard_map/ppermute | solution.py:250
  14.7 7.2 %collective-permute-start.2 = (bf16[2,256,256]{2,1,0:T(8,128)(2,1)S(1)}, bf16[2,256,256]{2,1,0:T(8,128)(2,1)S(1)}, u32[]{:S(2)}, u32[]{:S(2)}) collective-permute-start(bf16[2,256,256]{2,1,0:T(8,128)(2,1)S(1)} %collective-permute-done.1.refs_1_), channel_id=1, source_target_pairs={{0,2},{1,15},{2,4},{3,1},{4,6},{5,3},{6,8},{7,5},{8,10},{9,7},{10,... | collective-permute-start | bytes 786440 | tf_op jit(solution)/shard_map/ppermute | solution.py:259
  17.5 4.3 %collective-permute-start.4 = (bf16[256,256]{1,0:T(8,128)(2,1)S(1)}, bf16[256,256]{1,0:T(8,128)(2,1)S(1)}, u32[]{:S(2)}, u32[]{:S(2)}) collective-permute-start(bf16[256,256]{1,0:T(8,128)(2,1)S(1)} %shard_map.123), channel_id=1, source_target_pairs={{0,32},{32,0},{1,33},{33,1},{2,34},{34,2},{3,35},{35,3},{4,36},{36... | collective-permute-start | bytes 393224 | tf_op jit(solution)/shard_map/ppermute | solution.py:250
  20.0 18.4 %collective-permute-start.12 = (bf16[2,256,256]{2,1,0:T(8,128)(2,1)S(1)}, bf16[2,256,256]{2,1,0:T(8,128)(2,1)S(1)}, u32[]{:S(2)}, u32[]{:S(2)}) collective-permute-start(bf16[2,256,256]{2,1,0:T(8,128)(2,1)S(1)} %collective-permute-done.1.refs_1_), channel_id=1, source_target_pairs={{0,1},{1,0},{2,3},{3,2},{4,5},{5,4},{6,7},{7,6},{8,9},{9,8},{10,11... | collective-permute-start | bytes 786440 | tf_op jit(solution)/shard_map/ppermute | solution.py:250
  21.9 12.5 %collective-permute-start.7 = (bf16[2,256,256]{2,1,0:T(8,128)(2,1)S(1)}, bf16[2,256,256]{2,1,0:T(8,128)(2,1)S(1)}, u32[]{:S(2)}, u32[]{:S(2)}) collective-permute-start(bf16[2,256,256]{2,1,0:T(8,128)(2,1)S(1)} %pad_maximum_fusion.1.refs_6_.refs_7_), channel_id=1, source_target_pairs={{0,64},{64,128},{128,192},{192,0},{1,65},{65,129},{129,193},{193,1... | collective-permute-start | bytes 786440 | tf_op jit(solution)/shard_map/ppermute | solution.py:250
  23.2 11.1 %collective-permute-start.8 = (bf16[2,256,256]{2,1,0:T(8,128)(2,1)S(1)}, bf16[2,256,256]{2,1,0:T(8,128)(2,1)S(1)}, u32[]{:S(2)}, u32[]{:S(2)}) collective-permute-start(bf16[2,256,256]{2,1,0:T(8,128)(2,1)S(1)} %pad_maximum_fusion.1.refs_6_.refs_7_), channel_id=1, source_target_pairs={{0,192},{64,0},{128,64},{192,128},{1,193},{65,1},{129,65},{193,129... | collective-permute-start | bytes 786440 | tf_op jit(solution)/shard_map/ppermute | solution.py:250
  24.8 9.3 %collective-permute-start.5 = (bf16[2,256,256]{2,1,0:T(8,128)(2,1)S(1)}, bf16[2,256,256]{2,1,0:T(8,128)(2,1)S(1)}, u32[]{:S(2)}, u32[]{:S(2)}) collective-permute-start(bf16[2,256,256]{2,1,0:T(8,128)(2,1)S(1)} %collective-permute-done.2.refs_3_), channel_id=1, source_target_pairs={{0,2},{1,15},{2,4},{3,1},{4,6},{5,3},{6,8},{7,5},{8,10},{9,7},{10,... | collective-permute-start | bytes 786440 | tf_op jit(solution)/shard_map/ppermute | solution.py:259
  28.2 6.1 %collective-permute-start.6 = (bf16[2,256,256]{2,1,0:T(8,128)(2,1)S(1)}, bf16[2,256,256]{2,1,0:T(8,128)(2,1)S(1)}, u32[]{:S(2)}, u32[]{:S(2)}) collective-permute-start(bf16[2,256,256]{2,1,0:T(8,128)(2,1)S(1)} %collective-permute-done.3.refs_0_), channel_id=1, source_target_pairs={{0,2},{1,15},{2,4},{3,1},{4,6},{5,3},{6,8},{7,5},{8,10},{9,7},{10,... | collective-permute-start | bytes 786440 | tf_op jit(solution)/shard_map/ppermute | solution.py:259
  34.1 6.3 %collective-permute-start.13 = (bf16[2,256,256]{2,1,0:T(8,128)(2,1)S(1)}, bf16[2,256,256]{2,1,0:T(8,128)(2,1)S(1)}, u32[]{:S(2)}, u32[]{:S(2)}) collective-permute-start(bf16[2,256,256]{2,1,0:T(8,128)(2,1)S(1)} %collective-permute-done.2.refs_3_), channel_id=1, source_target_pairs={{0,1},{1,0},{2,3},{3,2},{4,5},{5,4},{6,7},{7,6},{8,9},{9,8},{10,11... | collective-permute-start | bytes 786440 | tf_op jit(solution)/shard_map/ppermute | solution.py:250
  34.3 6.1 %collective-permute-start.14 = (bf16[2,256,256]{2,1,0:T(8,128)(2,1)S(1)}, bf16[2,256,256]{2,1,0:T(8,128)(2,1)S(1)}, u32[]{:S(2)}, u32[]{:S(2)}) collective-permute-start(bf16[2,256,256]{2,1,0:T(8,128)(2,1)S(1)} %collective-permute-done.5.refs_5_), channel_id=1, source_target_pairs={{0,1},{1,0},{2,3},{3,2},{4,5},{5,4},{6,7},{7,6},{8,9},{9,8},{10,11... | collective-permute-start | bytes 786440 | tf_op jit(solution)/shard_map/ppermute | solution.py:250
  37.2 11.8 %collective-permute-start.10 = (bf16[2,256,256]{2,1,0:T(8,128)(2,1)S(1)}, bf16[2,256,256]{2,1,0:T(8,128)(2,1)S(1)}, u32[]{:S(2)}, u32[]{:S(2)}) collective-permute-start(bf16[2,256,256]{2,1,0:T(8,128)(2,1)S(1)} %collective-permute-done.6.refs_1_), channel_id=1, source_target_pairs={{0,2},{1,15},{2,4},{3,1},{4,6},{5,3},{6,8},{7,5},{8,10},{9,7},{10,... | collective-permute-start | bytes 786440 | tf_op jit(solution)/shard_map/ppermute | solution.py:259
  38.4 13.4 %collective-permute-start.19 = (bf16[2,256,256]{2,1,0:T(8,128)(2,1)S(1)}, bf16[2,256,256]{2,1,0:T(8,128)(2,1)S(1)}, u32[]{:S(2)}, u32[]{:S(2)}) collective-permute-start(bf16[2,256,256]{2,1,0:T(8,128)(2,1)S(1)} %collective-permute-done.6.refs_1_), channel_id=1, source_target_pairs={{0,1},{1,0},{2,3},{3,2},{4,5},{5,4},{6,7},{7,6},{8,9},{9,8},{10,11... | collective-permute-start | bytes 786440 | tf_op jit(solution)/shard_map/ppermute | solution.py:250
  38.4 13.2 %collective-permute-start.16 = (bf16[2,256,256]{2,1,0:T(8,128)(2,1)S(1)}, bf16[2,256,256]{2,1,0:T(8,128)(2,1)S(1)}, u32[]{:S(2)}, u32[]{:S(2)}) collective-permute-start(bf16[2,256,256]{2,1,0:T(8,128)(2,1)S(1)} %collective-permute-done.5.refs_5_), channel_id=1, source_target_pairs={{0,16},{16,0},{1,17},{17,1},{2,18},{18,2},{3,19},{19,3},{4,20},{20... | collective-permute-start | bytes 786440 | tf_op jit(solution)/shard_map/ppermute | solution.py:250
  40.4 8.5 %collective-permute-start.11 = (bf16[2,256,256]{2,1,0:T(8,128)(2,1)S(1)}, bf16[2,256,256]{2,1,0:T(8,128)(2,1)S(1)}, u32[]{:S(2)}, u32[]{:S(2)}) collective-permute-start(bf16[2,256,256]{2,1,0:T(8,128)(2,1)S(1)} %collective-permute-done.7.refs_8_.refs_9_), channel_id=1, source_target_pairs={{0,64},{64,128},{128,192},{192,0},{1,65},{65,129},{129,193},{193,1... | collective-permute-start | bytes 786440 | tf_op jit(solution)/shard_map/ppermute | solution.py:250
  40.5 4.5 %collective-permute-start.9 = (bf16[1,256,256]{2,1,0:T(8,128)(2,1)S(1)}, bf16[1,256,256]{2,1,0:T(8,128)(2,1)S(1)}, u32[]{:S(2)}, u32[]{:S(2)}) collective-permute-start(bf16[1,256,256]{2,1,0:T(8,128)(2,1)S(1)} %slice.3), channel_id=1, source_target_pairs={{0,2},{1,15},{2,4},{3,1},{4,6},{5,3},{6,8},{7,5},{8,10},{9,7},{10,... | collective-permute-start | bytes 393224 | tf_op jit(solution)/shard_map/ppermute | solution.py:259
  50.3 6.6 %collective-permute-start.18 = (bf16[1,256,256]{2,1,0:T(8,128)(2,1)S(1)}, bf16[1,256,256]{2,1,0:T(8,128)(2,1)S(1)}, u32[]{:S(2)}, u32[]{:S(2)}) collective-permute-start(bf16[1,256,256]{2,1,0:T(8,128)(2,1)S(1)} %collective-permute-done.9.refs_0_), channel_id=1, source_target_pairs={{0,16},{16,0},{1,17},{17,1},{2,18},{18,2},{3,19},{19,3},{4,20},{20... | collective-permute-start | bytes 393224 | tf_op jit(solution)/shard_map/ppermute | solution.py:250
  51.3 6.4 %collective-permute-start.15 = (bf16[1,256,256]{2,1,0:T(8,128)(2,1)S(1)}, bf16[1,256,256]{2,1,0:T(8,128)(2,1)S(1)}, u32[]{:S(2)}, u32[]{:S(2)}) collective-permute-start(bf16[1,256,256]{2,1,0:T(8,128)(2,1)S(1)} %collective-permute-done.9.refs_0_), channel_id=1, source_target_pairs={{0,1},{1,0},{2,3},{3,2},{4,5},{5,4},{6,7},{7,6},{8,9},{9,8},{10,11... | collective-permute-start | bytes 393224 | tf_op jit(solution)/shard_map/ppermute | solution.py:250
  51.6 6.1 %collective-permute-start.17 = (bf16[2,256,256]{2,1,0:T(8,128)(2,1)S(1)}, bf16[2,256,256]{2,1,0:T(8,128)(2,1)S(1)}, u32[]{:S(2)}, u32[]{:S(2)}) collective-permute-start(bf16[2,256,256]{2,1,0:T(8,128)(2,1)S(1)} %collective-permute-done.16.refs_2_), channel_id=1, source_target_pairs={{0,1},{1,0},{2,3},{3,2},{4,5},{5,4},{6,7},{7,6},{8,9},{9,8},{10,11... | collective-permute-start | bytes 786440 | tf_op jit(solution)/shard_map/ppermute | solution.py:250
  60.9 17.2 %collective-permute-start.22 = (bf16[4,256,256]{2,1,0:T(8,128)(2,1)S(1)}, bf16[4,256,256]{2,1,0:T(8,128)(2,1)S(1)}, u32[]{:S(2)}, u32[]{:S(2)}) collective-permute-start(bf16[4,256,256]{2,1,0:T(8,128)(2,1)S(1)} %get-tuple-element.73), channel_id=1, source_target_pairs={{0,32},{32,0},{1,33},{33,1},{2,34},{34,2},{3,35},{35,3},{4,36},{36... | collective-permute-start | bytes 1572872 | tf_op jit(solution)/shard_map/ppermute | solution.py:250
  78.8 16.7 %collective-permute-start.23 = (bf16[2,256,256]{2,1,0:T(8,128)(2,1)S(1)}, bf16[2,256,256]{2,1,0:T(8,128)(2,1)S(1)}, u32[]{:S(2)}, u32[]{:S(2)}) collective-permute-start(bf16[2,256,256]{2,1,0:T(8,128)(2,1)S(1)} %get-tuple-element.77), channel_id=1, source_target_pairs={{0,128},{64,192},{128,0},{192,64},{1,129},{65,193},{129,1},{193,65... | collective-permute-start | bytes 786440 | tf_op jit(solution)/shard_map/ppermute | solution.py:250
  96.3 15.1 %all-to-all-start.2 = ((f32[16,16,256]{2,1,0:T(8,128)}), f32[16,16,256]{2,1,0:T(8,128)S(1)}, u32[]{:S(2)}, u32[]{:S(2)}) async-start(f32[16,16,256]{2,1,0:T(8,128)} %shard_map.131), calls=%async_computation.2 | async-start | bytes 524288 | tf_op jit(solution)/shard_map/all_to_all | solution.py:474
  102.5 8.0 %collective-permute-start.24 = (bf16[256,256]{1,0:T(8,128)(2,1)S(1)}, bf16[256,256]{1,0:T(8,128)(2,1)S(1)}, u32[]{:S(2)}, u32[]{:S(2)}) collective-permute-start(bf16[256,256]{1,0:T(8,128)(2,1)S(1)} %get-tuple-element.82), channel_id=1, source_target_pairs={{0,64},{64,0},{128,192},{192,128},{1,65},{65,1},{129,193},{193,129... | collective-permute-start | bytes 393224 | tf_op jit(solution)/shard_map/ppermute | solution.py:466
  (12 other events, 105.4 us)

commit v3 on v2

--- a/solution.py
+++ b/solution.py
@@ -12,7 +12,7 @@
 NEAR = ROW + ("c",)
 FAR = ("xh", "z")
 TILE = 128
-UNROLL = 4
+UNROLL = 8
 STAGES = ((0, 1), (2, 3), (4, 5, 6))
 VMEM = pl.BlockSpec(memory_space=pltpu.VMEM)
 SMEM = pl.BlockSpec(memory_space=pltpu.SMEM)
@@ -105,14 +105,26 @@
     far_col[...] = jnp.exp(-later).reshape(tile_cols, 1, TILE)
 
 
+def join_kernel(*refs):
+    *in_refs, out_ref = refs
+    at = 0
+    for ref in in_refs:
+        block = ref[...].reshape((-1,) + out_ref.shape[1:])
+        out_ref[at : at + block.shape[0]] = block
+        at += block.shape[0]
+
+
 def take_panels(places, blocks, where_ref, panel):
     xh, z, c, ring = (where_ref[k] for k in range(2, 6))
-    for (flip, dz, other), block in zip(places, blocks):
-        chip = (xh ^ flip) * ring + lax.rem(z + (2 * c - 1) * dz + ring, ring)
-        for k in range(block.shape[0]):
+    for (other, parts), block in zip(places, blocks):
+        for index, part in enumerate(parts):
+            if part is None:
+                continue
+            flip, dz, k = part
+            chip = (xh ^ flip) * ring + lax.rem(z + (2 * c - 1) * dz + ring, ring)
             at = chip * 4 + (c ^ other ^ k) * 2
-            panel[at] = block[k, :, :TILE]
-            panel[at + 1] = block[k, :, TILE:]
+            panel[at] = block[index, :, :TILE]
+            panel[at + 1] = block[index, :, TILE:]
 
 
 def add_slots(ranges, ints, tables, values_ref, panel, total):
@@ -250,6 +262,18 @@
     return lax.ppermute(block, axis, [(i, (i + step) % size) for i in range(size)])
 
 
+def join(*blocks):
+    shape = blocks[0].shape[-2:]
+    count = sum(block.size for block in blocks) // (shape[0] * shape[1])
+    return pl.pallas_call(
+        join_kernel,
+        out_shape=jax.ShapeDtypeStruct((count,) + shape, BF16),
+        in_specs=[VMEM] * len(blocks),
+        out_specs=VMEM,
+        compiler_params=TIGHT,
+    )(*blocks)
+
+
 def onward(block):
     ring = lax.axis_size("z")
     pairs = []
@@ -262,37 +286,46 @@
 def gather(own, features, where, turn, make_tables, early):
     tie = lax.optimization_barrier
 
-    def both(flip, step, block):
-        return [(flip, step, 0, block), (flip, -step, 1, shift(block, "c", 1))]
-
-    pair = jnp.stack([own, shift(own, "c", 1)])
+    def both(block, *parts):
+        back = [part and (part[0], -part[1], part[2]) for part in parts]
+        return [(0, list(parts), block), (1, back, shift(block, "c", 1))]
+
+    def chip(flip, dz, size=2):
+        return [(flip, dz, k) for k in range(size)]
+
+    pair = join(own, shift(own, "c", 1))
     other = shift(pair, "xh", 1)
     first, features_t = tie((onward(pair), turn(features)))
-    second, other, beside_t = tie(
-        (onward(first), other, shift(features_t, "xl", 1))
+    beside_t = shift(features_t, "xl", 1)
+    second, other = tie((onward(first), other))
+    third = onward(join(other, second))
+    second, where = tie((second, where))
+    sides = join(features_t, beside_t)
+    below, above = shift(sides, "y", 1), shift(sides, "y", -1)
+    firsts, seconds = both(first, *chip(0, 1)), both(second, *chip(0, 2))
+    third, below, above, first_back, second_back, *beside = tie(
+        (third, below, above, firsts[1][2], seconds[1][2], *make_tables(where))
     )
-    second, where = tie((second, where))
-    sides = jnp.stack([features_t, beside_t])
-    below, above = shift(sides, "y", 1), shift(sides, "y", -1)
-    third, other_first, *beside = tie(
-        (onward(second), onward(other), *make_tables(where))
-    )
-    third, below, above = tie((third, below, above))
-    near = [(0, 0, 0, pair)] + both(0, 1, first) + both(0, 2, second)
-    near += both(0, 3, third)
-    fourth = onward(third[:1])
-    other_second = onward(other_first)
-    other_third = shift(third, "xh", 1)
+    fourth = onward(third[:3])
+    under = shift(below, "y", 1)
+    skip = [None] * 2
+    thirds = both(third, *chip(1, 1), *chip(0, 3))
+    near = [(0, chip(0, 0), pair), firsts[0], seconds[0]]
+    near += [firsts[1][:2] + (first_back,), seconds[1][:2] + (second_back,)]
+    near += [(at, skip + parts[2:], block) for at, parts, block in thirds]
     total = early(0, near, beside)
-    under = shift(below, "y", 1)
-    fourth, other_second, under, total = tie((fourth, other_second, under, total))
-    other_fourth = shift(fourth, "xh", 1)
-    sides = {0: sides, -1: below, 1: above, -2: under}
-    far = [(1, 0, 0, other)] + both(1, 1, other_first) + both(1, 2, other_second)
+    fourth, under, total = tie((fourth, under, total))
+    fifth = onward(fourth[:2])
+    crossed = shift(fourth[2:], "xh", 1)
+    fourths = both(fourth, *chip(1, 2), *chip(0, 4, 1))
+    far = [(0, chip(1, 0), other)]
+    far += [(at, parts[:2] + skip, block) for at, parts, block in thirds]
+    far += [(at, parts[:2] + [None], block) for at, parts, block in fourths]
     total = early(1, far, beside, total)
-    other_fourth, total = tie((other_fourth, total))
-    late = both(0, 4, fourth) + both(1, 3, other_third) + both(1, 4, other_fourth)
-    return late, total, beside, sides
+    fifth, crossed, total = tie((fifth, crossed, total))
+    late = [(at, skip + parts[2:], block) for at, parts, block in fourths]
+    late += both(fifth, *chip(1, 3)) + both(crossed, *chip(1, 4, 1))
+    return late, total, beside, {0: sides, -1: below, 1: above, -2: under}
 
 
 def shards(
@@ -349,7 +382,7 @@
             ],
             compiler_params=ROOM,
             cost_estimate=pl.CostEstimate(
-                flops=3 * 10**9, bytes_accessed=0, transcendentals=0
+                flops=6 * 10**9, bytes_accessed=0, transcendentals=0
             ),
         )(
             where,
@@ -370,7 +403,7 @@
         )(array)
 
     def split(found):
-        return [place[:3] for place in found], [place[3] for place in found]
+        return [place[:2] for place in found], [place[2] for place in found]
 
     panel = pltpu.VMEM((tile_rows, width, TILE), BF16)
     totals = (tile_cols, width, TILE)
@@ -386,7 +419,7 @@
             scratch_shapes=[panel],
             compiler_params=ROOM,
             cost_estimate=pl.CostEstimate(
-                flops=4 * 10**9, bytes_accessed=0, transcendentals=0
+                flops=3 * 10**9, bytes_accessed=0, transcendentals=0
             ),
         )(where, ends, tile_row, tile_col, *blocks, tile_value, *tables, *before)
 
@@ -412,7 +445,7 @@
         scratch_shapes=[panel, pltpu.VMEM(totals, F32)],
         compiler_params=ROOM,
         cost_estimate=pl.CostEstimate(
-            flops=4 * 10**9, bytes_accessed=0, transcendentals=0
+            flops=3 * 10**9, bytes_accessed=0, transcendentals=0
         ),
     )(
         where,
@@ -451,7 +484,6 @@
     )(where, keep, got)
     got = shift(give, "y", 2)
     slices = lax.all_to_all(spread(slices, n_far, BF16), FAR, 0, 0, tiled=True)
-    slices, got = lax.optimization_barrier((slices, got))
     keep, give = pl.pallas_call(
         quarter_kernel,
         out_shape=(
@@ -462,8 +494,8 @@
         out_specs=(VMEM, VMEM),
         compiler_params=TIGHT,
     )(keep, got)
-    slices, give = lax.optimization_barrier((spread(slices, n_near, F32), give))
     got = lax.ppermute(give, "y", [(y, y ^ 1) for y in range(reach)])
+    slices, got = lax.optimization_barrier((slices, got))
     grad_input = pl.pallas_call(
         finish_kernel,
         out_shape=jax.ShapeDtypeStruct((nodes, features.shape[1]), BF16),
@@ -471,7 +503,7 @@
         out_specs=VMEM,
         compiler_params=TIGHT,
     )(weight, keep, got)
-    slices = lax.all_to_all(slices, NEAR, 0, 0, tiled=True)
+    slices = lax.all_to_all(spread(slices, n_near, F32), NEAR, 0, 0, tiled=True)
     return grad_input, slices.reshape(features.shape[1], width)
 
 

time: 112 us -> 110 us (0.982)
  blocking collectives: 31.2 us -> 17.1 us
  waiting for transfers between devices: 18.3 us -> 25.8 us
  Pallas kernels: 11 us -> 14.1 us
    all_to_all x1 -> x0, blocking collectives: 15.1 us -> none  [shards(): slices = lax.all_to_all(spread(slices, n_far, BF16), FAR, 0, 0, tiled=True)]
    all_to_all x1 -> x2, waiting for transfers between devices: 0.01 us -> 14.5 us  [the longest x1 8.15 us: shards(): slices = lax.all_to_all(spread(slices, n_far, BF16), FAR, 0, 0, tiled=True)]
    ppermute x1, waiting for transfers between devices: 6.59 us -> 0.01 us  [shards(): got = lax.ppermute(give, 'y', [(y, y ^ 1) for y in range(reach)])]
    all_to_all x1 -> x2, starting transfers between devices: 6.28 us -> 12.8 us  [the longest x1 6.51 us: shards(): slices = lax.all_to_all(spread(slices, n_far, BF16), FAR, 0, 0, tiled=True)]
    ppermute x18 -> x15, starting transfers between devices: 21.6 us -> 15.4 us  [shift(): lax.ppermute(block, axis, [(i, (i + step) % size) for i in range(size)])]
    pallas_call x2, Pallas kernels: 3.06 us -> 4.76 us  [early(): pl.pallas_call(functools.partial(early_kernel, stage, places), out_shape=...]
    ppermute x6 -> x5, starting transfers between devices: 14.1 us -> 15.8 us  [onward(): return lax.ppermute(block, ('z', 'c'), pairs)]
    unnamed x21 -> x23, local copies, waits for them, and re-layouts: 6 us -> 6.34 us
  transfers between devices with their start and end apart: 26 -> 23, of which waited for: 7 -> 8; matrix products, arithmetic and copies ran while one was open for 0% -> 0% of each run, Pallas kernels for 7% -> 9%
where the time goes in v3:
time: 110 us
  starting transfers between devices  44.4 us (40%)
  waiting for transfers between devices  25.8 us (23%)
  blocking collectives  17.1 us (16%)
  Pallas kernels  14.1 us (13%)
  local copies, waits for them, and re-layouts  6.48 us (6%)
  between operations  2.15 us (2%)
    all_to_all x1, blocking collectives, shards(): slices = lax.all_to_all(local, NEAR, 0, 0, tiled=True)  17.1 us
    ppermute x5, starting transfers between devices, onward(): return lax.ppermute(block, ('z', 'c'), pairs)  15.8 us
    ppermute x15, starting transfers between devices, shift(): lax.ppermute(block, axis, [(i, (i + step) % size) for i in range(size)])  15.4 us
    ppermute x15, waiting for transfers between devices, shift(): lax.ppermute(block, axis, [(i, (i + step) % size) for i in range(size)])  11.3 us
    all_to_all x1, waiting for transfers between devices, shards(): slices = lax.all_to_all(spread(slices, n_far, BF16), FAR, 0, 0, tiled=True)  8.15 us
    all_to_all x1, starting transfers between devices, shards(): slices = lax.all_to_all(spread(slices, n_far, BF16), FAR, 0, 0, tiled=True)  6.51 us
    unnamed x23, local copies, waits for them, and re-layouts  6.34 us
    all_to_all x1, waiting for transfers between devices, shards(): slices = lax.all_to_all(spread(slices, n_near, F32), NEAR, 0, 0, tiled=True)  6.33 us
  transfers between devices with their start and end apart: 23, of which 8 were waited for; matrix products, arithmetic and copies ran while one was open for 0% of the time, Pallas kernels for 9%

profile of v3, /device:TPU:1, one launch (start us, length us, event | category | flops | bytes accessed | tf_op | source)
XLA Modules:
  0.0 110.0 jit_solution(5062179321643014246)
XLA Ops:
  2.6 3.3 %collective-permute-start = (bf16[256,256]{1,0:T(8,128)(2,1)S(1)}, bf16[256,256]{1,0:T(8,128)(2,1)S(1)}, u32[]{:S(2)}, u32[]{:S(2)}) collective-permute-start(bf16[256,256]{1,0:T(8,128)(2,1)S(1)} %shard_map.122.refs_0_), channel_id=1, source_target_pairs={{0,1},{1,0},{2,3},{3,2},{4,5},{5,4},{6,7},{7,6},{8,9},{9,8},{10,11... | collective-permute-start | bytes 393224 | tf_op jit(solution)/shard_map/ppermute | solution.py:262
  6.9 3.9 %collective-permute-start.1 = (bf16[2,256,256]{2,1,0:T(8,128)(2,1)S(1)}, bf16[2,256,256]{2,1,0:T(8,128)(2,1)S(1)}, u32[]{:S(2)}, u32[]{:S(2)}) collective-permute-start(bf16[2,256,256]{2,1,0:T(8,128)(2,1)S(1)} %shard_map.123.refs_0_), channel_id=1, source_target_pairs={{0,2},{1,15},{2,4},{3,1},{4,6},{5,3},{6,8},{7,5},{8,10},{9,7},{10,... | collective-permute-start | bytes 786440 | tf_op jit(solution)/shard_map/ppermute | solution.py:283
  11.8 2.8 %collective-permute-start.3 = (bf16[2,256,256]{2,1,0:T(8,128)(2,1)S(1)}, bf16[2,256,256]{2,1,0:T(8,128)(2,1)S(1)}, u32[]{:S(2)}, u32[]{:S(2)}) collective-permute-start(bf16[2,256,256]{2,1,0:T(8,128)(2,1)S(1)} %shard_map.123.refs_0_), channel_id=1, source_target_pairs={{0,16},{16,0},{1,17},{17,1},{2,18},{18,2},{3,19},{19,3},{4,20},{20... | collective-permute-start | bytes 786440 | tf_op jit(solution)/shard_map/ppermute | solution.py:262
  14.6 2.9 %collective-permute-start.2 = (bf16[2,256,256]{2,1,0:T(8,128)(2,1)S(1)}, bf16[2,256,256]{2,1,0:T(8,128)(2,1)S(1)}, u32[]{:S(2)}, u32[]{:S(2)}) collective-permute-start(bf16[2,256,256]{2,1,0:T(8,128)(2,1)S(1)} %collective-permute-done.1.refs_1_), channel_id=1, source_target_pairs={{0,2},{1,15},{2,4},{3,1},{4,6},{5,3},{6,8},{7,5},{8,10},{9,7},{10,... | collective-permute-start | bytes 786440 | tf_op jit(solution)/shard_map/ppermute | solution.py:283
  20.0 1.8 %collective-permute-done.5.refs_1_ = bf16[256,256]{1,0:T(8,128)(2,1)S(1)} collective-permute-done((bf16[256,256]{1,0:T(8,128)(2,1)S(1)}, bf16[256,256]{1,0:T(8,128)(2,1)S(1)}, u32[]{:S(2)}, u32[]{:S(2)}) %collective-permute-start.5) | collective-permute-done | bytes 131104 | tf_op jit(solution)/shard_map/ppermute | solution.py:262
  21.8 1.4 %collective-permute-start.6 = (bf16[2,256,256]{2,1,0:T(8,128)(2,1)S(1)}, bf16[2,256,256]{2,1,0:T(8,128)(2,1)S(1)}, u32[]{:S(2)}, u32[]{:S(2)}) collective-permute-start(bf16[2,256,256]{2,1,0:T(8,128)(2,1)S(1)} %shard_map.126.refs_6_.refs_7_), channel_id=1, source_target_pairs={{0,64},{64,128},{128,192},{192,0},{1,65},{65,129},{129,193},{193,1... | collective-permute-start | bytes 786440 | tf_op jit(solution)/shard_map/ppermute | solution.py:262
  23.2 1.5 %collective-permute-start.7 = (bf16[2,256,256]{2,1,0:T(8,128)(2,1)S(1)}, bf16[2,256,256]{2,1,0:T(8,128)(2,1)S(1)}, u32[]{:S(2)}, u32[]{:S(2)}) collective-permute-start(bf16[2,256,256]{2,1,0:T(8,128)(2,1)S(1)} %shard_map.126.refs_6_.refs_7_), channel_id=1, source_target_pairs={{0,192},{64,0},{128,64},{192,128},{1,193},{65,1},{129,65},{193,129... | collective-permute-start | bytes 786440 | tf_op jit(solution)/shard_map/ppermute | solution.py:262
  24.8 4.4 %collective-permute-start.4 = (bf16[4,256,256]{2,1,0:T(8,128)(2,1)S(1)}, bf16[4,256,256]{2,1,0:T(8,128)(2,1)S(1)}, u32[]{:S(2)}, u32[]{:S(2)}) collective-permute-start(bf16[4,256,256]{2,1,0:T(8,128)(2,1)S(1)} %shard_map.125), channel_id=1, source_target_pairs={{0,2},{1,15},{2,4},{3,1},{4,6},{5,3},{6,8},{7,5},{8,10},{9,7},{10,... | collective-permute-start | bytes 1572872 | tf_op jit(solution)/shard_map/ppermute | solution.py:283
  32.1 3.3 %shard_map.127 = (f32[64,128,128]{2,1,0:T(8,128)S(1)}, f32[64,128,128]{2,1,0:T(8,128)S(1)}, f32[16,1,128]{2,1,0:T(1,128)S(1)}, f32[16,1,128]{2,1,0:T(1,128)S(1)}, s32[14]{0:T(128)S(1)}) custom-call(s32[9]{0:T(128)S(1)} %stack.31.where_ref, s32[1,1]{1,0:T(1,128)S(6)} %copy.15.count_ref, f32[1]{0:T(128)S(6)} %copy.14.decay_ref, s32[1,176]{1,0:T(1,128)S(1)} %copy-done.4, ...), custom_call_target="tpu_custom_call" | custom-call | flops 6000000000 | tf_op jit(solution)/shard_map/pallas_call | solution.py:366
  35.4 1.2 %collective-permute-start.12 = (bf16[4,256,256]{2,1,0:T(8,128)(2,1)S(1)}, bf16[4,256,256]{2,1,0:T(8,128)(2,1)S(1)}, u32[]{:S(2)}, u32[]{:S(2)}) collective-permute-start(bf16[4,256,256]{2,1,0:T(8,128)(2,1)S(1)} %collective-permute-done.4.refs_5_.refs_1_), channel_id=1, source_target_pairs={{0,1},{1,0},{2,3},{3,2},{4,5},{5,4},{6,7},{7,6},{8,9},{9,8},{10,11... | collective-permute-start | bytes 1572872 | tf_op jit(solution)/shard_map/ppermute | solution.py:262
  36.7 1.9 %collective-permute-start.10 = (bf16[3,256,256]{2,1,0:T(8,128)(2,1)S(1)}, bf16[3,256,256]{2,1,0:T(8,128)(2,1)S(1)}, u32[]{:S(2)}, u32[]{:S(2)}) collective-permute-start(bf16[3,256,256]{2,1,0:T(8,128)(2,1)S(1)} %slice.9), channel_id=1, source_target_pairs={{0,2},{1,15},{2,4},{3,1},{4,6},{5,3},{6,8},{7,5},{8,10},{9,7},{10,... | collective-permute-start | bytes 1179656 | tf_op jit(solution)/shard_map/ppermute | solution.py:283
  38.7 2.8 %shard_map.128.refs_10_ = f32[16,256,128]{2,1,0:T(8,128)S(1)} custom-call(s32[9]{0:T(128)S(1)} %stack.31.where_ref, s32[14]{0:T(128)S(1)} %get-tuple-element.51.ends_ref, s32[1,176]{1,0:T(1,128)S(1)} %copy-done.5, s32[1,176]{1,0:T(1,128)S(1)} %copy-done.6, bf16[2,256,256]{2,1,0:T(8,128)(2,1)S(1)} %shard_map.123.refs_0_, ...), custom_call_target="tpu_custom_call" | custom-call | flops 3000000000 | tf_op jit(solution)/shard_map/pallas_call | solution.py:414
  41.5 5.1 %collective-permute-done.11.refs_12_.refs_13_ = bf16[2,256,256]{2,1,0:T(8,128)(2,1)S(1)} collective-permute-done((bf16[2,256,256]{2,1,0:T(8,128)(2,1)S(1)}, bf16[2,256,256]{2,1,0:T(8,128)(2,1)S(1)}, u32[]{:S(2)}, u32[]{:S(2)}) %collective-permute-start.11) | collective-permute-done | bytes 262176 | tf_op jit(solution)/shard_map/ppermute | solution.py:262
  46.6 2.7 %collective-permute-start.14 = (bf16[2,256,256]{2,1,0:T(8,128)(2,1)S(1)}, bf16[2,256,256]{2,1,0:T(8,128)(2,1)S(1)}, u32[]{:S(2)}, u32[]{:S(2)}) collective-permute-start(bf16[2,256,256]{2,1,0:T(8,128)(2,1)S(1)} %slice.10), channel_id=1, source_target_pairs={{0,2},{1,15},{2,4},{3,1},{4,6},{5,3},{6,8},{7,5},{8,10},{9,7},{10,... | collective-permute-start | bytes 786440 | tf_op jit(solution)/shard_map/ppermute | solution.py:283
  49.3 1.7 %collective-permute-start.15 = (bf16[1,256,256]{2,1,0:T(8,128)(2,1)S(1)}, bf16[1,256,256]{2,1,0:T(8,128)(2,1)S(1)}, u32[]{:S(2)}, u32[]{:S(2)}) collective-permute-start(bf16[1,256,256]{2,1,0:T(8,128)(2,1)S(1)} %slice.11), channel_id=1, source_target_pairs={{0,16},{16,0},{1,17},{17,1},{2,18},{18,2},{3,19},{19,3},{4,20},{20... | collective-permute-start | bytes 393224 | tf_op jit(solution)/shard_map/ppermute | solution.py:262
  51.0 2.0 %shard_map.129.refs_19_ = f32[16,256,128]{2,1,0:T(8,128)S(1)} custom-call(s32[9]{0:T(128)S(1)} %stack.31.where_ref, s32[14]{0:T(128)S(1)} %get-tuple-element.51.ends_ref, s32[1,176]{1,0:T(1,128)S(1)} %copy-done.5, s32[1,176]{1,0:T(1,128)S(1)} %copy-done.6, bf16[2,256,256]{2,1,0:T(8,128)(2,1)S(1)} %collective-permute-done.3.refs_0_, ...), custom_call_target="tpu_custom_call" | custom-call | flops 3000000000 | tf_op jit(solution)/shard_map/pallas_call | solution.py:414
  53.0 1.9 %collective-permute-done.15.refs_4_ = bf16[1,256,256]{2,1,0:T(8,128)(2,1)S(1)} collective-permute-done((bf16[1,256,256]{2,1,0:T(8,128)(2,1)S(1)}, bf16[1,256,256]{2,1,0:T(8,128)(2,1)S(1)}, u32[]{:S(2)}, u32[]{:S(2)}) %collective-permute-start.15) | collective-permute-done | bytes 131104 | tf_op jit(solution)/shard_map/ppermute | solution.py:262
  56.6 2.8 %shard_map.130 = (f32[4,256,256]{2,1,0:T(8,128)S(1)}, bf16[4,256,256]{2,1,0:T(8,128)(2,1)S(1)}, f32[16,16,256]{2,1,0:T(8,128)S(1)}) custom-call(s32[9]{0:T(128)S(1)} %stack.31.where_ref, s32[14]{0:T(128)S(1)} %get-tuple-element.51.ends_ref, s32[1,176]{1,0:T(1,128)S(1)} %copy-done.5, s32[1,176]{1,0:T(1,128)S(1)} %copy-done.6, ...), custom_call_target="tpu_custom_call" | custom-call | flops 3000000000 | tf_op jit(solution)/shard_map/pallas_call | solution.py:436
  59.7 17.1 %all_to_all.15.in_ref = f32[16,16,256]{2,1,0:T(8,128)S(1)} all-to-all(f32[16,16,256]{2,1,0:T(8,128)S(1)} %get-tuple-element.68), channel_id=1, replica_groups=mesh['y'=4,'xl'=2,'xh'=2,'z'=8,'c'=2] {'y','xl','c'}, dimensions={0} | all-to-all | bytes 524288 | tf_op jit(solution)/shard_map/all_to_all | solution.py:472
  77.4 1.5 %collective-permute-start.19 = (bf16[2,256,256]{2,1,0:T(8,128)(2,1)S(1)}, bf16[2,256,256]{2,1,0:T(8,128)(2,1)S(1)}, u32[]{:S(2)}, u32[]{:S(2)}) collective-permute-start(bf16[2,256,256]{2,1,0:T(8,128)(2,1)S(1)} %get-tuple-element.72), channel_id=1, source_target_pairs={{0,128},{64,192},{128,0},{192,64},{1,129},{65,193},{129,1},{193,65... | collective-permute-start | bytes 786440 | tf_op jit(solution)/shard_map/ppermute | solution.py:262
  79.6 6.5 %all-to-all-start.1 = ((bf16[16,16,256]{2,1,0:T(8,128)(2,1)}), bf16[16,16,256]{2,1,0:T(8,128)(2,1)S(1)}, u32[]{:S(2)}, u32[]{:S(2)}) async-start(bf16[16,16,256]{2,1,0:T(8,128)(2,1)} %shard_map.133), calls=%async_computation.1 | async-start | bytes 262144 | tf_op jit(solution)/shard_map/all_to_all | solution.py:486
  86.9 8.1 %all-to-all-done.1.in_ref = bf16[16,16,256]{2,1,0:T(8,128)(2,1)S(1)} async-done(((bf16[16,16,256]{2,1,0:T(8,128)(2,1)}), bf16[16,16,256]{2,1,0:T(8,128)(2,1)S(1)}, u32[]{:S(2)}, u32[]{:S(2)}) %all-to-all-start.1) | async-done | bytes 131104 | tf_op jit(solution)/shard_map/all_to_all | solution.py:486
  95.8 6.3 %all-to-all-start.2 = ((f32[16,16,256]{2,1,0:T(8,128)}), f32[16,16,256]{2,1,0:T(8,128)S(1)}, u32[]{:S(2)}, u32[]{:S(2)}) async-start(f32[16,16,256]{2,1,0:T(8,128)} %shard_map.135), calls=%async_computation.2 | async-start | bytes 524288 | tf_op jit(solution)/shard_map/all_to_all | solution.py:506
  103.0 6.3 %all-to-all-done.2 = f32[16,16,256]{2,1,0:T(8,128)S(1)} async-done(((f32[16,16,256]{2,1,0:T(8,128)}), f32[16,16,256]{2,1,0:T(8,128)S(1)}, u32[]{:S(2)}, u32[]{:S(2)}) %all-to-all-start.2) | async-done | bytes 262176 | tf_op jit(solution)/shard_map/all_to_all | solution.py:506
  (65 shorter events, 14.7 us)
Async XLA Ops:
  2.6 4.3 %collective-permute-start = (bf16[256,256]{1,0:T(8,128)(2,1)S(1)}, bf16[256,256]{1,0:T(8,128)(2,1)S(1)}, u32[]{:S(2)}, u32[]{:S(2)}) collective-permute-start(bf16[256,256]{1,0:T(8,128)(2,1)S(1)} %shard_map.122.refs_0_), channel_id=1, source_target_pairs={{0,1},{1,0},{2,3},{3,2},{4,5},{5,4},{6,7},{7,6},{8,9},{9,8},{10,11... | collective-permute-start | bytes 393224 | tf_op jit(solution)/shard_map/ppermute | solution.py:262
  6.9 7.8 %collective-permute-start.1 = (bf16[2,256,256]{2,1,0:T(8,128)(2,1)S(1)}, bf16[2,256,256]{2,1,0:T(8,128)(2,1)S(1)}, u32[]{:S(2)}, u32[]{:S(2)}) collective-permute-start(bf16[2,256,256]{2,1,0:T(8,128)(2,1)S(1)} %shard_map.123.refs_0_), channel_id=1, source_target_pairs={{0,2},{1,15},{2,4},{3,1},{4,6},{5,3},{6,8},{7,5},{8,10},{9,7},{10,... | collective-permute-start | bytes 786440 | tf_op jit(solution)/shard_map/ppermute | solution.py:283
  11.8 12.9 %collective-permute-start.3 = (bf16[2,256,256]{2,1,0:T(8,128)(2,1)S(1)}, bf16[2,256,256]{2,1,0:T(8,128)(2,1)S(1)}, u32[]{:S(2)}, u32[]{:S(2)}) collective-permute-start(bf16[2,256,256]{2,1,0:T(8,128)(2,1)S(1)} %shard_map.123.refs_0_), channel_id=1, source_target_pairs={{0,16},{16,0},{1,17},{17,1},{2,18},{18,2},{3,19},{19,3},{4,20},{20... | collective-permute-start | bytes 786440 | tf_op jit(solution)/shard_map/ppermute | solution.py:262
  14.6 10.1 %collective-permute-start.2 = (bf16[2,256,256]{2,1,0:T(8,128)(2,1)S(1)}, bf16[2,256,256]{2,1,0:T(8,128)(2,1)S(1)}, u32[]{:S(2)}, u32[]{:S(2)}) collective-permute-start(bf16[2,256,256]{2,1,0:T(8,128)(2,1)S(1)} %collective-permute-done.1.refs_1_), channel_id=1, source_target_pairs={{0,2},{1,15},{2,4},{3,1},{4,6},{5,3},{6,8},{7,5},{8,10},{9,7},{10,... | collective-permute-start | bytes 786440 | tf_op jit(solution)/shard_map/ppermute | solution.py:283
  17.5 4.3 %collective-permute-start.5 = (bf16[256,256]{1,0:T(8,128)(2,1)S(1)}, bf16[256,256]{1,0:T(8,128)(2,1)S(1)}, u32[]{:S(2)}, u32[]{:S(2)}) collective-permute-start(bf16[256,256]{1,0:T(8,128)(2,1)S(1)} %shard_map.124.refs_0_), channel_id=1, source_target_pairs={{0,32},{32,0},{1,33},{33,1},{2,34},{34,2},{3,35},{35,3},{4,36},{36... | collective-permute-start | bytes 393224 | tf_op jit(solution)/shard_map/ppermute | solution.py:262
  20.0 15.4 %collective-permute-start.8 = (bf16[2,256,256]{2,1,0:T(8,128)(2,1)S(1)}, bf16[2,256,256]{2,1,0:T(8,128)(2,1)S(1)}, u32[]{:S(2)}, u32[]{:S(2)}) collective-permute-start(bf16[2,256,256]{2,1,0:T(8,128)(2,1)S(1)} %collective-permute-done.1.refs_1_), channel_id=1, source_target_pairs={{0,1},{1,0},{2,3},{3,2},{4,5},{5,4},{6,7},{7,6},{8,9},{9,8},{10,11... | collective-permute-start | bytes 786440 | tf_op jit(solution)/shard_map/ppermute | solution.py:262
  21.8 13.6 %collective-permute-start.6 = (bf16[2,256,256]{2,1,0:T(8,128)(2,1)S(1)}, bf16[2,256,256]{2,1,0:T(8,128)(2,1)S(1)}, u32[]{:S(2)}, u32[]{:S(2)}) collective-permute-start(bf16[2,256,256]{2,1,0:T(8,128)(2,1)S(1)} %shard_map.126.refs_6_.refs_7_), channel_id=1, source_target_pairs={{0,64},{64,128},{128,192},{192,0},{1,65},{65,129},{129,193},{193,1... | collective-permute-start | bytes 786440 | tf_op jit(solution)/shard_map/ppermute | solution.py:262
  23.2 12.2 %collective-permute-start.7 = (bf16[2,256,256]{2,1,0:T(8,128)(2,1)S(1)}, bf16[2,256,256]{2,1,0:T(8,128)(2,1)S(1)}, u32[]{:S(2)}, u32[]{:S(2)}) collective-permute-start(bf16[2,256,256]{2,1,0:T(8,128)(2,1)S(1)} %shard_map.126.refs_6_.refs_7_), channel_id=1, source_target_pairs={{0,192},{64,0},{128,64},{192,128},{1,193},{65,1},{129,65},{193,129... | collective-permute-start | bytes 786440 | tf_op jit(solution)/shard_map/ppermute | solution.py:262
  24.7 10.7 %collective-permute-start.9 = (bf16[2,256,256]{2,1,0:T(8,128)(2,1)S(1)}, bf16[2,256,256]{2,1,0:T(8,128)(2,1)S(1)}, u32[]{:S(2)}, u32[]{:S(2)}) collective-permute-start(bf16[2,256,256]{2,1,0:T(8,128)(2,1)S(1)} %collective-permute-done.2.refs_1_.refs_2_), channel_id=1, source_target_pairs={{0,1},{1,0},{2,3},{3,2},{4,5},{5,4},{6,7},{7,6},{8,9},{9,8},{10,11... | collective-permute-start | bytes 786440 | tf_op jit(solution)/shard_map/ppermute | solution.py:262
  24.8 10.6 %collective-permute-start.4 = (bf16[4,256,256]{2,1,0:T(8,128)(2,1)S(1)}, bf16[4,256,256]{2,1,0:T(8,128)(2,1)S(1)}, u32[]{:S(2)}, u32[]{:S(2)}) collective-permute-start(bf16[4,256,256]{2,1,0:T(8,128)(2,1)S(1)} %shard_map.125), channel_id=1, source_target_pairs={{0,2},{1,15},{2,4},{3,1},{4,6},{5,3},{6,8},{7,5},{8,10},{9,7},{10,... | collective-permute-start | bytes 1572872 | tf_op jit(solution)/shard_map/ppermute | solution.py:283
  35.4 3.2 %collective-permute-start.12 = (bf16[4,256,256]{2,1,0:T(8,128)(2,1)S(1)}, bf16[4,256,256]{2,1,0:T(8,128)(2,1)S(1)}, u32[]{:S(2)}, u32[]{:S(2)}) collective-permute-start(bf16[4,256,256]{2,1,0:T(8,128)(2,1)S(1)} %collective-permute-done.4.refs_5_.refs_1_), channel_id=1, source_target_pairs={{0,1},{1,0},{2,3},{3,2},{4,5},{5,4},{6,7},{7,6},{8,9},{9,8},{10,11... | collective-permute-start | bytes 1572872 | tf_op jit(solution)/shard_map/ppermute | solution.py:262
  36.7 9.9 %collective-permute-start.10 = (bf16[3,256,256]{2,1,0:T(8,128)(2,1)S(1)}, bf16[3,256,256]{2,1,0:T(8,128)(2,1)S(1)}, u32[]{:S(2)}, u32[]{:S(2)}) collective-permute-start(bf16[3,256,256]{2,1,0:T(8,128)(2,1)S(1)} %slice.9), channel_id=1, source_target_pairs={{0,2},{1,15},{2,4},{3,1},{4,6},{5,3},{6,8},{7,5},{8,10},{9,7},{10,... | collective-permute-start | bytes 1179656 | tf_op jit(solution)/shard_map/ppermute | solution.py:283
  38.6 8.0 %collective-permute-start.11 = (bf16[2,256,256]{2,1,0:T(8,128)(2,1)S(1)}, bf16[2,256,256]{2,1,0:T(8,128)(2,1)S(1)}, u32[]{:S(2)}, u32[]{:S(2)}) collective-permute-start(bf16[2,256,256]{2,1,0:T(8,128)(2,1)S(1)} %collective-permute-done.6.refs_8_.refs_9_), channel_id=1, source_target_pairs={{0,64},{64,128},{128,192},{192,0},{1,65},{65,129},{129,193},{193,1... | collective-permute-start | bytes 786440 | tf_op jit(solution)/shard_map/ppermute | solution.py:262
  46.6 4.5 %collective-permute-start.13 = (bf16[3,256,256]{2,1,0:T(8,128)(2,1)S(1)}, bf16[3,256,256]{2,1,0:T(8,128)(2,1)S(1)}, u32[]{:S(2)}, u32[]{:S(2)}) collective-permute-start(bf16[3,256,256]{2,1,0:T(8,128)(2,1)S(1)} %collective-permute-done.10.refs_3_.refs_0_), channel_id=1, source_target_pairs={{0,1},{1,0},{2,3},{3,2},{4,5},{5,4},{6,7},{7,6},{8,9},{9,8},{10,11... | collective-permute-start | bytes 1179656 | tf_op jit(solution)/shard_map/ppermute | solution.py:262
  46.6 8.3 %collective-permute-start.14 = (bf16[2,256,256]{2,1,0:T(8,128)(2,1)S(1)}, bf16[2,256,256]{2,1,0:T(8,128)(2,1)S(1)}, u32[]{:S(2)}, u32[]{:S(2)}) collective-permute-start(bf16[2,256,256]{2,1,0:T(8,128)(2,1)S(1)} %slice.10), channel_id=1, source_target_pairs={{0,2},{1,15},{2,4},{3,1},{4,6},{5,3},{6,8},{7,5},{8,10},{9,7},{10,... | collective-permute-start | bytes 786440 | tf_op jit(solution)/shard_map/ppermute | solution.py:283
  49.3 5.6 %collective-permute-start.15 = (bf16[1,256,256]{2,1,0:T(8,128)(2,1)S(1)}, bf16[1,256,256]{2,1,0:T(8,128)(2,1)S(1)}, u32[]{:S(2)}, u32[]{:S(2)}) collective-permute-start(bf16[1,256,256]{2,1,0:T(8,128)(2,1)S(1)} %slice.11), channel_id=1, source_target_pairs={{0,16},{16,0},{1,17},{17,1},{2,18},{18,2},{3,19},{19,3},{4,20},{20... | collective-permute-start | bytes 393224 | tf_op jit(solution)/shard_map/ppermute | solution.py:262
  54.9 1.7 %collective-permute-start.16 = (bf16[2,256,256]{2,1,0:T(8,128)(2,1)S(1)}, bf16[2,256,256]{2,1,0:T(8,128)(2,1)S(1)}, u32[]{:S(2)}, u32[]{:S(2)}) collective-permute-start(bf16[2,256,256]{2,1,0:T(8,128)(2,1)S(1)} %collective-permute-done.14.refs_2_), channel_id=1, source_target_pairs={{0,1},{1,0},{2,3},{3,2},{4,5},{5,4},{6,7},{7,6},{8,9},{9,8},{10,11... | collective-permute-start | bytes 786440 | tf_op jit(solution)/shard_map/ppermute | solution.py:262
  54.9 1.7 %collective-permute-start.17 = (bf16[1,256,256]{2,1,0:T(8,128)(2,1)S(1)}, bf16[1,256,256]{2,1,0:T(8,128)(2,1)S(1)}, u32[]{:S(2)}, u32[]{:S(2)}) collective-permute-start(bf16[1,256,256]{2,1,0:T(8,128)(2,1)S(1)} %collective-permute-done.15.refs_4_), channel_id=1, source_target_pairs={{0,1},{1,0},{2,3},{3,2},{4,5},{5,4},{6,7},{7,6},{8,9},{9,8},{10,11... | collective-permute-start | bytes 393224 | tf_op jit(solution)/shard_map/ppermute | solution.py:262
  59.5 42.7 %copy-start.2 = (bf16[256,256]{1,0:T(8,128)(2,1)S(1)}, bf16[256,256]{1,0:T(8,128)(2,1)}, u32[]{:S(2)}) copy-start(bf16[256,256]{1,0:T(8,128)(2,1)} %weight_ref.1) | copy-start | bytes 393220
  59.5 17.3 %collective-permute-start.18 = (bf16[4,256,256]{2,1,0:T(8,128)(2,1)S(1)}, bf16[4,256,256]{2,1,0:T(8,128)(2,1)S(1)}, u32[]{:S(2)}, u32[]{:S(2)}) collective-permute-start(bf16[4,256,256]{2,1,0:T(8,128)(2,1)S(1)} %get-tuple-element.69), channel_id=1, source_target_pairs={{0,32},{32,0},{1,33},{33,1},{2,34},{34,2},{3,35},{35,3},{4,36},{36... | collective-permute-start | bytes 1572872 | tf_op jit(solution)/shard_map/ppermute | solution.py:262
  77.4 9.0 %collective-permute-start.19 = (bf16[2,256,256]{2,1,0:T(8,128)(2,1)S(1)}, bf16[2,256,256]{2,1,0:T(8,128)(2,1)S(1)}, u32[]{:S(2)}, u32[]{:S(2)}) collective-permute-start(bf16[2,256,256]{2,1,0:T(8,128)(2,1)S(1)} %get-tuple-element.72), channel_id=1, source_target_pairs={{0,128},{64,192},{128,0},{192,64},{1,129},{65,193},{129,1},{193,65... | collective-permute-start | bytes 786440 | tf_op jit(solution)/shard_map/ppermute | solution.py:262
  79.6 15.5 %all-to-all-start.1 = ((bf16[16,16,256]{2,1,0:T(8,128)(2,1)}), bf16[16,16,256]{2,1,0:T(8,128)(2,1)S(1)}, u32[]{:S(2)}, u32[]{:S(2)}) async-start(bf16[16,16,256]{2,1,0:T(8,128)(2,1)} %shard_map.133), calls=%async_computation.1 | async-start | bytes 262144 | tf_op jit(solution)/shard_map/all_to_all | solution.py:486
  86.5 8.6 %collective-permute-start.20 = (bf16[256,256]{1,0:T(8,128)(2,1)S(1)}, bf16[256,256]{1,0:T(8,128)(2,1)S(1)}, u32[]{:S(2)}, u32[]{:S(2)}) collective-permute-start(bf16[256,256]{1,0:T(8,128)(2,1)S(1)} %get-tuple-element.75), channel_id=1, source_target_pairs={{0,64},{64,0},{128,192},{192,128},{1,65},{65,1},{129,193},{193,129... | collective-permute-start | bytes 393224 | tf_op jit(solution)/shard_map/ppermute | solution.py:497
  95.8 13.5 %all-to-all-start.2 = ((f32[16,16,256]{2,1,0:T(8,128)}), f32[16,16,256]{2,1,0:T(8,128)S(1)}, u32[]{:S(2)}, u32[]{:S(2)}) async-start(f32[16,16,256]{2,1,0:T(8,128)} %shard_map.135), calls=%async_computation.2 | async-start | bytes 524288 | tf_op jit(solution)/shard_map/all_to_all | solution.py:506
  (10 other events, 34.7 us)

commit v4 on v3

--- a/solution.py
+++ b/solution.py
@@ -23,7 +23,15 @@
 BF16 = jnp.bfloat16
 
 
-def mask_kernel(grad_ref, act_ref, out_ref):
+def mask_kernel(grad_hbm, act_hbm, out_ref, grad_ref, act_ref, sems):
+    copies = [
+        pltpu.make_async_copy(src, dst, sems.at[k])
+        for k, (src, dst) in enumerate(((grad_hbm, grad_ref), (act_hbm, act_ref)))
+    ]
+    for copy in copies:
+        copy.start()
+    for copy in copies:
+        copy.wait()
     grad = grad_ref[...].astype(F32)
     kept = jnp.where(act_ref[...].astype(F32) > 0, grad, 0.0)
     out_ref[...] = kept.T.astype(BF16)
@@ -37,7 +45,7 @@
     where_ref,
     count_ref,
     decay_ref,
-    rows_ref,
+    rows_hbm,
     time_ref,
     degree_ref,
     near_row,
@@ -45,6 +53,7 @@
     near_col,
     far_col,
     ends_ref,
+    rows_ref,
     row_time,
     col_time,
     row_scale,
@@ -58,6 +67,7 @@
         (time_ref.at[pl.ds(row_at, tile_rows)], row_time),
         (time_ref.at[pl.ds(col_at, tile_cols)], col_time),
         (degree_ref.at[pl.ds(row_at, tile_rows)], row_scale),
+        (rows_hbm, rows_ref),
     ]
     copies = [
         pltpu.make_async_copy(src, dst, node_sem.at[k])
@@ -66,6 +76,8 @@
     for copy in copies:
         copy.start()
 
+    for copy in copies:
+        copy.wait()
     xh, z, ring = where_ref[2], where_ref[3], where_ref[5]
     slot = lax.broadcasted_iota(jnp.int32, rows_ref.shape, 1)
     rows = jnp.where(slot < count_ref[0, 0], rows_ref[...], tile_rows)
@@ -90,8 +102,6 @@
                 jnp.where(rows < chip * 4, 1, 0).astype(jnp.int32)
             )
 
-    for copy in copies:
-        copy.wait()
     decay = decay_ref[0]
     later = decay * row_time[...].astype(F32)
     scale = row_scale[...]
@@ -223,24 +233,19 @@
     local_ref[...] = local.reshape(local_ref.shape)
 
 
-def half_kernel(where_ref, keep_ref, got_ref, kept_ref, give_ref):
-    y = where_ref[6]
-    for k in range(4):
-        summed = keep_ref[y ^ k] + got_ref[y ^ k].astype(F32)
-        if k < 2:
-            kept_ref[k] = summed
-        else:
-            give_ref[k - 2] = summed.astype(BF16)
-
-
-def quarter_kernel(keep_ref, got_ref, kept_ref, give_ref):
-    kept_ref[...] = keep_ref[0] + got_ref[0].astype(F32)
-    give_ref[...] = (keep_ref[1] + got_ref[1].astype(F32)).astype(BF16)
-
-
-def finish_kernel(weight_ref, keep_ref, got_ref, out_ref):
-    summed = keep_ref[...] + got_ref[...].astype(F32)
-    out_ref[...] = lax.dot_general(
+def half_kernel(where_ref, keep_ref, got_ref, own_ref, *out_refs):
+    y, reach = where_ref[6], where_ref[8]
+    own_ref[...] = keep_ref[y] + got_ref[y].astype(F32)
+    for k, out_ref in enumerate(out_refs):
+        at = lax.rem(y + k + 1, reach)
+        out_ref[...] = (keep_ref[at] + got_ref[at].astype(F32)).astype(BF16)
+
+
+def finish_kernel(weight_ref, own_ref, *refs):
+    summed = own_ref[...]
+    for ref in refs[:-1]:
+        summed = summed + ref[...].astype(F32)
+    refs[-1][...] = lax.dot_general(
         summed.T.astype(BF16),
         weight_ref[...],
         (((1,), (1,)), ((), ())),
@@ -294,9 +299,10 @@
         return [(flip, dz, k) for k in range(size)]
 
     pair = join(own, shift(own, "c", 1))
-    other = shift(pair, "xh", 1)
-    first, features_t = tie((onward(pair), turn(features)))
-    beside_t = shift(features_t, "xl", 1)
+    other = shift(own, "xh", 1)
+    other = join(other, shift(other, "c", 1))
+    features_t = turn(features)
+    first, beside_t = tie((onward(pair), shift(features_t, "xl", 1)))
     second, other = tie((onward(first), other))
     third = onward(join(other, second))
     second, where = tie((second, where))
@@ -353,13 +359,21 @@
         + [lax.axis_index("y"), lax.axis_index("xl"), lax.axis_size("y")]
     ).astype(jnp.int32)
 
+    def stay(array):
+        return pltpu.with_memory_space_constraint(array, pltpu.HBM)
+
     masked = pl.pallas_call(
         mask_kernel,
         out_shape=jax.ShapeDtypeStruct((width, nodes), BF16),
-        in_specs=[VMEM] * 2,
+        in_specs=[HBM] * 2,
         out_specs=VMEM,
+        scratch_shapes=[
+            pltpu.VMEM(out_grad.shape, BF16),
+            pltpu.VMEM(out_grad.shape, BF16),
+            pltpu.SemaphoreType.DMA((2,)),
+        ],
         compiler_params=TIGHT,
-    )(out_grad, pre_act)
+    )(stay(out_grad), stay(pre_act))
 
     def make_tables(where):
         lane = (tile_cols, 1, TILE)
@@ -372,13 +386,14 @@
                 jax.ShapeDtypeStruct(lane, F32),
                 jax.ShapeDtypeStruct((14,), jnp.int32),
             ),
-            in_specs=[SMEM] * 3 + [VMEM] + [HBM] * 2,
+            in_specs=[SMEM] * 3 + [HBM] * 3,
             out_specs=(VMEM,) * 4 + (SMEM,),
             scratch_shapes=[
+                pltpu.VMEM((1, slots), jnp.int32),
                 pltpu.VMEM((tile_rows, TILE), jnp.int32),
                 pltpu.VMEM((tile_cols, TILE), jnp.int32),
                 pltpu.VMEM((tile_rows, TILE), F32),
-                pltpu.SemaphoreType.DMA((3,)),
+                pltpu.SemaphoreType.DMA((4,)),
             ],
             compiler_params=ROOM,
             cost_estimate=pl.CostEstimate(
@@ -388,9 +403,9 @@
             where,
             tile_count,
             decay_rate,
-            tile_row,
-            node_time.reshape(-1, TILE),
-            inv_degree.reshape(-1, TILE),
+            stay(tile_row),
+            stay(node_time.reshape(-1, TILE)),
+            stay(inv_degree.reshape(-1, TILE)),
         )
 
     def turn(array):
@@ -471,38 +486,27 @@
     got = shift(give, "xl", 1)
     slices = lax.all_to_all(local, NEAR, 0, 0, tiled=True)
     slices, got = lax.optimization_barrier((slices, got))
-    block = (2, width, nodes)
-    keep, give = pl.pallas_call(
+    block = (width, nodes)
+    own, *others = pl.pallas_call(
         half_kernel,
-        out_shape=(
-            jax.ShapeDtypeStruct(block, F32),
-            jax.ShapeDtypeStruct(block, BF16),
-        ),
+        out_shape=(jax.ShapeDtypeStruct(block, F32),)
+        + (jax.ShapeDtypeStruct(block, BF16),) * (reach - 1),
         in_specs=[SMEM, VMEM, VMEM],
-        out_specs=(VMEM, VMEM),
+        out_specs=(VMEM,) * reach,
         compiler_params=TIGHT,
     )(where, keep, got)
-    got = shift(give, "y", 2)
+    sent = [shift(other, "y", k + 1) for k, other in enumerate(others)]
     slices = lax.all_to_all(spread(slices, n_far, BF16), FAR, 0, 0, tiled=True)
-    keep, give = pl.pallas_call(
-        quarter_kernel,
-        out_shape=(
-            jax.ShapeDtypeStruct((width, nodes), F32),
-            jax.ShapeDtypeStruct((width, nodes), BF16),
-        ),
-        in_specs=[VMEM, VMEM],
-        out_specs=(VMEM, VMEM),
-        compiler_params=TIGHT,
-    )(keep, got)
-    got = lax.ppermute(give, "y", [(y, y ^ 1) for y in range(reach)])
-    slices, got = lax.optimization_barrier((slices, got))
     grad_input = pl.pallas_call(
         finish_kernel,
         out_shape=jax.ShapeDtypeStruct((nodes, features.shape[1]), BF16),
-        in_specs=[VMEM] * 3,
+        in_specs=[VMEM] * (len(sent) + 2),
         out_specs=VMEM,
+        cost_estimate=pl.CostEstimate(
+            flops=10**10, bytes_accessed=0, transcendentals=0
+        ),
         compiler_params=TIGHT,
-    )(weight, keep, got)
+    )(weight, own, *sent)
     slices = lax.all_to_all(spread(slices, n_near, F32), NEAR, 0, 0, tiled=True)
     return grad_input, slices.reshape(features.shape[1], width)
 

time: 110 us -> 106 us (0.964)
  local copies, waits for them, and re-layouts: 6.48 us -> 1.77 us
  Pallas kernels: 14.1 us -> 16.6 us
  blocking collectives: 17.1 us -> 15 us
  starting transfers between devices: 44.4 us -> 43.3 us
    unnamed x23 -> x13, local copies, waits for them, and re-layouts: 6.34 us -> 1.63 us
    all_to_all x1, waiting for transfers between devices: 8.15 us -> 5.22 us  [shards(): slices = lax.all_to_all(spread(slices, n_far, BF16), FAR, 0, 0, tiled=True)]
    ppermute x5, starting transfers between devices: 15.8 us -> 13.4 us  [onward(): return lax.ppermute(block, ('z', 'c'), pairs)]
    all_to_all x1, blocking collectives: 17.1 us -> 15 us  [shards(): slices = lax.all_to_all(local, NEAR, 0, 0, tiled=True)]
    ppermute x5, waiting for transfers between devices: 0.01 us -> 1.98 us  [onward(): return lax.ppermute(block, ('z', 'c'), pairs)]
    ppermute x15 -> x18, waiting for transfers between devices: 11.3 us -> 12.9 us  [shift(): lax.ppermute(block, axis, [(i, (i + step) % size) for i in range(size)])]
    ppermute x15 -> x18, starting transfers between devices: 15.4 us -> 16.9 us  [shift(): lax.ppermute(block, axis, [(i, (i + step) % size) for i in range(size)])]
    all_to_all x1, starting transfers between devices: 6.51 us -> 7.8 us  [shards(): slices = lax.all_to_all(spread(slices, n_far, BF16), FAR, 0, 0, tiled=True)]
  transfers between devices with their start and end apart: 23 -> 25, of which waited for: 8 -> 9; matrix products, arithmetic and copies ran while one was open for 0% -> 0% of each run, Pallas kernels for 9% -> 11%
where the time goes in v4:
time: 106 us; the launch traced here: 105 us
  starting transfers between devices  43.3 us (41%)
  waiting for transfers between devices  26.3 us (25%)
  Pallas kernels  16.6 us (16%)
  blocking collectives  15 us (14%)
  between operations  2.16 us (2%)
  local copies, waits for them, and re-layouts  1.77 us (2%)
    ppermute x18, starting transfers between devices, shift(): lax.ppermute(block, axis, [(i, (i + step) % size) for i in range(size)])  16.9 us
    all_to_all x1, blocking collectives, shards(): slices = lax.all_to_all(local, NEAR, 0, 0, tiled=True)  15 us
    ppermute x5, starting transfers between devices, onward(): return lax.ppermute(block, ('z', 'c'), pairs)  13.4 us
    ppermute x18, waiting for transfers between devices, shift(): lax.ppermute(block, axis, [(i, (i + step) % size) for i in range(size)])  12.9 us
    all_to_all x1, starting transfers between devices, shards(): slices = lax.all_to_all(spread(slices, n_far, BF16), FAR, 0, 0, tiled=True)  7.8 us
    all_to_all x1, waiting for transfers between devices, shards(): slices = lax.all_to_all(spread(slices, n_near, F32), NEAR, 0, 0, tiled=True)  6.26 us
    all_to_all x1, waiting for transfers between devices, shards(): slices = lax.all_to_all(spread(slices, n_far, BF16), FAR, 0, 0, tiled=True)  5.22 us
    all_to_all x1, starting transfers between devices, shards(): slices = lax.all_to_all(spread(slices, n_near, F32), NEAR, 0, 0, tiled=True)  5.2 us
  transfers between devices with their start and end apart: 25, of which 9 were waited for; matrix products, arithmetic and copies ran while one was open for 0% of the time, Pallas kernels for 11%

profile of v4, /device:TPU:1, one launch (start us, length us, event | category | flops | bytes accessed | tf_op | source)
XLA Modules:
  0.0 105.2 jit_solution(6949757955358726101)
XLA Ops:
  1.7 3.3 %collective-permute-start = (bf16[256,256]{1,0:T(8,128)(2,1)S(1)}, bf16[256,256]{1,0:T(8,128)(2,1)S(1)}, u32[]{:S(2)}, u32[]{:S(2)}) collective-permute-start(bf16[256,256]{1,0:T(8,128)(2,1)S(1)} %shard_map.122.refs_0_), channel_id=1, source_target_pairs={{0,1},{1,0},{2,3},{3,2},{4,5},{5,4},{6,7},{7,6},{8,9},{9,8},{10,11... | collective-permute-start | bytes 393224 | tf_op jit(solution)/shard_map/ppermute | solution.py:267
  6.1 3.9 %collective-permute-start.1 = (bf16[2,256,256]{2,1,0:T(8,128)(2,1)S(1)}, bf16[2,256,256]{2,1,0:T(8,128)(2,1)S(1)}, u32[]{:S(2)}, u32[]{:S(2)}) collective-permute-start(bf16[2,256,256]{2,1,0:T(8,128)(2,1)S(1)} %shard_map.123.refs_0_), channel_id=1, source_target_pairs={{0,2},{1,15},{2,4},{3,1},{4,6},{5,3},{6,8},{7,5},{8,10},{9,7},{10,... | collective-permute-start | bytes 786440 | tf_op jit(solution)/shard_map/ppermute | solution.py:288
  11.0 1.3 %collective-permute-start.2 = (bf16[256,256]{1,0:T(8,128)(2,1)S(1)}, bf16[256,256]{1,0:T(8,128)(2,1)S(1)}, u32[]{:S(2)}, u32[]{:S(2)}) collective-permute-start(bf16[256,256]{1,0:T(8,128)(2,1)S(1)} %shard_map.124.refs_0_), channel_id=1, source_target_pairs={{0,32},{32,0},{1,33},{33,1},{2,34},{34,2},{3,35},{35,3},{4,36},{36... | collective-permute-start | bytes 393224 | tf_op jit(solution)/shard_map/ppermute | solution.py:267
  12.3 2.5 %collective-permute-start.4 = (bf16[256,256]{1,0:T(8,128)(2,1)S(1)}, bf16[256,256]{1,0:T(8,128)(2,1)S(1)}, u32[]{:S(2)}, u32[]{:S(2)}) collective-permute-start(bf16[256,256]{1,0:T(8,128)(2,1)S(1)} %shard_map.122.refs_0_), channel_id=1, source_target_pairs={{0,16},{16,0},{1,17},{17,1},{2,18},{18,2},{3,19},{19,3},{4,20},{20... | collective-permute-start | bytes 393224 | tf_op jit(solution)/shard_map/ppermute | solution.py:267
  17.2 1.3 %collective-permute-done.4.refs_0_ = bf16[256,256]{1,0:T(8,128)(2,1)S(1)} collective-permute-done((bf16[256,256]{1,0:T(8,128)(2,1)S(1)}, bf16[256,256]{1,0:T(8,128)(2,1)S(1)}, u32[]{:S(2)}, u32[]{:S(2)}) %collective-permute-start.4) | collective-permute-done | bytes 131104 | tf_op jit(solution)/shard_map/ppermute | solution.py:267
  19.9 1.4 %collective-permute-start.7 = (bf16[2,256,256]{2,1,0:T(8,128)(2,1)S(1)}, bf16[2,256,256]{2,1,0:T(8,128)(2,1)S(1)}, u32[]{:S(2)}, u32[]{:S(2)}) collective-permute-start(bf16[2,256,256]{2,1,0:T(8,128)(2,1)S(1)} %shard_map.127.refs_6_.refs_7_), channel_id=1, source_target_pairs={{0,64},{64,128},{128,192},{192,0},{1,65},{65,129},{129,193},{193,1... | collective-permute-start | bytes 786440 | tf_op jit(solution)/shard_map/ppermute | solution.py:267
  21.3 1.5 %collective-permute-start.8 = (bf16[2,256,256]{2,1,0:T(8,128)(2,1)S(1)}, bf16[2,256,256]{2,1,0:T(8,128)(2,1)S(1)}, u32[]{:S(2)}, u32[]{:S(2)}) collective-permute-start(bf16[2,256,256]{2,1,0:T(8,128)(2,1)S(1)} %shard_map.127.refs_6_.refs_7_), channel_id=1, source_target_pairs={{0,192},{64,0},{128,64},{192,128},{1,193},{65,1},{129,65},{193,129... | collective-permute-start | bytes 786440 | tf_op jit(solution)/shard_map/ppermute | solution.py:267
  23.8 3.9 %collective-permute-start.6 = (bf16[4,256,256]{2,1,0:T(8,128)(2,1)S(1)}, bf16[4,256,256]{2,1,0:T(8,128)(2,1)S(1)}, u32[]{:S(2)}, u32[]{:S(2)}) collective-permute-start(bf16[4,256,256]{2,1,0:T(8,128)(2,1)S(1)} %shard_map.126), channel_id=1, source_target_pairs={{0,2},{1,15},{2,4},{3,1},{4,6},{5,3},{6,8},{7,5},{8,10},{9,7},{10,... | collective-permute-start | bytes 1572872 | tf_op jit(solution)/shard_map/ppermute | solution.py:288
  27.7 4.1 %shard_map.128 = (f32[64,128,128]{2,1,0:T(8,128)S(1)}, f32[64,128,128]{2,1,0:T(8,128)S(1)}, f32[16,1,128]{2,1,0:T(1,128)S(1)}, f32[16,1,128]{2,1,0:T(1,128)S(1)}, s32[14]{0:T(128)S(1)}) custom-call(s32[9]{0:T(128)S(1)} %stack.31.where_ref, s32[1,1]{1,0:T(1,128)S(6)} %copy.15.count_ref, f32[1]{0:T(128)S(6)} %copy.14.decay_ref, s32[1,176]{1,0:T(1,128)} %rows_ref.5, ...), custom_call_target="tpu_custom_call" | custom-call | flops 6000000000 | tf_op jit(solution)/shard_map/pallas_call | solution.py:380
  31.9 2.0 %collective-permute-done.6.refs_5_.refs_1_ = bf16[4,256,256]{2,1,0:T(8,128)(2,1)S(1)} collective-permute-done((bf16[4,256,256]{2,1,0:T(8,128)(2,1)S(1)}, bf16[4,256,256]{2,1,0:T(8,128)(2,1)S(1)}, u32[]{:S(2)}, u32[]{:S(2)}) %collective-permute-start.6) | collective-permute-done | bytes 524320 | tf_op jit(solution)/shard_map/ppermute | solution.py:288
  33.8 1.7 %collective-permute-start.13 = (bf16[4,256,256]{2,1,0:T(8,128)(2,1)S(1)}, bf16[4,256,256]{2,1,0:T(8,128)(2,1)S(1)}, u32[]{:S(2)}, u32[]{:S(2)}) collective-permute-start(bf16[4,256,256]{2,1,0:T(8,128)(2,1)S(1)} %collective-permute-done.6.refs_5_.refs_1_), channel_id=1, source_target_pairs={{0,1},{1,0},{2,3},{3,2},{4,5},{5,4},{6,7},{7,6},{8,9},{9,8},{10,11... | collective-permute-start | bytes 1572872 | tf_op jit(solution)/shard_map/ppermute | solution.py:267
  35.6 1.8 %collective-permute-start.11 = (bf16[3,256,256]{2,1,0:T(8,128)(2,1)S(1)}, bf16[3,256,256]{2,1,0:T(8,128)(2,1)S(1)}, u32[]{:S(2)}, u32[]{:S(2)}) collective-permute-start(bf16[3,256,256]{2,1,0:T(8,128)(2,1)S(1)} %slice.9), channel_id=1, source_target_pairs={{0,2},{1,15},{2,4},{3,1},{4,6},{5,3},{6,8},{7,5},{8,10},{9,7},{10,... | collective-permute-start | bytes 1179656 | tf_op jit(solution)/shard_map/ppermute | solution.py:288
  37.5 2.2 %shard_map.129.refs_10_ = f32[16,256,128]{2,1,0:T(8,128)S(1)} custom-call(s32[9]{0:T(128)S(1)} %stack.31.where_ref, s32[14]{0:T(128)S(1)} %get-tuple-element.49.ends_ref, s32[1,176]{1,0:T(1,128)S(1)} %copy-done.1, s32[1,176]{1,0:T(1,128)S(1)} %copy-done.2, bf16[2,256,256]{2,1,0:T(8,128)(2,1)S(1)} %shard_map.123.refs_0_, ...), custom_call_target="tpu_custom_call" | custom-call | flops 3000000000 | tf_op jit(solution)/shard_map/pallas_call | solution.py:429
  39.7 5.9 %collective-permute-done.12.refs_12_.refs_13_ = bf16[2,256,256]{2,1,0:T(8,128)(2,1)S(1)} collective-permute-done((bf16[2,256,256]{2,1,0:T(8,128)(2,1)S(1)}, bf16[2,256,256]{2,1,0:T(8,128)(2,1)S(1)}, u32[]{:S(2)}, u32[]{:S(2)}) %collective-permute-start.12) | collective-permute-done | bytes 262176 | tf_op jit(solution)/shard_map/ppermute | solution.py:267
  45.7 2.5 %collective-permute-start.15 = (bf16[2,256,256]{2,1,0:T(8,128)(2,1)S(1)}, bf16[2,256,256]{2,1,0:T(8,128)(2,1)S(1)}, u32[]{:S(2)}, u32[]{:S(2)}) collective-permute-start(bf16[2,256,256]{2,1,0:T(8,128)(2,1)S(1)} %slice.10), channel_id=1, source_target_pairs={{0,2},{1,15},{2,4},{3,1},{4,6},{5,3},{6,8},{7,5},{8,10},{9,7},{10,... | collective-permute-start | bytes 786440 | tf_op jit(solution)/shard_map/ppermute | solution.py:288
  48.7 2.6 %shard_map.130.refs_19_ = f32[16,256,128]{2,1,0:T(8,128)S(1)} custom-call(s32[9]{0:T(128)S(1)} %stack.31.where_ref, s32[14]{0:T(128)S(1)} %get-tuple-element.49.ends_ref, s32[1,176]{1,0:T(1,128)S(1)} %copy-done.1, s32[1,176]{1,0:T(1,128)S(1)} %copy-done.2, bf16[2,256,256]{2,1,0:T(8,128)(2,1)S(1)} %shard_map.125.refs_0_, ...), custom_call_target="tpu_custom_call" | custom-call | flops 3000000000 | tf_op jit(solution)/shard_map/pallas_call | solution.py:429
  51.4 2.2 %collective-permute-done.16.refs_4_ = bf16[1,256,256]{2,1,0:T(8,128)(2,1)S(1)} collective-permute-done((bf16[1,256,256]{2,1,0:T(8,128)(2,1)S(1)}, bf16[1,256,256]{2,1,0:T(8,128)(2,1)S(1)}, u32[]{:S(2)}, u32[]{:S(2)}) %collective-permute-start.16) | collective-permute-done | bytes 131104 | tf_op jit(solution)/shard_map/ppermute | solution.py:267
  55.3 3.4 %shard_map.131 = (f32[4,256,256]{2,1,0:T(8,128)S(1)}, bf16[4,256,256]{2,1,0:T(8,128)(2,1)S(1)}, f32[16,16,256]{2,1,0:T(8,128)S(1)}) custom-call(s32[9]{0:T(128)S(1)} %stack.31.where_ref, s32[14]{0:T(128)S(1)} %get-tuple-element.49.ends_ref, s32[1,176]{1,0:T(1,128)S(1)} %copy-done.1, s32[1,176]{1,0:T(1,128)S(1)} %copy-done.2, ...), custom_call_target="tpu_custom_call" | custom-call | flops 3000000000 | tf_op jit(solution)/shard_map/pallas_call | solution.py:451
  58.8 15.0 %all_to_all.15.in_ref = f32[16,16,256]{2,1,0:T(8,128)S(1)} all-to-all(f32[16,16,256]{2,1,0:T(8,128)S(1)} %get-tuple-element.66), channel_id=1, replica_groups=mesh['y'=4,'xl'=2,'xh'=2,'z'=8,'c'=2] {'y','xl','c'}, dimensions={0} | all-to-all | bytes 524288 | tf_op jit(solution)/shard_map/all_to_all | solution.py:487
  74.5 7.8 %all-to-all-start.1 = ((bf16[16,16,256]{2,1,0:T(8,128)(2,1)}), bf16[16,16,256]{2,1,0:T(8,128)(2,1)S(1)}, u32[]{:S(2)}, u32[]{:S(2)}) async-start(bf16[16,16,256]{2,1,0:T(8,128)(2,1)} %shard_map.134), calls=%async_computation.1 | async-start | bytes 262144 | tf_op jit(solution)/shard_map/all_to_all | solution.py:499
  83.3 2.0 %collective-permute-start.21 = (bf16[256,256]{1,0:T(8,128)(2,1)S(1)}, bf16[256,256]{1,0:T(8,128)(2,1)S(1)}, u32[]{:S(2)}, u32[]{:S(2)}) collective-permute-start(bf16[256,256]{1,0:T(8,128)(2,1)S(1)} %get-tuple-element.71), channel_id=1, source_target_pairs={{0,128},{64,192},{128,0},{192,64},{1,129},{65,193},{129,1},{193,65... | collective-permute-start | bytes 393224 | tf_op jit(solution)/shard_map/ppermute | solution.py:267
  86.1 5.2 %all-to-all-done.1.in_ref = bf16[16,16,256]{2,1,0:T(8,128)(2,1)S(1)} async-done(((bf16[16,16,256]{2,1,0:T(8,128)(2,1)}), bf16[16,16,256]{2,1,0:T(8,128)(2,1)S(1)}, u32[]{:S(2)}, u32[]{:S(2)}) %all-to-all-start.1) | async-done | bytes 131104 | tf_op jit(solution)/shard_map/all_to_all | solution.py:499
  92.0 5.2 %all-to-all-start.2 = ((f32[16,16,256]{2,1,0:T(8,128)}), f32[16,16,256]{2,1,0:T(8,128)S(1)}, u32[]{:S(2)}, u32[]{:S(2)}) async-start(f32[16,16,256]{2,1,0:T(8,128)} %shard_map.135), calls=%async_computation.2 | async-start | bytes 524288 | tf_op jit(solution)/shard_map/all_to_all | solution.py:510
  98.2 6.3 %all-to-all-done.2 = f32[16,16,256]{2,1,0:T(8,128)S(1)} async-done(((f32[16,16,256]{2,1,0:T(8,128)}), f32[16,16,256]{2,1,0:T(8,128)S(1)}, u32[]{:S(2)}, u32[]{:S(2)}) %all-to-all-start.2) | async-done | bytes 262176 | tf_op jit(solution)/shard_map/all_to_all | solution.py:510
  (59 shorter events, 14.0 us)
Async XLA Ops:
  1.7 4.3 %collective-permute-start = (bf16[256,256]{1,0:T(8,128)(2,1)S(1)}, bf16[256,256]{1,0:T(8,128)(2,1)S(1)}, u32[]{:S(2)}, u32[]{:S(2)}) collective-permute-start(bf16[256,256]{1,0:T(8,128)(2,1)S(1)} %shard_map.122.refs_0_), channel_id=1, source_target_pairs={{0,1},{1,0},{2,3},{3,2},{4,5},{5,4},{6,7},{7,6},{8,9},{9,8},{10,11... | collective-permute-start | bytes 393224 | tf_op jit(solution)/shard_map/ppermute | solution.py:267
  6.1 9.9 %collective-permute-start.1 = (bf16[2,256,256]{2,1,0:T(8,128)(2,1)S(1)}, bf16[2,256,256]{2,1,0:T(8,128)(2,1)S(1)}, u32[]{:S(2)}, u32[]{:S(2)}) collective-permute-start(bf16[2,256,256]{2,1,0:T(8,128)(2,1)S(1)} %shard_map.123.refs_0_), channel_id=1, source_target_pairs={{0,2},{1,15},{2,4},{3,1},{4,6},{5,3},{6,8},{7,5},{8,10},{9,7},{10,... | collective-permute-start | bytes 786440 | tf_op jit(solution)/shard_map/ppermute | solution.py:288
  11.0 5.0 %collective-permute-start.2 = (bf16[256,256]{1,0:T(8,128)(2,1)S(1)}, bf16[256,256]{1,0:T(8,128)(2,1)S(1)}, u32[]{:S(2)}, u32[]{:S(2)}) collective-permute-start(bf16[256,256]{1,0:T(8,128)(2,1)S(1)} %shard_map.124.refs_0_), channel_id=1, source_target_pairs={{0,32},{32,0},{1,33},{33,1},{2,34},{34,2},{3,35},{35,3},{4,36},{36... | collective-permute-start | bytes 393224 | tf_op jit(solution)/shard_map/ppermute | solution.py:267
  12.3 6.2 %collective-permute-start.4 = (bf16[256,256]{1,0:T(8,128)(2,1)S(1)}, bf16[256,256]{1,0:T(8,128)(2,1)S(1)}, u32[]{:S(2)}, u32[]{:S(2)}) collective-permute-start(bf16[256,256]{1,0:T(8,128)(2,1)S(1)} %shard_map.122.refs_0_), channel_id=1, source_target_pairs={{0,16},{16,0},{1,17},{17,1},{2,18},{18,2},{3,19},{19,3},{4,20},{20... | collective-permute-start | bytes 393224 | tf_op jit(solution)/shard_map/ppermute | solution.py:267
  16.0 7.8 %collective-permute-start.3 = (bf16[2,256,256]{2,1,0:T(8,128)(2,1)S(1)}, bf16[2,256,256]{2,1,0:T(8,128)(2,1)S(1)}, u32[]{:S(2)}, u32[]{:S(2)}) collective-permute-start(bf16[2,256,256]{2,1,0:T(8,128)(2,1)S(1)} %collective-permute-done.1.refs_1_), channel_id=1, source_target_pairs={{0,2},{1,15},{2,4},{3,1},{4,6},{5,3},{6,8},{7,5},{8,10},{9,7},{10,... | collective-permute-start | bytes 786440 | tf_op jit(solution)/shard_map/ppermute | solution.py:288
  19.9 11.9 %collective-permute-start.7 = (bf16[2,256,256]{2,1,0:T(8,128)(2,1)S(1)}, bf16[2,256,256]{2,1,0:T(8,128)(2,1)S(1)}, u32[]{:S(2)}, u32[]{:S(2)}) collective-permute-start(bf16[2,256,256]{2,1,0:T(8,128)(2,1)S(1)} %shard_map.127.refs_6_.refs_7_), channel_id=1, source_target_pairs={{0,64},{64,128},{128,192},{192,0},{1,65},{65,129},{129,193},{193,1... | collective-permute-start | bytes 786440 | tf_op jit(solution)/shard_map/ppermute | solution.py:267
  21.3 10.5 %collective-permute-start.8 = (bf16[2,256,256]{2,1,0:T(8,128)(2,1)S(1)}, bf16[2,256,256]{2,1,0:T(8,128)(2,1)S(1)}, u32[]{:S(2)}, u32[]{:S(2)}) collective-permute-start(bf16[2,256,256]{2,1,0:T(8,128)(2,1)S(1)} %shard_map.127.refs_6_.refs_7_), channel_id=1, source_target_pairs={{0,192},{64,0},{128,64},{192,128},{1,193},{65,1},{129,65},{193,129... | collective-permute-start | bytes 786440 | tf_op jit(solution)/shard_map/ppermute | solution.py:267
  22.9 9.0 %collective-permute-start.9 = (bf16[2,256,256]{2,1,0:T(8,128)(2,1)S(1)}, bf16[2,256,256]{2,1,0:T(8,128)(2,1)S(1)}, u32[]{:S(2)}, u32[]{:S(2)}) collective-permute-start(bf16[2,256,256]{2,1,0:T(8,128)(2,1)S(1)} %collective-permute-done.1.refs_1_), channel_id=1, source_target_pairs={{0,1},{1,0},{2,3},{3,2},{4,5},{5,4},{6,7},{7,6},{8,9},{9,8},{10,11... | collective-permute-start | bytes 786440 | tf_op jit(solution)/shard_map/ppermute | solution.py:267
  23.8 8.1 %collective-permute-start.10 = (bf16[2,256,256]{2,1,0:T(8,128)(2,1)S(1)}, bf16[2,256,256]{2,1,0:T(8,128)(2,1)S(1)}, u32[]{:S(2)}, u32[]{:S(2)}) collective-permute-start(bf16[2,256,256]{2,1,0:T(8,128)(2,1)S(1)} %collective-permute-done.3.refs_1_.refs_2_), channel_id=1, source_target_pairs={{0,1},{1,0},{2,3},{3,2},{4,5},{5,4},{6,7},{7,6},{8,9},{9,8},{10,11... | collective-permute-start | bytes 786440 | tf_op jit(solution)/shard_map/ppermute | solution.py:267
  23.8 10.0 %collective-permute-start.6 = (bf16[4,256,256]{2,1,0:T(8,128)(2,1)S(1)}, bf16[4,256,256]{2,1,0:T(8,128)(2,1)S(1)}, u32[]{:S(2)}, u32[]{:S(2)}) collective-permute-start(bf16[4,256,256]{2,1,0:T(8,128)(2,1)S(1)} %shard_map.126), channel_id=1, source_target_pairs={{0,2},{1,15},{2,4},{3,1},{4,6},{5,3},{6,8},{7,5},{8,10},{9,7},{10,... | collective-permute-start | bytes 1572872 | tf_op jit(solution)/shard_map/ppermute | solution.py:288
  33.8 3.7 %collective-permute-start.13 = (bf16[4,256,256]{2,1,0:T(8,128)(2,1)S(1)}, bf16[4,256,256]{2,1,0:T(8,128)(2,1)S(1)}, u32[]{:S(2)}, u32[]{:S(2)}) collective-permute-start(bf16[4,256,256]{2,1,0:T(8,128)(2,1)S(1)} %collective-permute-done.6.refs_5_.refs_1_), channel_id=1, source_target_pairs={{0,1},{1,0},{2,3},{3,2},{4,5},{5,4},{6,7},{7,6},{8,9},{9,8},{10,11... | collective-permute-start | bytes 1572872 | tf_op jit(solution)/shard_map/ppermute | solution.py:267
  35.6 10.1 %collective-permute-start.11 = (bf16[3,256,256]{2,1,0:T(8,128)(2,1)S(1)}, bf16[3,256,256]{2,1,0:T(8,128)(2,1)S(1)}, u32[]{:S(2)}, u32[]{:S(2)}) collective-permute-start(bf16[3,256,256]{2,1,0:T(8,128)(2,1)S(1)} %slice.9), channel_id=1, source_target_pairs={{0,2},{1,15},{2,4},{3,1},{4,6},{5,3},{6,8},{7,5},{8,10},{9,7},{10,... | collective-permute-start | bytes 1179656 | tf_op jit(solution)/shard_map/ppermute | solution.py:288
  37.4 8.2 %collective-permute-start.12 = (bf16[2,256,256]{2,1,0:T(8,128)(2,1)S(1)}, bf16[2,256,256]{2,1,0:T(8,128)(2,1)S(1)}, u32[]{:S(2)}, u32[]{:S(2)}) collective-permute-start(bf16[2,256,256]{2,1,0:T(8,128)(2,1)S(1)} %collective-permute-done.7.refs_8_.refs_9_), channel_id=1, source_target_pairs={{0,64},{64,128},{128,192},{192,0},{1,65},{65,129},{129,193},{193,1... | collective-permute-start | bytes 786440 | tf_op jit(solution)/shard_map/ppermute | solution.py:267
  45.7 3.1 %collective-permute-start.14 = (bf16[3,256,256]{2,1,0:T(8,128)(2,1)S(1)}, bf16[3,256,256]{2,1,0:T(8,128)(2,1)S(1)}, u32[]{:S(2)}, u32[]{:S(2)}) collective-permute-start(bf16[3,256,256]{2,1,0:T(8,128)(2,1)S(1)} %collective-permute-done.11.refs_3_.refs_0_), channel_id=1, source_target_pairs={{0,1},{1,0},{2,3},{3,2},{4,5},{5,4},{6,7},{7,6},{8,9},{9,8},{10,11... | collective-permute-start | bytes 1179656 | tf_op jit(solution)/shard_map/ppermute | solution.py:267
  45.7 7.9 %collective-permute-start.15 = (bf16[2,256,256]{2,1,0:T(8,128)(2,1)S(1)}, bf16[2,256,256]{2,1,0:T(8,128)(2,1)S(1)}, u32[]{:S(2)}, u32[]{:S(2)}) collective-permute-start(bf16[2,256,256]{2,1,0:T(8,128)(2,1)S(1)} %slice.10), channel_id=1, source_target_pairs={{0,2},{1,15},{2,4},{3,1},{4,6},{5,3},{6,8},{7,5},{8,10},{9,7},{10,... | collective-permute-start | bytes 786440 | tf_op jit(solution)/shard_map/ppermute | solution.py:288
  48.2 5.4 %collective-permute-start.16 = (bf16[1,256,256]{2,1,0:T(8,128)(2,1)S(1)}, bf16[1,256,256]{2,1,0:T(8,128)(2,1)S(1)}, u32[]{:S(2)}, u32[]{:S(2)}) collective-permute-start(bf16[1,256,256]{2,1,0:T(8,128)(2,1)S(1)} %slice.11), channel_id=1, source_target_pairs={{0,16},{16,0},{1,17},{17,1},{2,18},{18,2},{3,19},{19,3},{4,20},{20... | collective-permute-start | bytes 393224 | tf_op jit(solution)/shard_map/ppermute | solution.py:267
  53.6 1.7 %collective-permute-start.17 = (bf16[2,256,256]{2,1,0:T(8,128)(2,1)S(1)}, bf16[2,256,256]{2,1,0:T(8,128)(2,1)S(1)}, u32[]{:S(2)}, u32[]{:S(2)}) collective-permute-start(bf16[2,256,256]{2,1,0:T(8,128)(2,1)S(1)} %collective-permute-done.15.refs_2_), channel_id=1, source_target_pairs={{0,1},{1,0},{2,3},{3,2},{4,5},{5,4},{6,7},{7,6},{8,9},{9,8},{10,11... | collective-permute-start | bytes 786440 | tf_op jit(solution)/shard_map/ppermute | solution.py:267
  53.9 1.4 %collective-permute-start.18 = (bf16[1,256,256]{2,1,0:T(8,128)(2,1)S(1)}, bf16[1,256,256]{2,1,0:T(8,128)(2,1)S(1)}, u32[]{:S(2)}, u32[]{:S(2)}) collective-permute-start(bf16[1,256,256]{2,1,0:T(8,128)(2,1)S(1)} %collective-permute-done.16.refs_4_), channel_id=1, source_target_pairs={{0,1},{1,0},{2,3},{3,2},{4,5},{5,4},{6,7},{7,6},{8,9},{9,8},{10,11... | collective-permute-start | bytes 393224 | tf_op jit(solution)/shard_map/ppermute | solution.py:267
  58.7 15.1 %collective-permute-start.19 = (bf16[4,256,256]{2,1,0:T(8,128)(2,1)S(1)}, bf16[4,256,256]{2,1,0:T(8,128)(2,1)S(1)}, u32[]{:S(2)}, u32[]{:S(2)}) collective-permute-start(bf16[4,256,256]{2,1,0:T(8,128)(2,1)S(1)} %get-tuple-element.67), channel_id=1, source_target_pairs={{0,32},{32,0},{1,33},{33,1},{2,34},{34,2},{3,35},{35,3},{4,36},{36... | collective-permute-start | bytes 1572872 | tf_op jit(solution)/shard_map/ppermute | solution.py:267
  74.5 16.7 %all-to-all-start.1 = ((bf16[16,16,256]{2,1,0:T(8,128)(2,1)}), bf16[16,16,256]{2,1,0:T(8,128)(2,1)S(1)}, u32[]{:S(2)}, u32[]{:S(2)}) async-start(bf16[16,16,256]{2,1,0:T(8,128)(2,1)} %shard_map.134), calls=%async_computation.1 | async-start | bytes 262144 | tf_op jit(solution)/shard_map/all_to_all | solution.py:499
  83.0 14.2 %collective-permute-start.20 = (bf16[256,256]{1,0:T(8,128)(2,1)S(1)}, bf16[256,256]{1,0:T(8,128)(2,1)S(1)}, u32[]{:S(2)}, u32[]{:S(2)}) collective-permute-start(bf16[256,256]{1,0:T(8,128)(2,1)S(1)} %get-tuple-element.70), channel_id=1, source_target_pairs={{0,64},{64,128},{128,192},{192,0},{1,65},{65,129},{129,193},{193,1... | collective-permute-start | bytes 393224 | tf_op jit(solution)/shard_map/ppermute | solution.py:267
  83.3 14.0 %collective-permute-start.21 = (bf16[256,256]{1,0:T(8,128)(2,1)S(1)}, bf16[256,256]{1,0:T(8,128)(2,1)S(1)}, u32[]{:S(2)}, u32[]{:S(2)}) collective-permute-start(bf16[256,256]{1,0:T(8,128)(2,1)S(1)} %get-tuple-element.71), channel_id=1, source_target_pairs={{0,128},{64,192},{128,0},{192,64},{1,129},{65,193},{129,1},{193,65... | collective-permute-start | bytes 393224 | tf_op jit(solution)/shard_map/ppermute | solution.py:267
  85.2 12.0 %collective-permute-start.22 = (bf16[256,256]{1,0:T(8,128)(2,1)S(1)}, bf16[256,256]{1,0:T(8,128)(2,1)S(1)}, u32[]{:S(2)}, u32[]{:S(2)}) collective-permute-start(bf16[256,256]{1,0:T(8,128)(2,1)S(1)} %get-tuple-element.72), channel_id=1, source_target_pairs={{0,192},{64,0},{128,64},{192,128},{1,193},{65,1},{129,65},{193,129... | collective-permute-start | bytes 393224 | tf_op jit(solution)/shard_map/ppermute | solution.py:267
  92.0 12.4 %all-to-all-start.2 = ((f32[16,16,256]{2,1,0:T(8,128)}), f32[16,16,256]{2,1,0:T(8,128)S(1)}, u32[]{:S(2)}, u32[]{:S(2)}) async-start(f32[16,16,256]{2,1,0:T(8,128)} %shard_map.135), calls=%async_computation.2 | async-start | bytes 524288 | tf_op jit(solution)/shard_map/all_to_all | solution.py:510
  (7 other events, 87.4 us)

commit v5 on v4

--- a/solution.py
+++ b/solution.py
@@ -218,19 +218,17 @@
         owner = at * 2 + (xl ^ flip)
         sums = jnp.concatenate([total[owner * 2], total[owner * 2 + 1]], axis=1)
         high = sums.astype(BF16)
-        low = (sums - high.astype(F32)).astype(BF16)
         if flip:
             give_ref[at] = high
         else:
             keep_ref[at] = sums
-        for part in (high, low):
-            local = local + lax.dot_general(
-                feat_ref[flip],
-                part,
-                (((1,), (1,)), ((), ())),
-                preferred_element_type=F32,
-            )
-    local_ref[...] = local.reshape(local_ref.shape)
+        local = local + lax.dot_general(
+            feat_ref[flip],
+            high,
+            (((1,), (1,)), ((), ())),
+            preferred_element_type=F32,
+        )
+    local_ref[...] = local.astype(BF16).reshape(local_ref.shape)
 
 
 def half_kernel(where_ref, keep_ref, got_ref, own_ref, *out_refs):
@@ -453,7 +451,7 @@
         out_shape=(
             jax.ShapeDtypeStruct((reach, width, nodes), F32),
             jax.ShapeDtypeStruct((reach, width, nodes), BF16),
-            jax.ShapeDtypeStruct((n_near, part_rows, width), F32),
+            jax.ShapeDtypeStruct((n_near, part_rows, width), BF16),
         ),
         in_specs=[SMEM] * 4 + [VMEM] * (len(blocks) + len(around) + 6),
         out_specs=(VMEM, VMEM, VMEM),

time: 106 us -> 104 us (0.981)
  Pallas kernels: 16.6 us -> 12.4 us
  waiting for transfers between devices: 26.3 us -> 29.1 us
  starting transfers between devices: 43.3 us -> 44.8 us
  blocking collectives: 15 us -> 13.9 us
    pallas_call x2, Pallas kernels: 4.82 us -> 2 us  [early(): pl.pallas_call(functools.partial(early_kernel, stage, places), out_shape=...]
    ppermute x18, waiting for transfers between devices: 12.9 us -> 15.7 us  [shift(): lax.ppermute(block, axis, [(i, (i + step) % size) for i in range(size)])]
    pallas_call x1, Pallas kernels: 3.42 us -> 2 us  [shards(): pl.pallas_call(functools.partial(last_kernel, places, spots), out_shape=(...]
    all_to_all x1, blocking collectives: 15 us -> 13.9 us  [shards(): slices = lax.all_to_all(local, NEAR, 0, 0, tiled=True)]
    ppermute x18, starting transfers between devices: 16.9 us -> 18 us  [shift(): lax.ppermute(block, axis, [(i, (i + step) % size) for i in range(size)])]
  transfers between devices with their start and end apart: 25 -> 25, of which waited for: 9 -> 9; matrix products, arithmetic and copies ran while one was open for 0% -> 0% of each run, Pallas kernels for 11% -> 8%
where the time goes in v5:
time: 104 us
  starting transfers between devices  44.8 us (43%)
  waiting for transfers between devices  29.1 us (28%)
  blocking collectives  13.9 us (13%)
  Pallas kernels  12.4 us (12%)
  between operations  2.15 us (2%)
  local copies, waits for them, and re-layouts  1.77 us (2%)
    ppermute x18, starting transfers between devices, shift(): lax.ppermute(block, axis, [(i, (i + step) % size) for i in range(size)])  18 us
    ppermute x18, waiting for transfers between devices, shift(): lax.ppermute(block, axis, [(i, (i + step) % size) for i in range(size)])  15.7 us
    all_to_all x1, blocking collectives, shards(): slices = lax.all_to_all(local, NEAR, 0, 0, tiled=True)  13.9 us
    ppermute x5, starting transfers between devices, onward(): return lax.ppermute(block, ('z', 'c'), pairs)  13.4 us
    all_to_all x1, starting transfers between devices, shards(): slices = lax.all_to_all(spread(slices, n_far, BF16), FAR, 0, 0, tiled=True)  7.46 us
    all_to_all x1, waiting for transfers between devices, shards(): slices = lax.all_to_all(spread(slices, n_near, F32), NEAR, 0, 0, tiled=True)  6.26 us
    all_to_all x1, starting transfers between devices, shards(): slices = lax.all_to_all(spread(slices, n_near, F32), NEAR, 0, 0, tiled=True)  5.96 us
    all_to_all x1, waiting for transfers between devices, shards(): slices = lax.all_to_all(spread(slices, n_far, BF16), FAR, 0, 0, tiled=True)  5.18 us
  transfers between devices with their start and end apart: 25, of which 9 were waited for; matrix products, arithmetic and copies ran while one was open for 0% of the time, Pallas kernels for 8%

profile of v5, /device:TPU:1, one launch (start us, length us, event | category | flops | bytes accessed | tf_op | source)
XLA Modules:
  0.0 104.1 jit_solution(11669760873742133363)
XLA Ops:
  1.7 3.3 %collective-permute-start = (bf16[256,256]{1,0:T(8,128)(2,1)S(1)}, bf16[256,256]{1,0:T(8,128)(2,1)S(1)}, u32[]{:S(2)}, u32[]{:S(2)}) collective-permute-start(bf16[256,256]{1,0:T(8,128)(2,1)S(1)} %shard_map.122.refs_0_), channel_id=1, source_target_pairs={{0,1},{1,0},{2,3},{3,2},{4,5},{5,4},{6,7},{7,6},{8,9},{9,8},{10,11... | collective-permute-start | bytes 393224 | tf_op jit(solution)/shard_map/ppermute | solution.py:265
  6.1 3.9 %collective-permute-start.1 = (bf16[2,256,256]{2,1,0:T(8,128)(2,1)S(1)}, bf16[2,256,256]{2,1,0:T(8,128)(2,1)S(1)}, u32[]{:S(2)}, u32[]{:S(2)}) collective-permute-start(bf16[2,256,256]{2,1,0:T(8,128)(2,1)S(1)} %shard_map.123.refs_0_), channel_id=1, source_target_pairs={{0,2},{1,15},{2,4},{3,1},{4,6},{5,3},{6,8},{7,5},{8,10},{9,7},{10,... | collective-permute-start | bytes 786440 | tf_op jit(solution)/shard_map/ppermute | solution.py:286
  11.0 1.3 %collective-permute-start.2 = (bf16[256,256]{1,0:T(8,128)(2,1)S(1)}, bf16[256,256]{1,0:T(8,128)(2,1)S(1)}, u32[]{:S(2)}, u32[]{:S(2)}) collective-permute-start(bf16[256,256]{1,0:T(8,128)(2,1)S(1)} %shard_map.124.refs_0_), channel_id=1, source_target_pairs={{0,32},{32,0},{1,33},{33,1},{2,34},{34,2},{3,35},{35,3},{4,36},{36... | collective-permute-start | bytes 393224 | tf_op jit(solution)/shard_map/ppermute | solution.py:265
  12.3 2.5 %collective-permute-start.4 = (bf16[256,256]{1,0:T(8,128)(2,1)S(1)}, bf16[256,256]{1,0:T(8,128)(2,1)S(1)}, u32[]{:S(2)}, u32[]{:S(2)}) collective-permute-start(bf16[256,256]{1,0:T(8,128)(2,1)S(1)} %shard_map.122.refs_0_), channel_id=1, source_target_pairs={{0,16},{16,0},{1,17},{17,1},{2,18},{18,2},{3,19},{19,3},{4,20},{20... | collective-permute-start | bytes 393224 | tf_op jit(solution)/shard_map/ppermute | solution.py:265
  14.7 1.2 %collective-permute-done.2.refs_1_ = bf16[256,256]{1,0:T(8,128)(2,1)S(1)} collective-permute-done((bf16[256,256]{1,0:T(8,128)(2,1)S(1)}, bf16[256,256]{1,0:T(8,128)(2,1)S(1)}, u32[]{:S(2)}, u32[]{:S(2)}) %collective-permute-start.2) | collective-permute-done | bytes 131104 | tf_op jit(solution)/shard_map/ppermute | solution.py:265
  16.0 1.3 %collective-permute-start.3 = (bf16[2,256,256]{2,1,0:T(8,128)(2,1)S(1)}, bf16[2,256,256]{2,1,0:T(8,128)(2,1)S(1)}, u32[]{:S(2)}, u32[]{:S(2)}) collective-permute-start(bf16[2,256,256]{2,1,0:T(8,128)(2,1)S(1)} %collective-permute-done.1.refs_1_), channel_id=1, source_target_pairs={{0,2},{1,15},{2,4},{3,1},{4,6},{5,3},{6,8},{7,5},{8,10},{9,7},{10,... | collective-permute-start | bytes 786440 | tf_op jit(solution)/shard_map/ppermute | solution.py:286
  17.2 1.3 %collective-permute-done.4.refs_0_ = bf16[256,256]{1,0:T(8,128)(2,1)S(1)} collective-permute-done((bf16[256,256]{1,0:T(8,128)(2,1)S(1)}, bf16[256,256]{1,0:T(8,128)(2,1)S(1)}, u32[]{:S(2)}, u32[]{:S(2)}) %collective-permute-start.4) | collective-permute-done | bytes 131104 | tf_op jit(solution)/shard_map/ppermute | solution.py:265
  19.9 1.4 %collective-permute-start.7 = (bf16[2,256,256]{2,1,0:T(8,128)(2,1)S(1)}, bf16[2,256,256]{2,1,0:T(8,128)(2,1)S(1)}, u32[]{:S(2)}, u32[]{:S(2)}) collective-permute-start(bf16[2,256,256]{2,1,0:T(8,128)(2,1)S(1)} %shard_map.127.refs_6_.refs_7_), channel_id=1, source_target_pairs={{0,64},{64,128},{128,192},{192,0},{1,65},{65,129},{129,193},{193,1... | collective-permute-start | bytes 786440 | tf_op jit(solution)/shard_map/ppermute | solution.py:265
  21.3 1.5 %collective-permute-start.8 = (bf16[2,256,256]{2,1,0:T(8,128)(2,1)S(1)}, bf16[2,256,256]{2,1,0:T(8,128)(2,1)S(1)}, u32[]{:S(2)}, u32[]{:S(2)}) collective-permute-start(bf16[2,256,256]{2,1,0:T(8,128)(2,1)S(1)} %shard_map.127.refs_6_.refs_7_), channel_id=1, source_target_pairs={{0,192},{64,0},{128,64},{192,128},{1,193},{65,1},{129,65},{193,129... | collective-permute-start | bytes 786440 | tf_op jit(solution)/shard_map/ppermute | solution.py:265
  23.8 3.9 %collective-permute-start.6 = (bf16[4,256,256]{2,1,0:T(8,128)(2,1)S(1)}, bf16[4,256,256]{2,1,0:T(8,128)(2,1)S(1)}, u32[]{:S(2)}, u32[]{:S(2)}) collective-permute-start(bf16[4,256,256]{2,1,0:T(8,128)(2,1)S(1)} %shard_map.126), channel_id=1, source_target_pairs={{0,2},{1,15},{2,4},{3,1},{4,6},{5,3},{6,8},{7,5},{8,10},{9,7},{10,... | collective-permute-start | bytes 1572872 | tf_op jit(solution)/shard_map/ppermute | solution.py:286
  27.7 4.1 %shard_map.128 = (f32[64,128,128]{2,1,0:T(8,128)S(1)}, f32[64,128,128]{2,1,0:T(8,128)S(1)}, f32[16,1,128]{2,1,0:T(1,128)S(1)}, f32[16,1,128]{2,1,0:T(1,128)S(1)}, s32[14]{0:T(128)S(1)}) custom-call(s32[9]{0:T(128)S(1)} %stack.31.where_ref, s32[1,1]{1,0:T(1,128)S(6)} %copy.15.count_ref, f32[1]{0:T(128)S(6)} %copy.14.decay_ref, s32[1,176]{1,0:T(1,128)} %rows_ref.5, ...), custom_call_target="tpu_custom_call" | custom-call | flops 6000000000 | tf_op jit(solution)/shard_map/pallas_call | solution.py:378
  31.9 2.0 %collective-permute-done.6.refs_5_.refs_1_ = bf16[4,256,256]{2,1,0:T(8,128)(2,1)S(1)} collective-permute-done((bf16[4,256,256]{2,1,0:T(8,128)(2,1)S(1)}, bf16[4,256,256]{2,1,0:T(8,128)(2,1)S(1)}, u32[]{:S(2)}, u32[]{:S(2)}) %collective-permute-start.6) | collective-permute-done | bytes 524320 | tf_op jit(solution)/shard_map/ppermute | solution.py:286
  33.8 1.7 %collective-permute-start.13 = (bf16[4,256,256]{2,1,0:T(8,128)(2,1)S(1)}, bf16[4,256,256]{2,1,0:T(8,128)(2,1)S(1)}, u32[]{:S(2)}, u32[]{:S(2)}) collective-permute-start(bf16[4,256,256]{2,1,0:T(8,128)(2,1)S(1)} %collective-permute-done.6.refs_5_.refs_1_), channel_id=1, source_target_pairs={{0,1},{1,0},{2,3},{3,2},{4,5},{5,4},{6,7},{7,6},{8,9},{9,8},{10,11... | collective-permute-start | bytes 1572872 | tf_op jit(solution)/shard_map/ppermute | solution.py:265
  35.6 1.8 %collective-permute-start.11 = (bf16[3,256,256]{2,1,0:T(8,128)(2,1)S(1)}, bf16[3,256,256]{2,1,0:T(8,128)(2,1)S(1)}, u32[]{:S(2)}, u32[]{:S(2)}) collective-permute-start(bf16[3,256,256]{2,1,0:T(8,128)(2,1)S(1)} %slice.9), channel_id=1, source_target_pairs={{0,2},{1,15},{2,4},{3,1},{4,6},{5,3},{6,8},{7,5},{8,10},{9,7},{10,... | collective-permute-start | bytes 1179656 | tf_op jit(solution)/shard_map/ppermute | solution.py:286
  38.6 7.1 %collective-permute-done.12.refs_12_.refs_13_ = bf16[2,256,256]{2,1,0:T(8,128)(2,1)S(1)} collective-permute-done((bf16[2,256,256]{2,1,0:T(8,128)(2,1)S(1)}, bf16[2,256,256]{2,1,0:T(8,128)(2,1)S(1)}, u32[]{:S(2)}, u32[]{:S(2)}) %collective-permute-start.12) | collective-permute-done | bytes 262176 | tf_op jit(solution)/shard_map/ppermute | solution.py:265
  45.7 2.5 %collective-permute-start.15 = (bf16[2,256,256]{2,1,0:T(8,128)(2,1)S(1)}, bf16[2,256,256]{2,1,0:T(8,128)(2,1)S(1)}, u32[]{:S(2)}, u32[]{:S(2)}) collective-permute-start(bf16[2,256,256]{2,1,0:T(8,128)(2,1)S(1)} %slice.10), channel_id=1, source_target_pairs={{0,2},{1,15},{2,4},{3,1},{4,6},{5,3},{6,8},{7,5},{8,10},{9,7},{10,... | collective-permute-start | bytes 786440 | tf_op jit(solution)/shard_map/ppermute | solution.py:286
  49.7 3.9 %collective-permute-done.16.refs_4_ = bf16[1,256,256]{2,1,0:T(8,128)(2,1)S(1)} collective-permute-done((bf16[1,256,256]{2,1,0:T(8,128)(2,1)S(1)}, bf16[1,256,256]{2,1,0:T(8,128)(2,1)S(1)}, u32[]{:S(2)}, u32[]{:S(2)}) %collective-permute-start.16) | collective-permute-done | bytes 131104 | tf_op jit(solution)/shard_map/ppermute | solution.py:265
  55.3 2.0 %shard_map.131 = (f32[4,256,256]{2,1,0:T(8,128)S(1)}, bf16[4,256,256]{2,1,0:T(8,128)(2,1)S(1)}, bf16[16,16,256]{2,1,0:T(8,128)(2,1)S(1)}) custom-call(s32[9]{0:T(128)S(1)} %stack.31.where_ref, s32[14]{0:T(128)S(1)} %get-tuple-element.49.ends_ref, s32[1,176]{1,0:T(1,128)S(1)} %copy-done.1, s32[1,176]{1,0:T(1,128)S(1)} %copy-done.2, ...), custom_call_target="tpu_custom_call" | custom-call | flops 3000000000 | tf_op jit(solution)/shard_map/pallas_call | solution.py:449
  58.4 13.9 %all_to_all.15.in_ref = bf16[16,16,256]{2,1,0:T(8,128)(2,1)S(1)} all-to-all(bf16[16,16,256]{2,1,0:T(8,128)(2,1)S(1)} %get-tuple-element.66), channel_id=1, replica_groups=mesh['y'=4,'xl'=2,'xh'=2,'z'=8,'c'=2] {'y','xl','c'}, dimensions={0} | all-to-all | bytes 262144 | tf_op jit(solution)/shard_map/all_to_all | solution.py:485
  73.1 7.5 %all-to-all-start.1 = ((bf16[16,16,256]{2,1,0:T(8,128)(2,1)}), bf16[16,16,256]{2,1,0:T(8,128)(2,1)S(1)}, u32[]{:S(2)}, u32[]{:S(2)}) async-start(bf16[16,16,256]{2,1,0:T(8,128)(2,1)} %shard_map.134), calls=%async_computation.1 | async-start | bytes 262144 | tf_op jit(solution)/shard_map/all_to_all | solution.py:497
  81.3 2.3 %collective-permute-start.21 = (bf16[256,256]{1,0:T(8,128)(2,1)S(1)}, bf16[256,256]{1,0:T(8,128)(2,1)S(1)}, u32[]{:S(2)}, u32[]{:S(2)}) collective-permute-start(bf16[256,256]{1,0:T(8,128)(2,1)S(1)} %get-tuple-element.71), channel_id=1, source_target_pairs={{0,128},{64,192},{128,0},{192,64},{1,129},{65,193},{129,1},{193,65... | collective-permute-start | bytes 393224 | tf_op jit(solution)/shard_map/ppermute | solution.py:265
  84.3 5.2 %all-to-all-done.1.in_ref = bf16[16,16,256]{2,1,0:T(8,128)(2,1)S(1)} async-done(((bf16[16,16,256]{2,1,0:T(8,128)(2,1)}), bf16[16,16,256]{2,1,0:T(8,128)(2,1)S(1)}, u32[]{:S(2)}, u32[]{:S(2)}) %all-to-all-start.1) | async-done | bytes 131104 | tf_op jit(solution)/shard_map/all_to_all | solution.py:497
  90.2 6.0 %all-to-all-start.2 = ((f32[16,16,256]{2,1,0:T(8,128)}), f32[16,16,256]{2,1,0:T(8,128)S(1)}, u32[]{:S(2)}, u32[]{:S(2)}) async-start(f32[16,16,256]{2,1,0:T(8,128)} %shard_map.135), calls=%async_computation.2 | async-start | bytes 524288 | tf_op jit(solution)/shard_map/all_to_all | solution.py:508
  97.1 6.3 %all-to-all-done.2 = f32[16,16,256]{2,1,0:T(8,128)S(1)} async-done(((f32[16,16,256]{2,1,0:T(8,128)}), f32[16,16,256]{2,1,0:T(8,128)S(1)}, u32[]{:S(2)}, u32[]{:S(2)}) %all-to-all-start.2) | async-done | bytes 262176 | tf_op jit(solution)/shard_map/all_to_all | solution.py:508
  (59 shorter events, 14.3 us)
Async XLA Ops:
  1.7 4.3 %collective-permute-start = (bf16[256,256]{1,0:T(8,128)(2,1)S(1)}, bf16[256,256]{1,0:T(8,128)(2,1)S(1)}, u32[]{:S(2)}, u32[]{:S(2)}) collective-permute-start(bf16[256,256]{1,0:T(8,128)(2,1)S(1)} %shard_map.122.refs_0_), channel_id=1, source_target_pairs={{0,1},{1,0},{2,3},{3,2},{4,5},{5,4},{6,7},{7,6},{8,9},{9,8},{10,11... | collective-permute-start | bytes 393224 | tf_op jit(solution)/shard_map/ppermute | solution.py:265
  6.1 9.9 %collective-permute-start.1 = (bf16[2,256,256]{2,1,0:T(8,128)(2,1)S(1)}, bf16[2,256,256]{2,1,0:T(8,128)(2,1)S(1)}, u32[]{:S(2)}, u32[]{:S(2)}) collective-permute-start(bf16[2,256,256]{2,1,0:T(8,128)(2,1)S(1)} %shard_map.123.refs_0_), channel_id=1, source_target_pairs={{0,2},{1,15},{2,4},{3,1},{4,6},{5,3},{6,8},{7,5},{8,10},{9,7},{10,... | collective-permute-start | bytes 786440 | tf_op jit(solution)/shard_map/ppermute | solution.py:286
  11.0 5.0 %collective-permute-start.2 = (bf16[256,256]{1,0:T(8,128)(2,1)S(1)}, bf16[256,256]{1,0:T(8,128)(2,1)S(1)}, u32[]{:S(2)}, u32[]{:S(2)}) collective-permute-start(bf16[256,256]{1,0:T(8,128)(2,1)S(1)} %shard_map.124.refs_0_), channel_id=1, source_target_pairs={{0,32},{32,0},{1,33},{33,1},{2,34},{34,2},{3,35},{35,3},{4,36},{36... | collective-permute-start | bytes 393224 | tf_op jit(solution)/shard_map/ppermute | solution.py:265
  12.3 6.2 %collective-permute-start.4 = (bf16[256,256]{1,0:T(8,128)(2,1)S(1)}, bf16[256,256]{1,0:T(8,128)(2,1)S(1)}, u32[]{:S(2)}, u32[]{:S(2)}) collective-permute-start(bf16[256,256]{1,0:T(8,128)(2,1)S(1)} %shard_map.122.refs_0_), channel_id=1, source_target_pairs={{0,16},{16,0},{1,17},{17,1},{2,18},{18,2},{3,19},{19,3},{4,20},{20... | collective-permute-start | bytes 393224 | tf_op jit(solution)/shard_map/ppermute | solution.py:265
  16.0 7.8 %collective-permute-start.3 = (bf16[2,256,256]{2,1,0:T(8,128)(2,1)S(1)}, bf16[2,256,256]{2,1,0:T(8,128)(2,1)S(1)}, u32[]{:S(2)}, u32[]{:S(2)}) collective-permute-start(bf16[2,256,256]{2,1,0:T(8,128)(2,1)S(1)} %collective-permute-done.1.refs_1_), channel_id=1, source_target_pairs={{0,2},{1,15},{2,4},{3,1},{4,6},{5,3},{6,8},{7,5},{8,10},{9,7},{10,... | collective-permute-start | bytes 786440 | tf_op jit(solution)/shard_map/ppermute | solution.py:286
  19.9 11.9 %collective-permute-start.7 = (bf16[2,256,256]{2,1,0:T(8,128)(2,1)S(1)}, bf16[2,256,256]{2,1,0:T(8,128)(2,1)S(1)}, u32[]{:S(2)}, u32[]{:S(2)}) collective-permute-start(bf16[2,256,256]{2,1,0:T(8,128)(2,1)S(1)} %shard_map.127.refs_6_.refs_7_), channel_id=1, source_target_pairs={{0,64},{64,128},{128,192},{192,0},{1,65},{65,129},{129,193},{193,1... | collective-permute-start | bytes 786440 | tf_op jit(solution)/shard_map/ppermute | solution.py:265
  21.3 10.5 %collective-permute-start.8 = (bf16[2,256,256]{2,1,0:T(8,128)(2,1)S(1)}, bf16[2,256,256]{2,1,0:T(8,128)(2,1)S(1)}, u32[]{:S(2)}, u32[]{:S(2)}) collective-permute-start(bf16[2,256,256]{2,1,0:T(8,128)(2,1)S(1)} %shard_map.127.refs_6_.refs_7_), channel_id=1, source_target_pairs={{0,192},{64,0},{128,64},{192,128},{1,193},{65,1},{129,65},{193,129... | collective-permute-start | bytes 786440 | tf_op jit(solution)/shard_map/ppermute | solution.py:265
  22.9 9.0 %collective-permute-start.9 = (bf16[2,256,256]{2,1,0:T(8,128)(2,1)S(1)}, bf16[2,256,256]{2,1,0:T(8,128)(2,1)S(1)}, u32[]{:S(2)}, u32[]{:S(2)}) collective-permute-start(bf16[2,256,256]{2,1,0:T(8,128)(2,1)S(1)} %collective-permute-done.1.refs_1_), channel_id=1, source_target_pairs={{0,1},{1,0},{2,3},{3,2},{4,5},{5,4},{6,7},{7,6},{8,9},{9,8},{10,11... | collective-permute-start | bytes 786440 | tf_op jit(solution)/shard_map/ppermute | solution.py:265
  23.8 8.1 %collective-permute-start.10 = (bf16[2,256,256]{2,1,0:T(8,128)(2,1)S(1)}, bf16[2,256,256]{2,1,0:T(8,128)(2,1)S(1)}, u32[]{:S(2)}, u32[]{:S(2)}) collective-permute-start(bf16[2,256,256]{2,1,0:T(8,128)(2,1)S(1)} %collective-permute-done.3.refs_1_.refs_2_), channel_id=1, source_target_pairs={{0,1},{1,0},{2,3},{3,2},{4,5},{5,4},{6,7},{7,6},{8,9},{9,8},{10,11... | collective-permute-start | bytes 786440 | tf_op jit(solution)/shard_map/ppermute | solution.py:265
  23.8 10.0 %collective-permute-start.6 = (bf16[4,256,256]{2,1,0:T(8,128)(2,1)S(1)}, bf16[4,256,256]{2,1,0:T(8,128)(2,1)S(1)}, u32[]{:S(2)}, u32[]{:S(2)}) collective-permute-start(bf16[4,256,256]{2,1,0:T(8,128)(2,1)S(1)} %shard_map.126), channel_id=1, source_target_pairs={{0,2},{1,15},{2,4},{3,1},{4,6},{5,3},{6,8},{7,5},{8,10},{9,7},{10,... | collective-permute-start | bytes 1572872 | tf_op jit(solution)/shard_map/ppermute | solution.py:286
  33.8 3.7 %collective-permute-start.13 = (bf16[4,256,256]{2,1,0:T(8,128)(2,1)S(1)}, bf16[4,256,256]{2,1,0:T(8,128)(2,1)S(1)}, u32[]{:S(2)}, u32[]{:S(2)}) collective-permute-start(bf16[4,256,256]{2,1,0:T(8,128)(2,1)S(1)} %collective-permute-done.6.refs_5_.refs_1_), channel_id=1, source_target_pairs={{0,1},{1,0},{2,3},{3,2},{4,5},{5,4},{6,7},{7,6},{8,9},{9,8},{10,11... | collective-permute-start | bytes 1572872 | tf_op jit(solution)/shard_map/ppermute | solution.py:265
  35.6 10.1 %collective-permute-start.11 = (bf16[3,256,256]{2,1,0:T(8,128)(2,1)S(1)}, bf16[3,256,256]{2,1,0:T(8,128)(2,1)S(1)}, u32[]{:S(2)}, u32[]{:S(2)}) collective-permute-start(bf16[3,256,256]{2,1,0:T(8,128)(2,1)S(1)} %slice.9), channel_id=1, source_target_pairs={{0,2},{1,15},{2,4},{3,1},{4,6},{5,3},{6,8},{7,5},{8,10},{9,7},{10,... | collective-permute-start | bytes 1179656 | tf_op jit(solution)/shard_map/ppermute | solution.py:286
  37.4 8.2 %collective-permute-start.12 = (bf16[2,256,256]{2,1,0:T(8,128)(2,1)S(1)}, bf16[2,256,256]{2,1,0:T(8,128)(2,1)S(1)}, u32[]{:S(2)}, u32[]{:S(2)}) collective-permute-start(bf16[2,256,256]{2,1,0:T(8,128)(2,1)S(1)} %collective-permute-done.7.refs_8_.refs_9_), channel_id=1, source_target_pairs={{0,64},{64,128},{128,192},{192,0},{1,65},{65,129},{129,193},{193,1... | collective-permute-start | bytes 786440 | tf_op jit(solution)/shard_map/ppermute | solution.py:265
  45.7 3.1 %collective-permute-start.14 = (bf16[3,256,256]{2,1,0:T(8,128)(2,1)S(1)}, bf16[3,256,256]{2,1,0:T(8,128)(2,1)S(1)}, u32[]{:S(2)}, u32[]{:S(2)}) collective-permute-start(bf16[3,256,256]{2,1,0:T(8,128)(2,1)S(1)} %collective-permute-done.11.refs_3_.refs_0_), channel_id=1, source_target_pairs={{0,1},{1,0},{2,3},{3,2},{4,5},{5,4},{6,7},{7,6},{8,9},{9,8},{10,11... | collective-permute-start | bytes 1179656 | tf_op jit(solution)/shard_map/ppermute | solution.py:265
  45.7 7.9 %collective-permute-start.15 = (bf16[2,256,256]{2,1,0:T(8,128)(2,1)S(1)}, bf16[2,256,256]{2,1,0:T(8,128)(2,1)S(1)}, u32[]{:S(2)}, u32[]{:S(2)}) collective-permute-start(bf16[2,256,256]{2,1,0:T(8,128)(2,1)S(1)} %slice.10), channel_id=1, source_target_pairs={{0,2},{1,15},{2,4},{3,1},{4,6},{5,3},{6,8},{7,5},{8,10},{9,7},{10,... | collective-permute-start | bytes 786440 | tf_op jit(solution)/shard_map/ppermute | solution.py:286
  48.2 5.4 %collective-permute-start.16 = (bf16[1,256,256]{2,1,0:T(8,128)(2,1)S(1)}, bf16[1,256,256]{2,1,0:T(8,128)(2,1)S(1)}, u32[]{:S(2)}, u32[]{:S(2)}) collective-permute-start(bf16[1,256,256]{2,1,0:T(8,128)(2,1)S(1)} %slice.11), channel_id=1, source_target_pairs={{0,16},{16,0},{1,17},{17,1},{2,18},{18,2},{3,19},{19,3},{4,20},{20... | collective-permute-start | bytes 393224 | tf_op jit(solution)/shard_map/ppermute | solution.py:265
  53.6 1.7 %collective-permute-start.17 = (bf16[2,256,256]{2,1,0:T(8,128)(2,1)S(1)}, bf16[2,256,256]{2,1,0:T(8,128)(2,1)S(1)}, u32[]{:S(2)}, u32[]{:S(2)}) collective-permute-start(bf16[2,256,256]{2,1,0:T(8,128)(2,1)S(1)} %collective-permute-done.15.refs_2_), channel_id=1, source_target_pairs={{0,1},{1,0},{2,3},{3,2},{4,5},{5,4},{6,7},{7,6},{8,9},{9,8},{10,11... | collective-permute-start | bytes 786440 | tf_op jit(solution)/shard_map/ppermute | solution.py:265
  53.9 1.4 %collective-permute-start.18 = (bf16[1,256,256]{2,1,0:T(8,128)(2,1)S(1)}, bf16[1,256,256]{2,1,0:T(8,128)(2,1)S(1)}, u32[]{:S(2)}, u32[]{:S(2)}) collective-permute-start(bf16[1,256,256]{2,1,0:T(8,128)(2,1)S(1)} %collective-permute-done.16.refs_4_), channel_id=1, source_target_pairs={{0,1},{1,0},{2,3},{3,2},{4,5},{5,4},{6,7},{7,6},{8,9},{9,8},{10,11... | collective-permute-start | bytes 393224 | tf_op jit(solution)/shard_map/ppermute | solution.py:265
  57.3 15.1 %collective-permute-start.19 = (bf16[4,256,256]{2,1,0:T(8,128)(2,1)S(1)}, bf16[4,256,256]{2,1,0:T(8,128)(2,1)S(1)}, u32[]{:S(2)}, u32[]{:S(2)}) collective-permute-start(bf16[4,256,256]{2,1,0:T(8,128)(2,1)S(1)} %get-tuple-element.67), channel_id=1, source_target_pairs={{0,32},{32,0},{1,33},{33,1},{2,34},{34,2},{3,35},{35,3},{4,36},{36... | collective-permute-start | bytes 1572872 | tf_op jit(solution)/shard_map/ppermute | solution.py:265
  73.1 16.4 %all-to-all-start.1 = ((bf16[16,16,256]{2,1,0:T(8,128)(2,1)}), bf16[16,16,256]{2,1,0:T(8,128)(2,1)S(1)}, u32[]{:S(2)}, u32[]{:S(2)}) async-start(bf16[16,16,256]{2,1,0:T(8,128)(2,1)} %shard_map.134), calls=%async_computation.1 | async-start | bytes 262144 | tf_op jit(solution)/shard_map/all_to_all | solution.py:497
  81.2 15.0 %collective-permute-start.20 = (bf16[256,256]{1,0:T(8,128)(2,1)S(1)}, bf16[256,256]{1,0:T(8,128)(2,1)S(1)}, u32[]{:S(2)}, u32[]{:S(2)}) collective-permute-start(bf16[256,256]{1,0:T(8,128)(2,1)S(1)} %get-tuple-element.70), channel_id=1, source_target_pairs={{0,64},{64,128},{128,192},{192,0},{1,65},{65,129},{129,193},{193,1... | collective-permute-start | bytes 393224 | tf_op jit(solution)/shard_map/ppermute | solution.py:265
  81.3 14.9 %collective-permute-start.21 = (bf16[256,256]{1,0:T(8,128)(2,1)S(1)}, bf16[256,256]{1,0:T(8,128)(2,1)S(1)}, u32[]{:S(2)}, u32[]{:S(2)}) collective-permute-start(bf16[256,256]{1,0:T(8,128)(2,1)S(1)} %get-tuple-element.71), channel_id=1, source_target_pairs={{0,128},{64,192},{128,0},{192,64},{1,129},{65,193},{129,1},{193,65... | collective-permute-start | bytes 393224 | tf_op jit(solution)/shard_map/ppermute | solution.py:265
  83.6 12.7 %collective-permute-start.22 = (bf16[256,256]{1,0:T(8,128)(2,1)S(1)}, bf16[256,256]{1,0:T(8,128)(2,1)S(1)}, u32[]{:S(2)}, u32[]{:S(2)}) collective-permute-start(bf16[256,256]{1,0:T(8,128)(2,1)S(1)} %get-tuple-element.72), channel_id=1, source_target_pairs={{0,192},{64,0},{128,64},{192,128},{1,193},{65,1},{129,65},{193,129... | collective-permute-start | bytes 393224 | tf_op jit(solution)/shard_map/ppermute | solution.py:265
  90.2 13.2 %all-to-all-start.2 = ((f32[16,16,256]{2,1,0:T(8,128)}), f32[16,16,256]{2,1,0:T(8,128)S(1)}, u32[]{:S(2)}, u32[]{:S(2)}) async-start(f32[16,16,256]{2,1,0:T(8,128)} %shard_map.135), calls=%async_computation.2 | async-start | bytes 524288 | tf_op jit(solution)/shard_map/all_to_all | solution.py:508
  (7 other events, 88.0 us)

commit v6 on v5

--- a/solution.py
+++ b/solution.py
@@ -505,8 +505,8 @@
         ),
         compiler_params=TIGHT,
     )(weight, own, *sent)
-    slices = lax.all_to_all(spread(slices, n_near, F32), NEAR, 0, 0, tiled=True)
-    return grad_input, slices.reshape(features.shape[1], width)
+    slices = lax.all_to_all(spread(slices, n_near, BF16), NEAR, 0, 0, tiled=True)
+    return grad_input, slices.reshape(features.shape[1], width).astype(F32)
 
 
 def solution(mesh):

time: 104 us -> 103 us (level)
  starting transfers between devices: 44.8 us -> 43.1 us
  blocking collectives: 13.9 us -> 15.2 us
    ppermute x18, starting transfers between devices: 18 us -> 16.6 us  [shift(): lax.ppermute(block, axis, [(i, (i + step) % size) for i in range(size)])]
    all_to_all x1, blocking collectives: 13.9 us -> 15.2 us  [shards(): slices = lax.all_to_all(local, NEAR, 0, 0, tiled=True)]
where the time goes in v6:
time: 103 us
  starting transfers between devices  43.1 us (42%)
  waiting for transfers between devices  28.5 us (28%)
  blocking collectives  15.2 us (15%)
  Pallas kernels  12.3 us (12%)
  between operations  2.17 us (2%)
  local copies, waits for them, and re-layouts  1.07 us (1%)
    ppermute x18, starting transfers between devices, shift(): lax.ppermute(block, axis, [(i, (i + step) % size) for i in range(size)])  16.6 us
    ppermute x18, waiting for transfers between devices, shift(): lax.ppermute(block, axis, [(i, (i + step) % size) for i in range(size)])  15.7 us
    all_to_all x1, blocking collectives, shards(): slices = lax.all_to_all(local, NEAR, 0, 0, tiled=True)  15.2 us
    ppermute x5, starting transfers between devices, onward(): return lax.ppermute(block, ('z', 'c'), pairs)  13.4 us
    all_to_all x1, starting transfers between devices, shards(): slices = lax.all_to_all(spread(slices, n_far, BF16), FAR, 0, 0, tiled=True)  7.82 us
    all_to_all x1, waiting for transfers between devices, shards(): slices = lax.all_to_all(spread(slices, n_far, BF16), FAR, 0, 0, tiled=True)  5.54 us
    all_to_all x1, starting transfers between devices, shards(): lax.all_to_all(spread(slices, n_near, BF16), NEAR, 0, 0, tiled=True)  5.29 us
    all_to_all x1, waiting for transfers between devices, shards(): lax.all_to_all(spread(slices, n_near, BF16), NEAR, 0, 0, tiled=True)  5.26 us
  transfers between devices with their start and end apart: 25, of which 9 were waited for; matrix products, arithmetic and copies ran while one was open for 0% of the time, Pallas kernels for 8%

profile of v6, /device:TPU:1, one launch (start us, length us, event | category | flops | bytes accessed | tf_op | source)
XLA Modules:
  0.0 103.0 jit_solution(3051370966372364624)
XLA Ops:
  1.7 3.3 %collective-permute-start = (bf16[256,256]{1,0:T(8,128)(2,1)S(1)}, bf16[256,256]{1,0:T(8,128)(2,1)S(1)}, u32[]{:S(2)}, u32[]{:S(2)}) collective-permute-start(bf16[256,256]{1,0:T(8,128)(2,1)S(1)} %shard_map.122.refs_0_), channel_id=1, source_target_pairs={{0,1},{1,0},{2,3},{3,2},{4,5},{5,4},{6,7},{7,6},{8,9},{9,8},{10,11... | collective-permute-start | bytes 393224 | tf_op jit(solution)/shard_map/ppermute | solution.py:265
  6.1 3.9 %collective-permute-start.1 = (bf16[2,256,256]{2,1,0:T(8,128)(2,1)S(1)}, bf16[2,256,256]{2,1,0:T(8,128)(2,1)S(1)}, u32[]{:S(2)}, u32[]{:S(2)}) collective-permute-start(bf16[2,256,256]{2,1,0:T(8,128)(2,1)S(1)} %shard_map.123.refs_0_), channel_id=1, source_target_pairs={{0,2},{1,15},{2,4},{3,1},{4,6},{5,3},{6,8},{7,5},{8,10},{9,7},{10,... | collective-permute-start | bytes 786440 | tf_op jit(solution)/shard_map/ppermute | solution.py:286
  11.0 1.3 %collective-permute-start.2 = (bf16[256,256]{1,0:T(8,128)(2,1)S(1)}, bf16[256,256]{1,0:T(8,128)(2,1)S(1)}, u32[]{:S(2)}, u32[]{:S(2)}) collective-permute-start(bf16[256,256]{1,0:T(8,128)(2,1)S(1)} %shard_map.124.refs_0_), channel_id=1, source_target_pairs={{0,32},{32,0},{1,33},{33,1},{2,34},{34,2},{3,35},{35,3},{4,36},{36... | collective-permute-start | bytes 393224 | tf_op jit(solution)/shard_map/ppermute | solution.py:265
  12.3 2.5 %collective-permute-start.4 = (bf16[256,256]{1,0:T(8,128)(2,1)S(1)}, bf16[256,256]{1,0:T(8,128)(2,1)S(1)}, u32[]{:S(2)}, u32[]{:S(2)}) collective-permute-start(bf16[256,256]{1,0:T(8,128)(2,1)S(1)} %shard_map.122.refs_0_), channel_id=1, source_target_pairs={{0,16},{16,0},{1,17},{17,1},{2,18},{18,2},{3,19},{19,3},{4,20},{20... | collective-permute-start | bytes 393224 | tf_op jit(solution)/shard_map/ppermute | solution.py:265
  16.0 1.3 %collective-permute-start.3 = (bf16[2,256,256]{2,1,0:T(8,128)(2,1)S(1)}, bf16[2,256,256]{2,1,0:T(8,128)(2,1)S(1)}, u32[]{:S(2)}, u32[]{:S(2)}) collective-permute-start(bf16[2,256,256]{2,1,0:T(8,128)(2,1)S(1)} %collective-permute-done.1.refs_1_), channel_id=1, source_target_pairs={{0,2},{1,15},{2,4},{3,1},{4,6},{5,3},{6,8},{7,5},{8,10},{9,7},{10,... | collective-permute-start | bytes 786440 | tf_op jit(solution)/shard_map/ppermute | solution.py:286
  17.2 1.3 %collective-permute-done.4.refs_0_ = bf16[256,256]{1,0:T(8,128)(2,1)S(1)} collective-permute-done((bf16[256,256]{1,0:T(8,128)(2,1)S(1)}, bf16[256,256]{1,0:T(8,128)(2,1)S(1)}, u32[]{:S(2)}, u32[]{:S(2)}) %collective-permute-start.4) | collective-permute-done | bytes 131104 | tf_op jit(solution)/shard_map/ppermute | solution.py:265
  19.9 1.4 %collective-permute-start.7 = (bf16[2,256,256]{2,1,0:T(8,128)(2,1)S(1)}, bf16[2,256,256]{2,1,0:T(8,128)(2,1)S(1)}, u32[]{:S(2)}, u32[]{:S(2)}) collective-permute-start(bf16[2,256,256]{2,1,0:T(8,128)(2,1)S(1)} %shard_map.127.refs_6_.refs_7_), channel_id=1, source_target_pairs={{0,64},{64,128},{128,192},{192,0},{1,65},{65,129},{129,193},{193,1... | collective-permute-start | bytes 786440 | tf_op jit(solution)/shard_map/ppermute | solution.py:265
  21.3 1.5 %collective-permute-start.8 = (bf16[2,256,256]{2,1,0:T(8,128)(2,1)S(1)}, bf16[2,256,256]{2,1,0:T(8,128)(2,1)S(1)}, u32[]{:S(2)}, u32[]{:S(2)}) collective-permute-start(bf16[2,256,256]{2,1,0:T(8,128)(2,1)S(1)} %shard_map.127.refs_6_.refs_7_), channel_id=1, source_target_pairs={{0,192},{64,0},{128,64},{192,128},{1,193},{65,1},{129,65},{193,129... | collective-permute-start | bytes 786440 | tf_op jit(solution)/shard_map/ppermute | solution.py:265
  23.8 3.9 %collective-permute-start.6 = (bf16[4,256,256]{2,1,0:T(8,128)(2,1)S(1)}, bf16[4,256,256]{2,1,0:T(8,128)(2,1)S(1)}, u32[]{:S(2)}, u32[]{:S(2)}) collective-permute-start(bf16[4,256,256]{2,1,0:T(8,128)(2,1)S(1)} %shard_map.126), channel_id=1, source_target_pairs={{0,2},{1,15},{2,4},{3,1},{4,6},{5,3},{6,8},{7,5},{8,10},{9,7},{10,... | collective-permute-start | bytes 1572872 | tf_op jit(solution)/shard_map/ppermute | solution.py:286
  27.7 4.1 %shard_map.128 = (f32[64,128,128]{2,1,0:T(8,128)S(1)}, f32[64,128,128]{2,1,0:T(8,128)S(1)}, f32[16,1,128]{2,1,0:T(1,128)S(1)}, f32[16,1,128]{2,1,0:T(1,128)S(1)}, s32[14]{0:T(128)S(1)}) custom-call(s32[9]{0:T(128)S(1)} %stack.31.where_ref, s32[1,1]{1,0:T(1,128)S(6)} %copy.14.count_ref, f32[1]{0:T(128)S(6)} %copy.13.decay_ref, s32[1,176]{1,0:T(1,128)} %rows_ref.5, ...), custom_call_target="tpu_custom_call" | custom-call | flops 6000000000 | tf_op jit(solution)/shard_map/pallas_call | solution.py:378
  31.9 2.0 %collective-permute-done.6.refs_5_.refs_1_ = bf16[4,256,256]{2,1,0:T(8,128)(2,1)S(1)} collective-permute-done((bf16[4,256,256]{2,1,0:T(8,128)(2,1)S(1)}, bf16[4,256,256]{2,1,0:T(8,128)(2,1)S(1)}, u32[]{:S(2)}, u32[]{:S(2)}) %collective-permute-start.6) | collective-permute-done | bytes 524320 | tf_op jit(solution)/shard_map/ppermute | solution.py:286
  33.8 1.7 %collective-permute-start.13 = (bf16[4,256,256]{2,1,0:T(8,128)(2,1)S(1)}, bf16[4,256,256]{2,1,0:T(8,128)(2,1)S(1)}, u32[]{:S(2)}, u32[]{:S(2)}) collective-permute-start(bf16[4,256,256]{2,1,0:T(8,128)(2,1)S(1)} %collective-permute-done.6.refs_5_.refs_1_), channel_id=1, source_target_pairs={{0,1},{1,0},{2,3},{3,2},{4,5},{5,4},{6,7},{7,6},{8,9},{9,8},{10,11... | collective-permute-start | bytes 1572872 | tf_op jit(solution)/shard_map/ppermute | solution.py:265
  35.6 1.8 %collective-permute-start.11 = (bf16[3,256,256]{2,1,0:T(8,128)(2,1)S(1)}, bf16[3,256,256]{2,1,0:T(8,128)(2,1)S(1)}, u32[]{:S(2)}, u32[]{:S(2)}) collective-permute-start(bf16[3,256,256]{2,1,0:T(8,128)(2,1)S(1)} %slice.9), channel_id=1, source_target_pairs={{0,2},{1,15},{2,4},{3,1},{4,6},{5,3},{6,8},{7,5},{8,10},{9,7},{10,... | collective-permute-start | bytes 1179656 | tf_op jit(solution)/shard_map/ppermute | solution.py:286
  38.6 7.1 %collective-permute-done.12.refs_12_.refs_13_ = bf16[2,256,256]{2,1,0:T(8,128)(2,1)S(1)} collective-permute-done((bf16[2,256,256]{2,1,0:T(8,128)(2,1)S(1)}, bf16[2,256,256]{2,1,0:T(8,128)(2,1)S(1)}, u32[]{:S(2)}, u32[]{:S(2)}) %collective-permute-start.12) | collective-permute-done | bytes 262176 | tf_op jit(solution)/shard_map/ppermute | solution.py:265
  45.7 2.5 %collective-permute-start.15 = (bf16[2,256,256]{2,1,0:T(8,128)(2,1)S(1)}, bf16[2,256,256]{2,1,0:T(8,128)(2,1)S(1)}, u32[]{:S(2)}, u32[]{:S(2)}) collective-permute-start(bf16[2,256,256]{2,1,0:T(8,128)(2,1)S(1)} %slice.10), channel_id=1, source_target_pairs={{0,2},{1,15},{2,4},{3,1},{4,6},{5,3},{6,8},{7,5},{8,10},{9,7},{10,... | collective-permute-start | bytes 786440 | tf_op jit(solution)/shard_map/ppermute | solution.py:286
  49.7 3.9 %collective-permute-done.16.refs_4_ = bf16[1,256,256]{2,1,0:T(8,128)(2,1)S(1)} collective-permute-done((bf16[1,256,256]{2,1,0:T(8,128)(2,1)S(1)}, bf16[1,256,256]{2,1,0:T(8,128)(2,1)S(1)}, u32[]{:S(2)}, u32[]{:S(2)}) %collective-permute-start.16) | collective-permute-done | bytes 131104 | tf_op jit(solution)/shard_map/ppermute | solution.py:265
  55.3 2.0 %shard_map.131 = (f32[4,256,256]{2,1,0:T(8,128)S(1)}, bf16[4,256,256]{2,1,0:T(8,128)(2,1)S(1)}, bf16[16,16,256]{2,1,0:T(8,128)(2,1)S(1)}) custom-call(s32[9]{0:T(128)S(1)} %stack.31.where_ref, s32[14]{0:T(128)S(1)} %get-tuple-element.49.ends_ref, s32[1,176]{1,0:T(1,128)S(1)} %copy-done.1, s32[1,176]{1,0:T(1,128)S(1)} %copy-done.2, ...), custom_call_target="tpu_custom_call" | custom-call | flops 3000000000 | tf_op jit(solution)/shard_map/pallas_call | solution.py:449
  57.4 15.2 %all_to_all.15.in_ref = bf16[16,16,256]{2,1,0:T(8,128)(2,1)S(1)} all-to-all(bf16[16,16,256]{2,1,0:T(8,128)(2,1)S(1)} %get-tuple-element.66), channel_id=1, replica_groups=mesh['y'=4,'xl'=2,'xh'=2,'z'=8,'c'=2] {'y','xl','c'}, dimensions={0} | all-to-all | bytes 262144 | tf_op jit(solution)/shard_map/all_to_all | solution.py:485
  73.4 7.8 %all-to-all-start.1 = ((bf16[16,16,256]{2,1,0:T(8,128)(2,1)}), bf16[16,16,256]{2,1,0:T(8,128)(2,1)S(1)}, u32[]{:S(2)}, u32[]{:S(2)}) async-start(bf16[16,16,256]{2,1,0:T(8,128)(2,1)} %shard_map.134), calls=%async_computation.1 | async-start | bytes 262144 | tf_op jit(solution)/shard_map/all_to_all | solution.py:497
  81.9 1.4 %collective-permute-start.21 = (bf16[256,256]{1,0:T(8,128)(2,1)S(1)}, bf16[256,256]{1,0:T(8,128)(2,1)S(1)}, u32[]{:S(2)}, u32[]{:S(2)}) collective-permute-start(bf16[256,256]{1,0:T(8,128)(2,1)S(1)} %get-tuple-element.71), channel_id=1, source_target_pairs={{0,128},{64,192},{128,0},{192,64},{1,129},{65,193},{129,1},{193,65... | collective-permute-start | bytes 393224 | tf_op jit(solution)/shard_map/ppermute | solution.py:265
  83.3 1.3 %collective-permute-start.22 = (bf16[256,256]{1,0:T(8,128)(2,1)S(1)}, bf16[256,256]{1,0:T(8,128)(2,1)S(1)}, u32[]{:S(2)}, u32[]{:S(2)}) collective-permute-start(bf16[256,256]{1,0:T(8,128)(2,1)S(1)} %get-tuple-element.72), channel_id=1, source_target_pairs={{0,192},{64,0},{128,64},{192,128},{1,193},{65,1},{129,65},{193,129... | collective-permute-start | bytes 393224 | tf_op jit(solution)/shard_map/ppermute | solution.py:265
  84.6 5.5 %all-to-all-done.1.in_ref = bf16[16,16,256]{2,1,0:T(8,128)(2,1)S(1)} async-done(((bf16[16,16,256]{2,1,0:T(8,128)(2,1)}), bf16[16,16,256]{2,1,0:T(8,128)(2,1)S(1)}, u32[]{:S(2)}, u32[]{:S(2)}) %all-to-all-start.1) | async-done | bytes 131104 | tf_op jit(solution)/shard_map/all_to_all | solution.py:497
  90.8 5.3 %all-to-all-start.2 = ((bf16[16,16,256]{2,1,0:T(8,128)(2,1)}), bf16[16,16,256]{2,1,0:T(8,128)(2,1)S(1)}, u32[]{:S(2)}, u32[]{:S(2)}) async-start(bf16[16,16,256]{2,1,0:T(8,128)(2,1)} %shard_map.135), calls=%async_computation.2 | async-start | bytes 262144 | tf_op jit(solution)/shard_map/all_to_all | solution.py:508
  97.1 5.3 %all-to-all-done.2 = bf16[16,16,256]{2,1,0:T(8,128)(2,1)S(1)} async-done(((bf16[16,16,256]{2,1,0:T(8,128)(2,1)}), bf16[16,16,256]{2,1,0:T(8,128)(2,1)S(1)}, u32[]{:S(2)}, u32[]{:S(2)}) %all-to-all-start.2) | async-done | bytes 131104 | tf_op jit(solution)/shard_map/all_to_all | solution.py:508
  (59 shorter events, 13.7 us)
Async XLA Ops:
  1.7 4.3 %collective-permute-start = (bf16[256,256]{1,0:T(8,128)(2,1)S(1)}, bf16[256,256]{1,0:T(8,128)(2,1)S(1)}, u32[]{:S(2)}, u32[]{:S(2)}) collective-permute-start(bf16[256,256]{1,0:T(8,128)(2,1)S(1)} %shard_map.122.refs_0_), channel_id=1, source_target_pairs={{0,1},{1,0},{2,3},{3,2},{4,5},{5,4},{6,7},{7,6},{8,9},{9,8},{10,11... | collective-permute-start | bytes 393224 | tf_op jit(solution)/shard_map/ppermute | solution.py:265
  6.1 9.9 %collective-permute-start.1 = (bf16[2,256,256]{2,1,0:T(8,128)(2,1)S(1)}, bf16[2,256,256]{2,1,0:T(8,128)(2,1)S(1)}, u32[]{:S(2)}, u32[]{:S(2)}) collective-permute-start(bf16[2,256,256]{2,1,0:T(8,128)(2,1)S(1)} %shard_map.123.refs_0_), channel_id=1, source_target_pairs={{0,2},{1,15},{2,4},{3,1},{4,6},{5,3},{6,8},{7,5},{8,10},{9,7},{10,... | collective-permute-start | bytes 786440 | tf_op jit(solution)/shard_map/ppermute | solution.py:286
  11.0 5.0 %collective-permute-start.2 = (bf16[256,256]{1,0:T(8,128)(2,1)S(1)}, bf16[256,256]{1,0:T(8,128)(2,1)S(1)}, u32[]{:S(2)}, u32[]{:S(2)}) collective-permute-start(bf16[256,256]{1,0:T(8,128)(2,1)S(1)} %shard_map.124.refs_0_), channel_id=1, source_target_pairs={{0,32},{32,0},{1,33},{33,1},{2,34},{34,2},{3,35},{35,3},{4,36},{36... | collective-permute-start | bytes 393224 | tf_op jit(solution)/shard_map/ppermute | solution.py:265
  12.3 6.2 %collective-permute-start.4 = (bf16[256,256]{1,0:T(8,128)(2,1)S(1)}, bf16[256,256]{1,0:T(8,128)(2,1)S(1)}, u32[]{:S(2)}, u32[]{:S(2)}) collective-permute-start(bf16[256,256]{1,0:T(8,128)(2,1)S(1)} %shard_map.122.refs_0_), channel_id=1, source_target_pairs={{0,16},{16,0},{1,17},{17,1},{2,18},{18,2},{3,19},{19,3},{4,20},{20... | collective-permute-start | bytes 393224 | tf_op jit(solution)/shard_map/ppermute | solution.py:265
  16.0 7.8 %collective-permute-start.3 = (bf16[2,256,256]{2,1,0:T(8,128)(2,1)S(1)}, bf16[2,256,256]{2,1,0:T(8,128)(2,1)S(1)}, u32[]{:S(2)}, u32[]{:S(2)}) collective-permute-start(bf16[2,256,256]{2,1,0:T(8,128)(2,1)S(1)} %collective-permute-done.1.refs_1_), channel_id=1, source_target_pairs={{0,2},{1,15},{2,4},{3,1},{4,6},{5,3},{6,8},{7,5},{8,10},{9,7},{10,... | collective-permute-start | bytes 786440 | tf_op jit(solution)/shard_map/ppermute | solution.py:286
  19.9 11.9 %collective-permute-start.7 = (bf16[2,256,256]{2,1,0:T(8,128)(2,1)S(1)}, bf16[2,256,256]{2,1,0:T(8,128)(2,1)S(1)}, u32[]{:S(2)}, u32[]{:S(2)}) collective-permute-start(bf16[2,256,256]{2,1,0:T(8,128)(2,1)S(1)} %shard_map.127.refs_6_.refs_7_), channel_id=1, source_target_pairs={{0,64},{64,128},{128,192},{192,0},{1,65},{65,129},{129,193},{193,1... | collective-permute-start | bytes 786440 | tf_op jit(solution)/shard_map/ppermute | solution.py:265
  21.3 10.5 %collective-permute-start.8 = (bf16[2,256,256]{2,1,0:T(8,128)(2,1)S(1)}, bf16[2,256,256]{2,1,0:T(8,128)(2,1)S(1)}, u32[]{:S(2)}, u32[]{:S(2)}) collective-permute-start(bf16[2,256,256]{2,1,0:T(8,128)(2,1)S(1)} %shard_map.127.refs_6_.refs_7_), channel_id=1, source_target_pairs={{0,192},{64,0},{128,64},{192,128},{1,193},{65,1},{129,65},{193,129... | collective-permute-start | bytes 786440 | tf_op jit(solution)/shard_map/ppermute | solution.py:265
  22.9 9.0 %collective-permute-start.9 = (bf16[2,256,256]{2,1,0:T(8,128)(2,1)S(1)}, bf16[2,256,256]{2,1,0:T(8,128)(2,1)S(1)}, u32[]{:S(2)}, u32[]{:S(2)}) collective-permute-start(bf16[2,256,256]{2,1,0:T(8,128)(2,1)S(1)} %collective-permute-done.1.refs_1_), channel_id=1, source_target_pairs={{0,1},{1,0},{2,3},{3,2},{4,5},{5,4},{6,7},{7,6},{8,9},{9,8},{10,11... | collective-permute-start | bytes 786440 | tf_op jit(solution)/shard_map/ppermute | solution.py:265
  23.8 8.1 %collective-permute-start.10 = (bf16[2,256,256]{2,1,0:T(8,128)(2,1)S(1)}, bf16[2,256,256]{2,1,0:T(8,128)(2,1)S(1)}, u32[]{:S(2)}, u32[]{:S(2)}) collective-permute-start(bf16[2,256,256]{2,1,0:T(8,128)(2,1)S(1)} %collective-permute-done.3.refs_1_.refs_2_), channel_id=1, source_target_pairs={{0,1},{1,0},{2,3},{3,2},{4,5},{5,4},{6,7},{7,6},{8,9},{9,8},{10,11... | collective-permute-start | bytes 786440 | tf_op jit(solution)/shard_map/ppermute | solution.py:265
  23.8 10.0 %collective-permute-start.6 = (bf16[4,256,256]{2,1,0:T(8,128)(2,1)S(1)}, bf16[4,256,256]{2,1,0:T(8,128)(2,1)S(1)}, u32[]{:S(2)}, u32[]{:S(2)}) collective-permute-start(bf16[4,256,256]{2,1,0:T(8,128)(2,1)S(1)} %shard_map.126), channel_id=1, source_target_pairs={{0,2},{1,15},{2,4},{3,1},{4,6},{5,3},{6,8},{7,5},{8,10},{9,7},{10,... | collective-permute-start | bytes 1572872 | tf_op jit(solution)/shard_map/ppermute | solution.py:286
  33.8 3.7 %collective-permute-start.13 = (bf16[4,256,256]{2,1,0:T(8,128)(2,1)S(1)}, bf16[4,256,256]{2,1,0:T(8,128)(2,1)S(1)}, u32[]{:S(2)}, u32[]{:S(2)}) collective-permute-start(bf16[4,256,256]{2,1,0:T(8,128)(2,1)S(1)} %collective-permute-done.6.refs_5_.refs_1_), channel_id=1, source_target_pairs={{0,1},{1,0},{2,3},{3,2},{4,5},{5,4},{6,7},{7,6},{8,9},{9,8},{10,11... | collective-permute-start | bytes 1572872 | tf_op jit(solution)/shard_map/ppermute | solution.py:265
  35.6 10.1 %collective-permute-start.11 = (bf16[3,256,256]{2,1,0:T(8,128)(2,1)S(1)}, bf16[3,256,256]{2,1,0:T(8,128)(2,1)S(1)}, u32[]{:S(2)}, u32[]{:S(2)}) collective-permute-start(bf16[3,256,256]{2,1,0:T(8,128)(2,1)S(1)} %slice.9), channel_id=1, source_target_pairs={{0,2},{1,15},{2,4},{3,1},{4,6},{5,3},{6,8},{7,5},{8,10},{9,7},{10,... | collective-permute-start | bytes 1179656 | tf_op jit(solution)/shard_map/ppermute | solution.py:286
  37.4 8.2 %collective-permute-start.12 = (bf16[2,256,256]{2,1,0:T(8,128)(2,1)S(1)}, bf16[2,256,256]{2,1,0:T(8,128)(2,1)S(1)}, u32[]{:S(2)}, u32[]{:S(2)}) collective-permute-start(bf16[2,256,256]{2,1,0:T(8,128)(2,1)S(1)} %collective-permute-done.7.refs_8_.refs_9_), channel_id=1, source_target_pairs={{0,64},{64,128},{128,192},{192,0},{1,65},{65,129},{129,193},{193,1... | collective-permute-start | bytes 786440 | tf_op jit(solution)/shard_map/ppermute | solution.py:265
  45.7 3.1 %collective-permute-start.14 = (bf16[3,256,256]{2,1,0:T(8,128)(2,1)S(1)}, bf16[3,256,256]{2,1,0:T(8,128)(2,1)S(1)}, u32[]{:S(2)}, u32[]{:S(2)}) collective-permute-start(bf16[3,256,256]{2,1,0:T(8,128)(2,1)S(1)} %collective-permute-done.11.refs_3_.refs_0_), channel_id=1, source_target_pairs={{0,1},{1,0},{2,3},{3,2},{4,5},{5,4},{6,7},{7,6},{8,9},{9,8},{10,11... | collective-permute-start | bytes 1179656 | tf_op jit(solution)/shard_map/ppermute | solution.py:265
  45.7 7.9 %collective-permute-start.15 = (bf16[2,256,256]{2,1,0:T(8,128)(2,1)S(1)}, bf16[2,256,256]{2,1,0:T(8,128)(2,1)S(1)}, u32[]{:S(2)}, u32[]{:S(2)}) collective-permute-start(bf16[2,256,256]{2,1,0:T(8,128)(2,1)S(1)} %slice.10), channel_id=1, source_target_pairs={{0,2},{1,15},{2,4},{3,1},{4,6},{5,3},{6,8},{7,5},{8,10},{9,7},{10,... | collective-permute-start | bytes 786440 | tf_op jit(solution)/shard_map/ppermute | solution.py:286
  48.2 5.4 %collective-permute-start.16 = (bf16[1,256,256]{2,1,0:T(8,128)(2,1)S(1)}, bf16[1,256,256]{2,1,0:T(8,128)(2,1)S(1)}, u32[]{:S(2)}, u32[]{:S(2)}) collective-permute-start(bf16[1,256,256]{2,1,0:T(8,128)(2,1)S(1)} %slice.11), channel_id=1, source_target_pairs={{0,16},{16,0},{1,17},{17,1},{2,18},{18,2},{3,19},{19,3},{4,20},{20... | collective-permute-start | bytes 393224 | tf_op jit(solution)/shard_map/ppermute | solution.py:265
  53.6 1.7 %collective-permute-start.17 = (bf16[2,256,256]{2,1,0:T(8,128)(2,1)S(1)}, bf16[2,256,256]{2,1,0:T(8,128)(2,1)S(1)}, u32[]{:S(2)}, u32[]{:S(2)}) collective-permute-start(bf16[2,256,256]{2,1,0:T(8,128)(2,1)S(1)} %collective-permute-done.15.refs_2_), channel_id=1, source_target_pairs={{0,1},{1,0},{2,3},{3,2},{4,5},{5,4},{6,7},{7,6},{8,9},{9,8},{10,11... | collective-permute-start | bytes 786440 | tf_op jit(solution)/shard_map/ppermute | solution.py:265
  53.9 1.4 %collective-permute-start.18 = (bf16[1,256,256]{2,1,0:T(8,128)(2,1)S(1)}, bf16[1,256,256]{2,1,0:T(8,128)(2,1)S(1)}, u32[]{:S(2)}, u32[]{:S(2)}) collective-permute-start(bf16[1,256,256]{2,1,0:T(8,128)(2,1)S(1)} %collective-permute-done.16.refs_4_), channel_id=1, source_target_pairs={{0,1},{1,0},{2,3},{3,2},{4,5},{5,4},{6,7},{7,6},{8,9},{9,8},{10,11... | collective-permute-start | bytes 393224 | tf_op jit(solution)/shard_map/ppermute | solution.py:265
  57.3 15.4 %collective-permute-start.19 = (bf16[4,256,256]{2,1,0:T(8,128)(2,1)S(1)}, bf16[4,256,256]{2,1,0:T(8,128)(2,1)S(1)}, u32[]{:S(2)}, u32[]{:S(2)}) collective-permute-start(bf16[4,256,256]{2,1,0:T(8,128)(2,1)S(1)} %get-tuple-element.67), channel_id=1, source_target_pairs={{0,32},{32,0},{1,33},{33,1},{2,34},{34,2},{3,35},{35,3},{4,36},{36... | collective-permute-start | bytes 1572872 | tf_op jit(solution)/shard_map/ppermute | solution.py:265
  73.4 16.8 %all-to-all-start.1 = ((bf16[16,16,256]{2,1,0:T(8,128)(2,1)}), bf16[16,16,256]{2,1,0:T(8,128)(2,1)S(1)}, u32[]{:S(2)}, u32[]{:S(2)}) async-start(bf16[16,16,256]{2,1,0:T(8,128)(2,1)} %shard_map.134), calls=%async_computation.1 | async-start | bytes 262144 | tf_op jit(solution)/shard_map/all_to_all | solution.py:497
  81.8 14.3 %collective-permute-start.20 = (bf16[256,256]{1,0:T(8,128)(2,1)S(1)}, bf16[256,256]{1,0:T(8,128)(2,1)S(1)}, u32[]{:S(2)}, u32[]{:S(2)}) collective-permute-start(bf16[256,256]{1,0:T(8,128)(2,1)S(1)} %get-tuple-element.70), channel_id=1, source_target_pairs={{0,64},{64,128},{128,192},{192,0},{1,65},{65,129},{129,193},{193,1... | collective-permute-start | bytes 393224 | tf_op jit(solution)/shard_map/ppermute | solution.py:265
  81.9 14.2 %collective-permute-start.21 = (bf16[256,256]{1,0:T(8,128)(2,1)S(1)}, bf16[256,256]{1,0:T(8,128)(2,1)S(1)}, u32[]{:S(2)}, u32[]{:S(2)}) collective-permute-start(bf16[256,256]{1,0:T(8,128)(2,1)S(1)} %get-tuple-element.71), channel_id=1, source_target_pairs={{0,128},{64,192},{128,0},{192,64},{1,129},{65,193},{129,1},{193,65... | collective-permute-start | bytes 393224 | tf_op jit(solution)/shard_map/ppermute | solution.py:265
  83.3 12.8 %collective-permute-start.22 = (bf16[256,256]{1,0:T(8,128)(2,1)S(1)}, bf16[256,256]{1,0:T(8,128)(2,1)S(1)}, u32[]{:S(2)}, u32[]{:S(2)}) collective-permute-start(bf16[256,256]{1,0:T(8,128)(2,1)S(1)} %get-tuple-element.72), channel_id=1, source_target_pairs={{0,192},{64,0},{128,64},{192,128},{1,193},{65,1},{129,65},{193,129... | collective-permute-start | bytes 393224 | tf_op jit(solution)/shard_map/ppermute | solution.py:265
  90.8 11.5 %all-to-all-start.2 = ((bf16[16,16,256]{2,1,0:T(8,128)(2,1)}), bf16[16,16,256]{2,1,0:T(8,128)(2,1)S(1)}, u32[]{:S(2)}, u32[]{:S(2)}) async-start(bf16[16,16,256]{2,1,0:T(8,128)(2,1)} %shard_map.135), calls=%async_computation.2 | async-start | bytes 262144 | tf_op jit(solution)/shard_map/all_to_all | solution.py:508
  (7 other events, 88.0 us)
